TPU v7x, 128 devices: a whole 4x4x4 slice. The times are simulated.
128 devices in a mesh: island: 16 (over z_lo, x, core), fsdp: 8 (over z_hi, y).
Axes of the slice: x: 4, y: 4, z: 4 (z_hi: 2, z_lo: 2; z = z_hi * 2 + z_lo), core: 2. Of those that a mesh axis runs over, the one named last changes fastest.
Arguments:
- acts: bfloat16 [16, 2048, 8192], P('island', 'fsdp'), may hold values from -6 to 6
- cotangent: bfloat16 [16, 2048, 1024], P('island', 'fsdp'), may hold values from -0.125 to 0.125
- inner_weight: float32 [16, 8192, 1024], P('island', 'fsdp'), may hold values from -3 to 3
- first_moment: float32 [16, 8192, 1024], P('island', 'fsdp'), may hold values from -0.6 to 0.6
- second_moment: float32 [16, 8192, 1024], P('island', 'fsdp'), may hold values from 0.02 to 0.2
- outer_weight: float32 [8, 1024, 1024], P('fsdp', 'island'), may hold values from -3 to 3
- outer_momentum: float32 [8, 1024, 1024], P('fsdp', 'island'), may hold values from -1.5 to 1.5
Outputs:
- input_grad: bfloat16 [16, 2048, 8192], P('island', 'fsdp')
- mixed_weight: float32 [16, 8192, 1024], P('island', 'fsdp')
- new_outer: float32 [8, 1024, 1024], P('fsdp', 'island')
- new_momentum: float32 [8, 1024, 1024], P('fsdp', 'island')
All inputs are finite; a program needn't handle non-finite values.
Results may differ from a plain program's by a relative error of at most 0.015.
Values may be sent and summed in bfloat16 or wider, within the bound.
No kernel may reach another device: no remote copies, remote signals or barrier semaphores. Data moves between devices by JAX's collectives and lax.ppermute only.
A program may use at most 192 MiB of HBM per device.

v0:
```python
import jax
import jax.numpy as jnp
from jax import lax
from jax.sharding import PartitionSpec as P

STEP = 10


def outer_update(anchor, momentum, summed, islands):
    pseudo = anchor - summed / islands
    new_momentum = 0.9 * momentum + pseudo
    new_anchor = anchor - 0.7 * (pseudo + 0.9 * new_momentum)
    return (new_anchor, new_momentum)


def shards(
    acts, cotangent, inner_weight, first_moment, second_moment, outer_weight, outer_momentum
):
    local_acts = acts[0]
    local_cot = cotangent[0]
    master = inner_weight[0]
    weight_bf = master.astype(jnp.bfloat16)
    gradient = lax.psum_scatter(
        lax.dot_general(
            local_acts, local_cot, (((0,), (0,)), ((), ())), preferred_element_type=jnp.float32
        ).astype(jnp.bfloat16),
        "fsdp",
        scatter_dimension=0,
        tiled=True,
    ).astype(jnp.float32)
    input_grad = lax.dot_general(
        local_cot,
        lax.all_gather(weight_bf, "fsdp", axis=0, tiled=True),
        (((1,), (1,)), ((), ())),
        preferred_element_type=jnp.float32,
    ).astype(jnp.bfloat16)
    moment_one = 0.9 * first_moment[0] + 0.1 * gradient
    moment_two = 0.95 * second_moment[0] + 0.05 * gradient * gradient
    correct_one = 1.0 - 0.9**STEP
    correct_two = 1.0 - 0.95**STEP
    updated = master - 0.5 * (moment_one / correct_one) / (
        jnp.sqrt(moment_two / correct_two) + 1e-08
    )
    islands = lax.axis_size("island")
    anchor = outer_weight[0]
    momentum = outer_momentum[0]
    summed = lax.psum_scatter(
        updated.astype(jnp.bfloat16), "island", scatter_dimension=0, tiled=True
    ).astype(jnp.float32)
    new_anchor, new_momentum = outer_update(anchor, momentum, summed, islands)
    anchor_rows = lax.all_gather(
        new_anchor.astype(jnp.bfloat16), "island", axis=0, tiled=True
    ).astype(new_anchor.dtype)
    mixed_weight = 0.5 * updated + 0.5 * anchor_rows
    return (input_grad[None], mixed_weight[None], new_anchor[None], new_momentum[None])


def solution(mesh):
    placed = (
        P("island", "fsdp", None),
        P("island", "fsdp", None),
        P("island", "fsdp", None),
        P("island", "fsdp", None),
        P("island", "fsdp", None),
        P("fsdp", "island", None),
        P("fsdp", "island", None),
    )
    return jax.shard_map(
        shards,
        mesh=mesh,
        in_specs=placed,
        out_specs=(
            P("island", "fsdp", None),
            P("island", "fsdp", None),
            P("fsdp", "island", None),
            P("fsdp", "island", None),
        ),
        check_vma=False,
    )
```

profile of v0, /device:TPU:1, one launch (start us, length us, event | category | flops | bytes accessed | tf_op | source)
XLA Modules:
  0.0 521.0 jit_solution(10699965948479476381)
XLA Ops:
  7.2 0.0 copy-start
  7.2 0.0 reduce-scatter.3.cloned.1.call-start
  7.2 1.0 copy-done
  8.2 10.4 %convolution_convert_fusion = bf16[8192,1024]{1,0:T(8,128)(2,1)} fusion(bf16[1,256,8192]{2,1,0:T(8,128)(2,1)} %param.7, bf16[1,256,1024]{2,1,0:T(8,128)(2,1)S(1)} %copy-done), kind=kOutput, calls=%fused_computation | convolution fusion | flops 4303355904 | bytes 21495808 | tf_op jit(solution)/shard_map/dot_general | solution.py:24
  18.6 0.0 reduce-scatter.3.cloned.1.call-update
  18.7 0.0 reduce-scatter.5.cloned.1.call-start
  18.7 194.3 %reduce-scatter.3.cloned.1.call-done = bf16[1024,1024]{1,0:T(8,128)(2,1)} async-done(((bf16[8192,1024]{1,0:T(8,128)(2,1)}), bf16[1024,1024]{1,0:T(8,128)(2,1)}) %reduce-scatter.3.cloned.1.call-update) | async-done | bytes 2097168 | tf_op jit(solution)/shard_map/reduce_scatter | solution.py:23
  213.0 8.4 %fusion.15 = (bf16[1024,1024]{1,0:T(8,128)(2,1)}, f32[1024,1024]{1,0:T(8,128)}) fusion(f32[1,1024,1024]{2,1,0:T(8,128)} %param.11, bf16[1024,1024]{1,0:T(8,128)(2,1)} %reduce-scatter.3.cloned.1.call-done, f32[1,1024,1024]{2,1,0:T(8,128)} %param.10, f32[1,1024,1024]{2,1,0:T(8,128)} %param.9), kind=kLoop, calls=%fused_computation.24 | loop fusion | flops 14680064 | bytes 20971520 | tf_op jit(solution)/shard_map/convert_element_type | solution.py:48
  221.5 0.0 reduce-scatter.5.cloned.1.call-update
  221.5 0.0 copy-start.1
  221.5 0.0 copy-start.2
  221.5 0.0 all-gather.3.cloned.1.call-start
  221.6 3.9 bitcast_convert_fusion
  225.4 0.0 all-gather.3.cloned.1.call-update
  225.5 0.0 all-gather.5.cloned.1.call-start
  225.5 58.0 %reduce-scatter.5.cloned.1.call-done = bf16[64,1024]{1,0:T(8,128)(2,1)} async-done(((bf16[1024,1024]{1,0:T(8,128)(2,1)}), bf16[64,1024]{1,0:T(8,128)(2,1)}) %reduce-scatter.5.cloned.1.call-update) | async-done | bytes 131088 | tf_op jit(solution)/shard_map/reduce_scatter | solution.py:47
  283.5 0.0 copy-done.1
  283.5 0.0 copy-done.2
  283.5 1.8 fusion.12
  285.3 0.0 all-gather.5.cloned.1.call-update
  285.3 189.1 %all-gather.3.cloned.1.call-done = bf16[8192,1024]{1,0:T(8,128)(2,1)} async-done(((bf16[1024,1024]{1,0:T(8,128)(2,1)}), bf16[8192,1024]{1,0:T(8,128)(2,1)}) %all-gather.3.cloned.1.call-update) | async-done | bytes 16777232 | tf_op jit(solution)/shard_map/all_gather | solution.py:33
  474.4 9.5 %fusion = bf16[1,256,8192]{2,1,0:T(8,128)(2,1)} fusion(bf16[8192,1024]{1,0:T(8,128)(2,1)} %all-gather.3.cloned.1.call-done, bf16[1,256,1024]{2,1,0:T(8,128)(2,1)S(1)} %copy-done), kind=kOutput, calls=%fused_computation.2 | convolution fusion | flops 4297064448 | bytes 21495808 | tf_op jit(solution)/shard_map/dot_general | solution.py:31
  483.8 24.7 %all-gather.5.cloned.1.call-done = bf16[1024,1024]{1,0:T(8,128)(2,1)} async-done(((bf16[64,1024]{1,0:T(8,128)(2,1)}), bf16[1024,1024]{1,0:T(8,128)(2,1)}) %all-gather.5.cloned.1.call-update) | async-done | bytes 2097168 | tf_op jit(solution)/shard_map/all_gather | solution.py:51
  508.5 5.9 %multiply_bitcast_fusion = f32[1,1024,1024]{2,1,0:T(8,128)} fusion(f32[1024,1024]{1,0:T(8,128)} %get-tuple-element.5, bf16[1024,1024]{1,0:T(8,128)(2,1)} %all-gather.5.cloned.1.call-done), kind=kLoop, calls=%fused_computation.15 | loop fusion | flops 3145728 | bytes 10485760 | tf_op jit(solution)/shard_map/broadcast_in_dim | solution.py:55
Async XLA Ops:
  7.2 1.0 copy-start
  7.2 205.8 %reduce-scatter.3.cloned.1.call-start = ((), (), s32[]{:S(2)}) async-start(), calls=%async_computation.3 | async-start | bytes 18874368 | tf_op jit(solution)/shard_map/reduce_scatter | solution.py:23
  18.7 264.8 %reduce-scatter.5.cloned.1.call-start = ((), (), s32[]{:S(2)}) async-start(), calls=%async_computation.4 | async-start | bytes 2228224 | tf_op jit(solution)/shard_map/reduce_scatter | solution.py:47
  221.5 62.0 %copy-start.1 = (f32[1,64,1024]{2,1,0:T(8,128)S(1)}, f32[1,64,1024]{2,1,0:T(8,128)}, u32[]{:S(2)}) copy-start(f32[1,64,1024]{2,1,0:T(8,128)} %param.12) | copy-start | bytes 786436
  221.5 62.0 %copy-start.2 = (f32[1,64,1024]{2,1,0:T(8,128)S(1)}, f32[1,64,1024]{2,1,0:T(8,128)}, u32[]{:S(2)}) copy-start(f32[1,64,1024]{2,1,0:T(8,128)} %param.13) | copy-start | bytes 786436
  221.5 252.9 %all-gather.3.cloned.1.call-start = ((), (), s32[]{:S(2)}) async-start(), calls=%async_computation.2 | async-start | bytes 18874368 | tf_op jit(solution)/shard_map/all_gather | solution.py:33
  225.5 283.1 %all-gather.5.cloned.1.call-start = ((), (), s32[]{:S(2)}) async-start(), calls=%async_computation.5 | async-start | bytes 2228224 | tf_op jit(solution)/shard_map/all_gather | solution.py:51
Sparse Core Ops, SparseCore 0:
  18.8 194.1 reduce-scatter.2
  221.6 61.8 reduce-scatter.4
  286.4 187.9 all-gather.2
  475.9 32.5 all-gather.4
where the time goes:
time: 521 us
  waiting for transfers between devices  466 us (89%)
  other arithmetic  20.1 us (4%)
  matrix products  19.9 us (4%)
  between operations  13.8 us (3%)
    reduce_scatter x1, waiting for transfers between devices, shards(): lax.psum_scatter(lax.dot_general(local_acts, local_cot, (((0,), (0,)), ((...  194 us
    all_gather x1, waiting for transfers between devices, shards(): lax.all_gather(weight_bf, 'fsdp', axis=0, tiled=True)  189 us
    reduce_scatter x1, waiting for transfers between devices, shards(): lax.psum_scatter(updated.astype(jnp.bfloat16), 'island', scatter_dimensio...  58 us
    all_gather x1, waiting for transfers between devices, shards(): lax.all_gather(new_anchor.astype(jnp.bfloat16), 'island', axis=0, tiled=T...  24.7 us
    dot_general x1, matrix products, shards(): lax.dot_general(local_acts, local_cot, (((0,), (0,)), ((), ())), preferre...  10.4 us
  transfers between devices with their start and end apart: 4, of which 4 were waited for; matrix products, arithmetic and copies ran while one was open for 3% of the time, Pallas kernels for 0%

commit v1 on v0

v1 whole, which is shorter than its diff:
```python
import jax
import jax.numpy as jnp
from jax import lax
from jax.experimental import pallas as pl
from jax.experimental.pallas import tpu as pltpu
from jax.sharding import PartitionSpec as P

STEP = 10
BF = jnp.bfloat16
F32 = jnp.float32
ROWS = 1024
KV = 1024
TOK = 256
MIB = 1 << 20


def f_index(zh, y):
    return (zh % 2) * 4 + y % 4


def along_y(array, step):
    pairs = [(f_index(z, y), f_index(z, y + step)) for z in range(2) for y in range(4)]
    return lax.ppermute(array, "fsdp", pairs)


def swap_z(array):
    pairs = [(f_index(z, y), f_index(z + 1, y)) for z in range(2) for y in range(4)]
    return lax.ppermute(array, "fsdp", pairs)


def island_shift(array, dz, dx, dc):
    def index(z, x, c):
        return ((z % 2) * 4 + x % 4) * 2 + c % 2

    pairs = [
        (index(z, x, c), index(z + dz, x + dx, c + dc))
        for z in range(2)
        for x in range(4)
        for c in range(2)
    ]
    return lax.ppermute(array, "island", pairs)


def cost(flops, moved):
    return pl.CostEstimate(flops=flops, bytes_accessed=moved, transcendentals=0)


def params(mib):
    return pltpu.CompilerParams(vmem_limit_bytes=mib * MIB)


ANY = pl.BlockSpec(memory_space=pl.ANY)


def pack(acts, place):
    def kernel(place_ref, acts_ref, *refs):
        outs, sems = refs[:6], refs[6]
        zh, y = place_ref[0], place_ref[1]
        copies = []
        for n in range(6):
            dz, dy = 1 - n // 3, n % 3 + 1
            block = lax.rem(zh + dz, 2) * 4 + lax.rem(y + dy, 4)
            columns = pl.ds(pl.multiple_of(block * ROWS, ROWS), ROWS)
            copies.append(pltpu.make_async_copy(acts_ref.at[:, columns], outs[n], sems.at[n]))
        for copy in copies:
            copy.start()
        for copy in copies:
            copy.wait()

    outs = pl.pallas_call(
        kernel,
        out_shape=[jax.ShapeDtypeStruct((TOK, ROWS), BF)] * 6,
        in_specs=[pl.BlockSpec(memory_space=pltpu.SMEM), ANY],
        out_specs=[ANY] * 6,
        scratch_shapes=[pltpu.SemaphoreType.DMA((6,))],
        cost_estimate=cost(0, 6 * MIB),
        compiler_params=params(1),
        name="pack_acts",
    )(place, acts)
    return outs[:3], outs[3:]


def t_dot(a, c):
    return lax.dot_general(a, c, (((0,), (0,)), ((), ())), preferred_element_type=F32)


def partial_sums(block, acts, others, cots):
    tile = 256

    def kernel(block_ref, a0, a1, a2, a3, c0, c1, c2, c3, out):
        total = t_dot(a0[...], c0[...])
        for a, c in ((a1, c1), (a2, c2), (a3, c3)):
            total += t_dot(a[...], c[...])
        out[...] = total.astype(BF)

    strip = pl.BlockSpec((TOK, tile), lambda j, s: (0, j))
    whole = pl.BlockSpec((TOK, KV), lambda j, s: (0, 0))
    return pl.pallas_call(
        kernel,
        out_shape=jax.ShapeDtypeStruct((ROWS, KV), BF),
        grid_spec=pltpu.PrefetchScalarGridSpec(
            num_scalar_prefetch=1,
            grid=(ROWS // tile,),
            in_specs=[pl.BlockSpec((TOK, tile), lambda j, s: (0, s[0] * (ROWS // tile) + j))]
            + [strip] * 3
            + [whole] * 4,
            out_specs=pl.BlockSpec((tile, KV), lambda j, s: (j, 0)),
        ),
        cost_estimate=cost(2 * ROWS * KV * 4 * TOK, 6 * MIB),
        compiler_params=params(16),
        name="partial_sums",
    )(block, acts, *others, *cots)


def adam(info, acts, others, cots, received, master, first, second):
    tile = 256
    correct_one = 1.0 - 0.9**STEP
    correct_two = 1.0 - 0.95**STEP

    def kernel(info_ref, a0, a1, a2, a3, c0, c1, c2, c3, got, w, m1, m2, upd, keep, send):
        grad = t_dot(a0[...], c0[...])
        for a, c in ((a1, c1), (a2, c2), (a3, c3)):
            grad += t_dot(a[...], c[...])
        grad += got[...].astype(F32)
        one = 0.9 * m1[...] + 0.1 * grad
        two = 0.95 * m2[...] + 0.05 * grad * grad
        upd[...] = w[...] - 0.5 * (one / correct_one) / (jnp.sqrt(two / correct_two) + 1e-8)
        core = info_ref[1]
        for p in range(tile // 128):
            mine = pl.ds(pl.multiple_of(p * 128 + core * 64, 64), 64)
            other = pl.ds(pl.multiple_of(p * 128 + (1 - core) * 64, 64), 64)
            keep[p] = upd[mine, :].astype(BF)
            send[p] = upd[other, :].astype(BF)

    strip = pl.BlockSpec((TOK, tile), lambda j, s: (0, j))
    whole = pl.BlockSpec((TOK, KV), lambda j, s: (0, 0))
    rows = pl.BlockSpec((tile, KV), lambda j, s: (j, 0))
    halves = pl.BlockSpec((tile // 128, 64, KV), lambda j, s: (j, 0, 0))
    return pl.pallas_call(
        kernel,
        out_shape=[
            jax.ShapeDtypeStruct((ROWS, KV), F32),
            jax.ShapeDtypeStruct((8, 64, KV), BF),
            jax.ShapeDtypeStruct((8, 64, KV), BF),
        ],
        grid_spec=pltpu.PrefetchScalarGridSpec(
            num_scalar_prefetch=1,
            grid=(ROWS // tile,),
            in_specs=[pl.BlockSpec((TOK, tile), lambda j, s: (0, s[0] * (ROWS // tile) + j))]
            + [strip] * 3
            + [whole] * 4
            + [rows] * 4,
            out_specs=[rows, halves, halves],
        ),
        cost_estimate=cost(2 * ROWS * KV * 4 * TOK, 24 * MIB),
        compiler_params=params(32),
        name="adam_step",
    )(info, acts, *others, *cots, received, master, first, second)


def input_blocks(weight, cots):
    def kernel(w, c0, c1, c2, c3, *outs):
        for c, out in zip((c0, c1, c2, c3), outs):
            out[...] = lax.dot_general(
                c[...], w[...], (((1,), (1,)), ((), ())), preferred_element_type=F32
            ).astype(BF)

    tile = 256
    whole = pl.BlockSpec((TOK, KV), lambda j: (0, 0))
    return pl.pallas_call(
        kernel,
        out_shape=[jax.ShapeDtypeStruct((TOK, ROWS), BF)] * 4,
        grid=(ROWS // tile,),
        in_specs=[pl.BlockSpec((tile, KV), lambda j: (j, 0))] + [whole] * 4,
        out_specs=[pl.BlockSpec((TOK, tile), lambda j: (0, j))] * 4,
        cost_estimate=cost(2 * ROWS * KV * 4 * TOK, 6 * MIB),
        compiler_params=params(16),
        name="input_blocks",
    )(weight, *cots)


def assemble(place, blocks, base, dz):
    def kernel(place_ref, *refs):
        ins, out, sems = refs[:4], refs[-2], refs[-1]
        zh, y = place_ref[0], place_ref[1]
        copies = []
        for k in range(4):
            block = lax.rem(zh + dz, 2) * 4 + lax.rem(y + 4 - k, 4)
            columns = pl.ds(pl.multiple_of(block * ROWS, ROWS), ROWS)
            copies.append(pltpu.make_async_copy(ins[k], out.at[:, columns], sems.at[k]))
        for copy in copies:
            copy.start()
        for copy in copies:
            copy.wait()

    extra = [] if base is None else [base]
    return pl.pallas_call(
        kernel,
        out_shape=jax.ShapeDtypeStruct((TOK, 8 * ROWS), BF),
        in_specs=[pl.BlockSpec(memory_space=pltpu.SMEM)] + [ANY] * (4 + len(extra)),
        out_specs=ANY,
        scratch_shapes=[pltpu.SemaphoreType.DMA((4,))],
        input_output_aliases={5: 0} if extra else {},
        cost_estimate=cost(0, 4 * MIB),
        compiler_params=params(1),
        name="assemble",
    )(place, *blocks, *extra)


VM = pl.BlockSpec(memory_space=pltpu.VMEM)
SM = pl.BlockSpec(memory_space=pltpu.SMEM)


def core_sums(x_place, keep, received):
    def kernel(x_ref, keep_ref, got_ref, *outs):
        for dx in range(4):
            target = lax.rem(x_ref[0] + dx, 4)
            for z in range(2):
                total = keep_ref[z * 4 + target].astype(F32) + got_ref[z * 4 + target].astype(F32)
                outs[dx][z] = total.astype(BF)

    return pl.pallas_call(
        kernel,
        out_shape=[jax.ShapeDtypeStruct((2, 64, KV), BF)] * 4,
        in_specs=[SM, VM, VM],
        out_specs=[VM] * 4,
        cost_estimate=cost(0, 3 * MIB),
        compiler_params=params(16),
        name="core_sums",
    )(x_place, keep, received)


def x_sums(z_place, parts):
    def kernel(z_ref, p0, p1, p2, p3, mine, other):
        def total(z):
            return (p0[z].astype(F32) + p1[z].astype(F32)) + (
                p2[z].astype(F32) + p3[z].astype(F32)
            )

        mine[...] = total(z_ref[0])
        other[...] = total(1 - z_ref[0]).astype(BF)

    return pl.pallas_call(
        kernel,
        out_shape=[jax.ShapeDtypeStruct((64, KV), F32), jax.ShapeDtypeStruct((64, KV), BF)],
        in_specs=[SM] + [VM] * 4,
        out_specs=[VM] * 2,
        cost_estimate=cost(0, 2 * MIB),
        compiler_params=params(8),
        name="x_sums",
    )(z_place, *parts)


def outer_step(mine, received, anchor, momentum):
    def kernel(s, got, w, m, new_w, new_m, rounded):
        pseudo = w[...] - (s[...] + got[...].astype(F32)) / 16.0
        speed = 0.9 * m[...] + pseudo
        fresh = w[...] - 0.7 * (pseudo + 0.9 * speed)
        new_w[...] = fresh
        new_m[...] = speed
        rounded[...] = fresh.astype(BF)

    return pl.pallas_call(
        kernel,
        out_shape=[
            jax.ShapeDtypeStruct((64, KV), F32),
            jax.ShapeDtypeStruct((64, KV), F32),
            jax.ShapeDtypeStruct((64, KV), BF),
        ],
        in_specs=[VM] * 4,
        out_specs=[VM] * 3,
        cost_estimate=cost(0, 2 * MIB),
        compiler_params=params(8),
        name="outer_step",
    )(mine, received, anchor, momentum)


def mix(place, updated, blocks):
    def kernel(place_ref, upd, *refs):
        ins, out = refs[:-1], refs[-1]
        step = pl.program_id(0)
        zl, core = place_ref[0], place_ref[2]
        dx, dz = step // 2, lax.rem(step, 2)
        for k in range(4):

            @pl.when(dx == k)
            def _():
                for dc in range(2):
                    c = lax.rem(core + dc, 2)
                    rows = pl.ds(pl.multiple_of(c * 64, 64), 64)
                    fresh = ins[2 * k + dc][dz].astype(F32)
                    out[rows, :] = 0.5 * upd[rows, :] + 0.5 * fresh

    def at(step, place):
        zl = lax.rem(place[0] + lax.rem(step, 2), 2)
        return (zl * 4 + lax.rem(place[1] + 4 - step // 2, 4), 0)

    rows = pl.BlockSpec((128, KV), at)
    block = pl.BlockSpec((2, 64, KV), lambda step, place: (0, 0, 0))
    return pl.pallas_call(
        kernel,
        out_shape=jax.ShapeDtypeStruct((ROWS, KV), F32),
        grid_spec=pltpu.PrefetchScalarGridSpec(
            num_scalar_prefetch=1,
            grid=(8,),
            in_specs=[rows] + [block] * 8,
            out_specs=rows,
        ),
        cost_estimate=cost(0, 10 * MIB),
        compiler_params=params(16),
        name="mix",
    )(place, updated, *blocks)


def shards(
    acts, cotangent, inner_weight, first_moment, second_moment, outer_weight, outer_momentum
):
    acts, cot, master = acts[0], cotangent[0], inner_weight[0]
    f, i = lax.axis_index("fsdp"), lax.axis_index("island")
    zh, y = f // 4, f % 4
    zl, x, core = i // 8, (i // 2) % 4, i % 2
    f_place = jnp.stack([zh, y]).astype(jnp.int32)
    i_place = jnp.stack([zl, x, core]).astype(jnp.int32)

    cots = [cot] + [along_y(cot, k) for k in (1, 2, 3)]
    to_other, to_own = pack(acts, f_place)
    acts_other = [along_y(a, k + 1) for k, a in enumerate(to_other)]
    acts_own = [along_y(a, k + 1) for k, a in enumerate(to_own)]
    weight = master.astype(BF)
    weight_other = swap_z(weight)

    other_block = ((1 - zh) * 4 + y).astype(jnp.int32)[None]
    partial = partial_sums(other_block, acts, acts_other, cots)
    partial_got = swap_z(partial)
    info = jnp.stack([f, core]).astype(jnp.int32)
    updated, keep, send = adam(
        info, acts, acts_own, cots, partial_got, master, first_moment[0], second_moment[0]
    )

    mine = input_blocks(weight, cots)
    mine = [mine[0]] + [along_y(mine[4 - k], k) for k in (1, 2, 3)]
    others = input_blocks(weight_other, cots)
    others = [others[0]] + [along_y(others[4 - k], k) for k in (1, 2, 3)]
    input_grad = assemble(f_place, mine, None, 0)
    input_grad = assemble(f_place, others, input_grad, 1)

    sums = core_sums(x[None].astype(jnp.int32), keep, island_shift(send, 0, 0, 1))
    sums = [sums[0]] + [island_shift(sums[k], 0, k, 0) for k in (1, 2, 3)]
    mine_sum, other_sum = x_sums(zl[None].astype(jnp.int32), sums)
    new_outer, new_momentum, rounded = outer_step(
        mine_sum, island_shift(other_sum, 1, 0, 0), outer_weight[0], outer_momentum[0]
    )
    pair = jnp.stack([rounded, island_shift(rounded, 1, 0, 0)])
    lines = [pair] + [island_shift(pair, 0, k, 0) for k in (1, 2, 3)]
    blocks = []
    for line in lines:
        blocks += [line, island_shift(line, 0, 0, 1)]
    mixed = mix(i_place, updated, blocks)
    return (input_grad[None], mixed[None], new_outer[None], new_momentum[None])


def solution(mesh):
    by_island = P("island", "fsdp", None)
    by_rows = P("fsdp", "island", None)
    return jax.shard_map(
        shards,
        mesh=mesh,
        in_specs=(by_island,) * 5 + (by_rows,) * 2,
        out_specs=(by_island, by_island, by_rows, by_rows),
        check_vma=False,
    )
```

time: 521 us -> 211 us (0.40)
  waiting for transfers between devices: 466 us -> 115 us
  starting transfers between devices: 0.16 us -> 37.9 us
  Pallas kernels: 0 us -> 37.3 us
  matrix products: 19.9 us -> 0 us
  other arithmetic: 20.1 us -> 0.57 us
  local copies, waits for them, and re-layouts: 1.01 us -> 18.5 us
  between operations: 13.8 us -> 0.87 us
    reduce_scatter x2 -> x0, waiting for transfers between devices: 252 us -> none  [the longest x1 194 us: shards(): lax.psum_scatter(lax.dot_general(local_acts, local_cot, (((0,), (0,)), ((...]
    all_gather x2 -> x0, waiting for transfers between devices: 214 us -> none  [the longest x1 189 us: shards(): lax.all_gather(weight_bf, 'fsdp', axis=0, tiled=True)]
    ppermute x0 -> x30, waiting for transfers between devices: none -> 115 us  [the longest x15 88.3 us: along_y(): return lax.ppermute(array, 'fsdp', pairs)]
    ppermute x0 -> x30, starting transfers between devices: none -> 37.9 us  [the longest x15 20.6 us: along_y(): return lax.ppermute(array, 'fsdp', pairs)]
    pallas_call x0 -> x11, Pallas kernels: none -> 37.3 us  [the longest x1 9.6 us: adam(): pl.pallas_call(kernel, out_shape=[jax.ShapeDtypeStruct((ROWS, KV), F32),...]
    dot_general x2 -> x0, matrix products: 19.9 us -> none  [the longest x1 10.4 us: shards(): lax.dot_general(local_acts, local_cot, (((0,), (0,)), ((), ())), preferre...]
    unnamed x6 -> x40, local copies, waits for them, and re-layouts: 1.01 us -> 18.5 us
    convert_element_type x2 -> x1, other arithmetic: 12.3 us -> 0.32 us  [shards(): weight = master.astype(BF)]
  transfers between devices with their start and end apart: 4 -> 30, of which waited for: 4 -> 15; matrix products, arithmetic and copies ran while one was open for 3% -> 0% of each run, Pallas kernels for 0% -> 12%
where the time goes in v1:
time: 211 us; the launch traced here: 210 us
  waiting for transfers between devices  115 us (55%)
  starting transfers between devices  37.9 us (18%)
  Pallas kernels  37.3 us (18%)
  local copies, waits for them, and re-layouts  18.5 us (9%)
    ppermute x15, waiting for transfers between devices, along_y(): return lax.ppermute(array, 'fsdp', pairs)  88.3 us
    ppermute x15, starting transfers between devices, along_y(): return lax.ppermute(array, 'fsdp', pairs)  20.6 us
    unnamed x40, local copies, waits for them, and re-layouts  18.5 us
    ppermute x2, waiting for transfers between devices, swap_z(): return lax.ppermute(array, 'fsdp', pairs)  17.4 us
    ppermute x13, starting transfers between devices, island_shift(): return lax.ppermute(array, 'island', pairs)  13.6 us
    pallas_call x1, Pallas kernels, adam(): pl.pallas_call(kernel, out_shape=[jax.ShapeDtypeStruct((ROWS, KV), F32),...  9.6 us
    ppermute x13, waiting for transfers between devices, island_shift(): return lax.ppermute(array, 'island', pairs)  9.1 us
    pallas_call x2, Pallas kernels, input_blocks(): pl.pallas_call(kernel, out_shape=[jax.ShapeDtypeStruct((TOK, ROWS), BF)]...  7.83 us
  transfers between devices with their start and end apart: 30, of which 15 were waited for; matrix products, arithmetic and copies ran while one was open for 0% of the time, Pallas kernels for 12%

profile of v1, /device:TPU:1, one launch (start us, length us, event | category | flops | bytes accessed | tf_op | source)
XLA Modules:
  0.0 209.9 jit_solution(14441073805514756397)
XLA Ops:
  0.7 2.2 %copy-done = bf16[1,256,8192]{2,1,0:T(8,128)(2,1)S(1)} copy-done((bf16[1,256,8192]{2,1,0:T(8,128)(2,1)S(1)}, bf16[1,256,8192]{2,1,0:T(8,128)(2,1)}, u32[]{:S(2)}) %copy-start) | copy-done | bytes 4194328
  2.9 2.1 %pack_acts.1 = (bf16[256,1024]{1,0:T(8,128)(2,1)S(1)}, bf16[256,1024]{1,0:T(8,128)(2,1)}, bf16[256,1024]{1,0:T(8,128)(2,1)}, bf16[256,1024]{1,0:T(8,128)(2,1)}, ...) custom-call(s32[2]{0:T(128)S(1)} %pad_add_fusion.place_ref, bf16[256,8192]{1,0:T(8,128)(2,1)S(1)} %bitcast.21), custom_call_target="tpu_custom_call" | custom-call | bytes 6291456 | tf_op jit(solution)/shard_map/pack_acts/pallas_call | solution.py:70
  5.1 2.2 %collective-permute-start.13 = (bf16[256,1024]{1,0:T(8,128)(2,1)S(1)}, bf16[256,1024]{1,0:T(8,128)(2,1)S(1)}, u32[]{:S(2)}, u32[]{:S(2)}) collective-permute-start(bf16[256,1024]{1,0:T(8,128)(2,1)S(1)} %get-tuple-element.41), channel_id=1, source_target_pairs={{0,1},{1,2},{2,3},{3,0},{4,5},{5,6},{6,7},{7,4},{8,9},{9,10},{10,1... | collective-permute-start | bytes 1572872 | tf_op jit(solution)/shard_map/ppermute | solution.py:23
  7.3 2.6 %collective-permute-start.14 = (bf16[256,1024]{1,0:T(8,128)(2,1)}, bf16[256,1024]{1,0:T(8,128)(2,1)S(1)}, u32[]{:S(2)}, u32[]{:S(2)}) collective-permute-start(bf16[256,1024]{1,0:T(8,128)(2,1)} %get-tuple-element.42), channel_id=1, source_target_pairs={{0,2},{1,3},{2,0},{3,1},{4,6},{5,7},{6,4},{7,5},{8,10},{9,11},{10,... | collective-permute-start | bytes 1572872 | tf_op jit(solution)/shard_map/ppermute | solution.py:23
  9.9 1.1 collective-permute-start.15
  12.1 8.1 %collective-permute-done.13.a1 = bf16[256,1024]{1,0:T(8,128)(2,1)S(1)} collective-permute-done((bf16[256,1024]{1,0:T(8,128)(2,1)S(1)}, bf16[256,1024]{1,0:T(8,128)(2,1)S(1)}, u32[]{:S(2)}, u32[]{:S(2)}) %collective-permute-start.13) | collective-permute-done | bytes 524320 | tf_op jit(solution)/shard_map/ppermute | solution.py:23
  20.2 1.3 collective-permute-start.3
  21.5 11.0 %collective-permute-done.14.a2 = bf16[256,1024]{1,0:T(8,128)(2,1)S(1)} collective-permute-done((bf16[256,1024]{1,0:T(8,128)(2,1)}, bf16[256,1024]{1,0:T(8,128)(2,1)S(1)}, u32[]{:S(2)}, u32[]{:S(2)}) %collective-permute-start.14) | collective-permute-done | bytes 524320 | tf_op jit(solution)/shard_map/ppermute | solution.py:23
  32.8 9.8 %collective-permute-done.1.c1 = bf16[256,1024]{1,0:T(8,128)(2,1)S(1)} collective-permute-done((bf16[256,1024]{1,0:T(8,128)(2,1)S(1)}, bf16[256,1024]{1,0:T(8,128)(2,1)S(1)}, u32[]{:S(2)}, u32[]{:S(2)}) %collective-permute-start.1) | collective-permute-done | bytes 524320 | tf_op jit(solution)/shard_map/ppermute | solution.py:23
  42.7 12.3 %collective-permute-done.2.c2 = bf16[256,1024]{1,0:T(8,128)(2,1)S(1)} collective-permute-done((bf16[256,1024]{1,0:T(8,128)(2,1)S(1)}, bf16[256,1024]{1,0:T(8,128)(2,1)S(1)}, u32[]{:S(2)}, u32[]{:S(2)}) %collective-permute-start.2) | collective-permute-done | bytes 524320 | tf_op jit(solution)/shard_map/ppermute | solution.py:23
  55.0 2.6 %copy-done.1 = bf16[1,256,8192]{2,1,0:T(8,128)(2,1)S(1)} copy-done((bf16[1,256,8192]{2,1,0:T(8,128)(2,1)S(1)}, bf16[1,256,8192]{2,1,0:T(8,128)(2,1)}, u32[]{:S(2)}) %copy-start.1) | copy-done | bytes 4194328
  57.5 5.3 %partial_sums.1 = bf16[1024,1024]{1,0:T(8,128)(2,1)} custom-call(s32[1]{0:T(128)} %bitcast.10.block_ref, bf16[256,8192]{1,0:T(8,128)(2,1)S(1)} %bitcast.22, bf16[256,1024]{1,0:T(8,128)(2,1)S(1)} %collective-permute-done.13.a1, bf16[256,1024]{1,0:T(8,128)(2,1)S(1)} %collective-permute-done.14.a2, bf16[256,1024]{1,0:T(8,128)(2,1)} %collective-permute-done.15.a3, ...), custom_call_target="tpu_custom_call" | custom-call | flops 2147483648 | bytes 6291456 | tf_op jit(solution)/shard_map/partial_sums/pallas_call | solution.py:98
  62.8 3.6 %collective-permute-start.16 = (bf16[1024,1024]{1,0:T(8,128)(2,1)}, bf16[1024,1024]{1,0:T(8,128)(2,1)}, u32[]{:S(2)}, u32[]{:S(2)}) collective-permute-start(bf16[1024,1024]{1,0:T(8,128)(2,1)} %partial_sums.1), channel_id=1, source_target_pairs={{0,4},{1,5},{2,6},{3,7},{4,0},{5,1},{6,2},{7,3},{8,12},{9,13},{10,... | collective-permute-start | bytes 6291464 | tf_op jit(solution)/shard_map/ppermute | solution.py:28
  66.9 1.3 collective-permute-start.10
  68.1 2.9 %collective-permute-start.11 = (bf16[256,1024]{1,0:T(8,128)(2,1)}, bf16[256,1024]{1,0:T(8,128)(2,1)}, u32[]{:S(2)}, u32[]{:S(2)}) collective-permute-start(bf16[256,1024]{1,0:T(8,128)(2,1)} %get-tuple-element.39), channel_id=1, source_target_pairs={{0,2},{1,3},{2,0},{3,1},{4,6},{5,7},{6,4},{7,5},{8,10},{9,11},{10,... | collective-permute-start | bytes 1572872 | tf_op jit(solution)/shard_map/ppermute | solution.py:23
  71.1 9.4 %collective-permute-done.10.a1 = bf16[256,1024]{1,0:T(8,128)(2,1)} collective-permute-done((bf16[256,1024]{1,0:T(8,128)(2,1)}, bf16[256,1024]{1,0:T(8,128)(2,1)}, u32[]{:S(2)}, u32[]{:S(2)}) %collective-permute-start.10) | collective-permute-done | bytes 524320 | tf_op jit(solution)/shard_map/ppermute | solution.py:23
  80.5 13.3 %collective-permute-done.11.a2 = bf16[256,1024]{1,0:T(8,128)(2,1)} collective-permute-done((bf16[256,1024]{1,0:T(8,128)(2,1)}, bf16[256,1024]{1,0:T(8,128)(2,1)}, u32[]{:S(2)}, u32[]{:S(2)}) %collective-permute-start.11) | collective-permute-done | bytes 524320 | tf_op jit(solution)/shard_map/ppermute | solution.py:23
  93.8 17.4 %collective-permute-done.16.got = bf16[1024,1024]{1,0:T(8,128)(2,1)} collective-permute-done((bf16[1024,1024]{1,0:T(8,128)(2,1)}, bf16[1024,1024]{1,0:T(8,128)(2,1)}, u32[]{:S(2)}, u32[]{:S(2)}) %collective-permute-start.16) | collective-permute-done | bytes 2097184 | tf_op jit(solution)/shard_map/ppermute | solution.py:28
  111.1 2.2 %copy-done.2 = bf16[1,256,8192]{2,1,0:T(8,128)(2,1)S(1)} copy-done((bf16[1,256,8192]{2,1,0:T(8,128)(2,1)S(1)}, bf16[1,256,8192]{2,1,0:T(8,128)(2,1)}, u32[]{:S(2)}) %copy-start.2) | copy-done | bytes 4194328
  113.3 2.2 %copy-done.4 = f32[1,1024,1024]{2,1,0:T(8,128)S(1)} copy-done((f32[1,1024,1024]{2,1,0:T(8,128)S(1)}, f32[1,1024,1024]{2,1,0:T(8,128)}, u32[]{:S(2)}) %copy-start.4) | copy-done | bytes 4194328
  115.5 1.0 copy-done.9
  117.6 9.6 %adam_step.1 = (f32[1024,1024]{1,0:T(8,128)S(1)}, bf16[8,64,1024]{2,1,0:T(8,128)(2,1)S(1)}, bf16[8,64,1024]{2,1,0:T(8,128)(2,1)}) custom-call(s32[2]{0:T(128)S(1)} %pad_add_fusion.2.info_ref, bf16[256,8192]{1,0:T(8,128)(2,1)S(1)} %bitcast.23, bf16[256,1024]{1,0:T(8,128)(2,1)} %collective-permute-done.10.a1, bf16[256,1024]{1,0:T(8,128)(2,1)} %collective-permute-done.11.a2, ...), custom_call_target="tpu_custom_call" | custom-call | flops 2147483648 | bytes 25165824 | tf_op jit(solution)/shard_map/adam_step/pallas_call | solution.py:139
  127.2 2.0 copy-done.5
  130.2 4.0 %collective-permute-start.17 = (bf16[8,64,1024]{2,1,0:T(8,128)(2,1)}, bf16[8,64,1024]{2,1,0:T(8,128)(2,1)}, u32[]{:S(2)}, u32[]{:S(2)}) collective-permute-start(bf16[8,64,1024]{2,1,0:T(8,128)(2,1)} %get-tuple-element.46), channel_id=1, source_target_pairs={{0,8},{8,0},{16,24},{24,16},{32,40},{40,32},{48,56},{56,48},{64,72... | collective-permute-start | bytes 3145736 | tf_op jit(solution)/shard_map/ppermute | solution.py:41
  134.2 2.6 %collective-permute-done.17.got_ref = bf16[8,64,1024]{2,1,0:T(8,128)(2,1)} collective-permute-done((bf16[8,64,1024]{2,1,0:T(8,128)(2,1)}, bf16[8,64,1024]{2,1,0:T(8,128)(2,1)}, u32[]{:S(2)}, u32[]{:S(2)}) %collective-permute-start.17) | collective-permute-done | bytes 1048608 | tf_op jit(solution)/shard_map/ppermute | solution.py:41
  136.8 1.2 copy-done.17
  138.0 2.2 %core_sums.1 = (bf16[2,64,1024]{2,1,0:T(8,128)(2,1)S(1)}, bf16[2,64,1024]{2,1,0:T(8,128)(2,1)}, bf16[2,64,1024]{2,1,0:T(8,128)(2,1)}, bf16[2,64,1024]{2,1,0:T(8,128)(2,1)}) custom-call(s32[1]{0:T(128)} %bitcast.6.x_ref, bf16[8,64,1024]{2,1,0:T(8,128)(2,1)S(1)} %copy-done.17, bf16[8,64,1024]{2,1,0:T(8,128)(2,1)} %collective-permute-done.17.got_ref), custom_call_target="tpu_custom_call" | custom-call | bytes 3145728 | tf_op jit(solution)/shard_map/core_sums/pallas_call | solution.py:222
  140.2 1.2 collective-permute-start.18
  141.5 2.5 %collective-permute-start.19 = (bf16[2,64,1024]{2,1,0:T(8,128)(2,1)}, bf16[2,64,1024]{2,1,0:T(8,128)(2,1)}, u32[]{:S(2)}, u32[]{:S(2)}) collective-permute-start(bf16[2,64,1024]{2,1,0:T(8,128)(2,1)} %get-tuple-element.49), channel_id=1, source_target_pairs={{0,32},{8,40},{16,48},{24,56},{32,0},{40,8},{48,16},{56,24},{64,96... | collective-permute-start | bytes 786440 | tf_op jit(solution)/shard_map/ppermute | solution.py:41
  143.9 1.2 collective-permute-start.20
  147.2 3.3 %input_blocks.3 = (bf16[256,1024]{1,0:T(8,128)(2,1)S(1)}, bf16[256,1024]{1,0:T(8,128)(2,1)S(1)}, bf16[256,1024]{1,0:T(8,128)(2,1)S(1)}, bf16[256,1024]{1,0:T(8,128)(2,1)S(1)}) custom-call(bf16[1024,1024]{1,0:T(8,128)(2,1)S(1)} %bitcast_convert_fusion.w, bf16[256,1024]{1,0:T(8,128)(2,1)S(1)} %bitcast.30, bf16[256,1024]{1,0:T(8,128)(2,1)S(1)} %collective-permute-done.1.c1, ...), custom_call_target="tpu_custom_call" | custom-call | flops 2147483648 | bytes 6291456 | tf_op jit(solution)/shard_map/input_blocks/pallas_call | solution.py:170
  151.4 2.0 collective-permute-start.8
  153.4 2.5 %collective-permute-done.19.p2 = bf16[2,64,1024]{2,1,0:T(8,128)(2,1)} collective-permute-done((bf16[2,64,1024]{2,1,0:T(8,128)(2,1)}, bf16[2,64,1024]{2,1,0:T(8,128)(2,1)}, u32[]{:S(2)}, u32[]{:S(2)}) %collective-permute-start.19) | collective-permute-done | bytes 262176 | tf_op jit(solution)/shard_map/ppermute | solution.py:41
  155.9 1.7 collective-permute-start.9
  157.6 1.2 x_sums.1
  158.9 1.4 collective-permute-start.21
  160.3 4.6 %input_blocks.2 = (bf16[256,1024]{1,0:T(8,128)(2,1)S(1)}, bf16[256,1024]{1,0:T(8,128)(2,1)S(1)}, bf16[256,1024]{1,0:T(8,128)(2,1)S(1)}, bf16[256,1024]{1,0:T(8,128)(2,1)S(1)}) custom-call(bf16[1024,1024]{1,0:T(8,128)(2,1)} %collective-permute-done.w, bf16[256,1024]{1,0:T(8,128)(2,1)S(1)} %bitcast.31, bf16[256,1024]{1,0:T(8,128)(2,1)S(1)} %collective-permute-done.1.c1, ...), custom_call_target="tpu_custom_call" | custom-call | flops 2147483648 | bytes 6291456 | tf_op jit(solution)/shard_map/input_blocks/pallas_call | solution.py:170
  166.0 4.0 %collective-permute-done.22 = bf16[64,1024]{1,0:T(8,128)(2,1)S(1)} collective-permute-done((bf16[64,1024]{1,0:T(8,128)(2,1)S(1)}, bf16[64,1024]{1,0:T(8,128)(2,1)S(1)}, u32[]{:S(2)}, u32[]{:S(2)}) %collective-permute-start.22) | collective-permute-done | bytes 131104 | tf_op jit(solution)/shard_map/ppermute | solution.py:41
  170.0 2.0 collective-permute-start.5
  172.0 1.3 collective-permute-start.6
  173.3 2.2 %collective-permute-done.8.refs_2_ = bf16[256,1024]{1,0:T(8,128)(2,1)S(1)} collective-permute-done((bf16[256,1024]{1,0:T(8,128)(2,1)S(1)}, bf16[256,1024]{1,0:T(8,128)(2,1)S(1)}, u32[]{:S(2)}, u32[]{:S(2)}) %collective-permute-start.8) | collective-permute-done | bytes 524320 | tf_op jit(solution)/shard_map/ppermute | solution.py:23
  175.7 2.0 collective-permute-done.9.refs_3_
  177.9 11.9 %collective-permute-done.4.refs_1_ = bf16[256,1024]{1,0:T(8,128)(2,1)S(1)} collective-permute-done((bf16[256,1024]{1,0:T(8,128)(2,1)S(1)}, bf16[256,1024]{1,0:T(8,128)(2,1)S(1)}, u32[]{:S(2)}, u32[]{:S(2)}) %collective-permute-start.4) | collective-permute-done | bytes 524320 | tf_op jit(solution)/shard_map/ppermute | solution.py:23
  189.9 8.1 %collective-permute-done.5.refs_2_ = bf16[256,1024]{1,0:T(8,128)(2,1)S(1)} collective-permute-done((bf16[256,1024]{1,0:T(8,128)(2,1)S(1)}, bf16[256,1024]{1,0:T(8,128)(2,1)S(1)}, u32[]{:S(2)}, u32[]{:S(2)}) %collective-permute-start.5) | collective-permute-done | bytes 524320 | tf_op jit(solution)/shard_map/ppermute | solution.py:23
  197.9 2.1 %collective-permute-start.23 = (bf16[2,64,1024]{2,1,0:T(8,128)(2,1)S(1)}, bf16[2,64,1024]{2,1,0:T(8,128)(2,1)S(1)}, u32[]{:S(2)}, u32[]{:S(2)}) collective-permute-start(bf16[2,64,1024]{2,1,0:T(8,128)(2,1)S(1)} %pad_maximum_fusion.refs_0_), channel_id=1, source_target_pairs={{0,8},{8,0},{16,24},{24,16},{32,40},{40,32},{48,56},{56,48},{64,72... | collective-permute-start | bytes 786440 | tf_op jit(solution)/shard_map/ppermute | solution.py:41
  200.7 1.9 assemble.2.refs_4_
  202.7 1.9 assemble.3
  205.6 4.3 %mix.1 = f32[1024,1024]{1,0:T(8,128)} custom-call(s32[3]{0:T(128)S(1)} %pad_add_fusion.1.place_ref, f32[1024,1024]{1,0:T(8,128)S(1)} %copy-done.6, bf16[2,64,1024]{2,1,0:T(8,128)(2,1)S(1)} %pad_maximum_fusion.refs_0_, bf16[2,64,1024]{2,1,0:T(8,128)(2,1)S(1)} %collective-permute-done.23.refs_1_, bf16[2,64,1024]{2,1,0:T(8,128)(2,1)S(1)} %collective-permute-done.24.refs_2_, ...), custom_call_target="tpu_custom_call" | custom-call | bytes 10485760 | tf_op jit(solution)/shard_map/mix/pallas_call | solution.py:300
  (68 shorter events, 10.6 us)
Async XLA Ops:
  0.7 2.2 %copy-start = (bf16[1,256,8192]{2,1,0:T(8,128)(2,1)S(1)}, bf16[1,256,8192]{2,1,0:T(8,128)(2,1)}, u32[]{:S(2)}) copy-start(bf16[1,256,8192]{2,1,0:T(8,128)(2,1)} %param.7) | copy-start | bytes 12582916
  2.9 8.0 %copy-start.7 = (bf16[1,256,1024]{2,1,0:T(8,128)(2,1)S(1)}, bf16[1,256,1024]{2,1,0:T(8,128)(2,1)}, u32[]{:S(2)}) copy-start(bf16[1,256,1024]{2,1,0:T(8,128)(2,1)} %param.8) | copy-start | bytes 1572868
  5.1 15.1 %collective-permute-start.13 = (bf16[256,1024]{1,0:T(8,128)(2,1)S(1)}, bf16[256,1024]{1,0:T(8,128)(2,1)S(1)}, u32[]{:S(2)}, u32[]{:S(2)}) collective-permute-start(bf16[256,1024]{1,0:T(8,128)(2,1)S(1)} %get-tuple-element.41), channel_id=1, source_target_pairs={{0,1},{1,2},{2,3},{3,0},{4,5},{5,6},{6,7},{7,4},{8,9},{9,10},{10,1... | collective-permute-start | bytes 1572872 | tf_op jit(solution)/shard_map/ppermute | solution.py:23
  7.3 25.2 %collective-permute-start.14 = (bf16[256,1024]{1,0:T(8,128)(2,1)}, bf16[256,1024]{1,0:T(8,128)(2,1)S(1)}, u32[]{:S(2)}, u32[]{:S(2)}) collective-permute-start(bf16[256,1024]{1,0:T(8,128)(2,1)} %get-tuple-element.42), channel_id=1, source_target_pairs={{0,2},{1,3},{2,0},{3,1},{4,6},{5,7},{6,4},{7,5},{8,10},{9,11},{10,... | collective-permute-start | bytes 1572872 | tf_op jit(solution)/shard_map/ppermute | solution.py:23
  9.9 23.0 %collective-permute-start.15 = (bf16[256,1024]{1,0:T(8,128)(2,1)}, bf16[256,1024]{1,0:T(8,128)(2,1)}, u32[]{:S(2)}, u32[]{:S(2)}) collective-permute-start(bf16[256,1024]{1,0:T(8,128)(2,1)} %get-tuple-element.43), channel_id=1, source_target_pairs={{0,3},{1,0},{2,1},{3,2},{4,7},{5,4},{6,5},{7,6},{8,11},{9,8},{10,9... | collective-permute-start | bytes 1572872 | tf_op jit(solution)/shard_map/ppermute | solution.py:23
  10.9 31.7 %collective-permute-start.1 = (bf16[256,1024]{1,0:T(8,128)(2,1)S(1)}, bf16[256,1024]{1,0:T(8,128)(2,1)S(1)}, u32[]{:S(2)}, u32[]{:S(2)}) collective-permute-start(bf16[256,1024]{1,0:T(8,128)(2,1)S(1)} %bitcast.25), channel_id=1, source_target_pairs={{0,1},{1,2},{2,3},{3,0},{4,5},{5,6},{6,7},{7,4},{8,9},{9,10},{10,1... | collective-permute-start | bytes 1572872 | tf_op jit(solution)/shard_map/ppermute | solution.py:23
  11.3 43.6 %collective-permute-start.2 = (bf16[256,1024]{1,0:T(8,128)(2,1)S(1)}, bf16[256,1024]{1,0:T(8,128)(2,1)S(1)}, u32[]{:S(2)}, u32[]{:S(2)}) collective-permute-start(bf16[256,1024]{1,0:T(8,128)(2,1)S(1)} %bitcast.26), channel_id=1, source_target_pairs={{0,2},{1,3},{2,0},{3,1},{4,6},{5,7},{6,4},{7,5},{8,10},{9,11},{10,... | collective-permute-start | bytes 1572872 | tf_op jit(solution)/shard_map/ppermute | solution.py:23
  20.2 34.8 %collective-permute-start.3 = (bf16[256,1024]{1,0:T(8,128)(2,1)S(1)}, bf16[256,1024]{1,0:T(8,128)(2,1)S(1)}, u32[]{:S(2)}, u32[]{:S(2)}) collective-permute-start(bf16[256,1024]{1,0:T(8,128)(2,1)S(1)} %bitcast.27), channel_id=1, source_target_pairs={{0,3},{1,0},{2,1},{3,2},{4,7},{5,4},{6,5},{7,6},{8,11},{9,8},{10,9... | collective-permute-start | bytes 1572872 | tf_op jit(solution)/shard_map/ppermute | solution.py:23
  55.0 7.9 %copy-start.8 = (bf16[256,1024]{1,0:T(8,128)(2,1)}, bf16[256,1024]{1,0:T(8,128)(2,1)S(1)}, u32[]{:S(2)}) copy-start(bf16[256,1024]{1,0:T(8,128)(2,1)S(1)} %collective-permute-done.2.c2) | copy-start | bytes 1572868
  55.0 7.9 %copy-start.12 = (bf16[256,1024]{1,0:T(8,128)(2,1)}, bf16[256,1024]{1,0:T(8,128)(2,1)S(1)}, u32[]{:S(2)}) copy-start(bf16[256,1024]{1,0:T(8,128)(2,1)S(1)} %collective-permute-done.3.c3) | copy-start | bytes 1572868
  55.0 2.6 %copy-start.1 = (bf16[1,256,8192]{2,1,0:T(8,128)(2,1)S(1)}, bf16[1,256,8192]{2,1,0:T(8,128)(2,1)}, u32[]{:S(2)}) copy-start(bf16[1,256,8192]{2,1,0:T(8,128)(2,1)} %param.7) | copy-start | bytes 12582916
  57.5 8.9 %copy-start.3 = (f32[1,1024,1024]{2,1,0:T(8,128)S(1)}, f32[1,1024,1024]{2,1,0:T(8,128)}, u32[]{:S(2)}) copy-start(f32[1,1024,1024]{2,1,0:T(8,128)} %param.9) | copy-start | bytes 12582916
  62.8 48.3 %collective-permute-start.16 = (bf16[1024,1024]{1,0:T(8,128)(2,1)}, bf16[1024,1024]{1,0:T(8,128)(2,1)}, u32[]{:S(2)}, u32[]{:S(2)}) collective-permute-start(bf16[1024,1024]{1,0:T(8,128)(2,1)} %partial_sums.1), channel_id=1, source_target_pairs={{0,4},{1,5},{2,6},{3,7},{4,0},{5,1},{6,2},{7,3},{8,12},{9,13},{10,... | collective-permute-start | bytes 6291464 | tf_op jit(solution)/shard_map/ppermute | solution.py:28
  66.8 93.5 %collective-permute-start = (bf16[1024,1024]{1,0:T(8,128)(2,1)S(1)}, bf16[1024,1024]{1,0:T(8,128)(2,1)}, u32[]{:S(2)}, u32[]{:S(2)}) collective-permute-start(bf16[1024,1024]{1,0:T(8,128)(2,1)S(1)} %bitcast_convert_fusion.w), channel_id=1, source_target_pairs={{0,4},{1,5},{2,6},{3,7},{4,0},{5,1},{6,2},{7,3},{8,12},{9,13},{10,... | collective-permute-start | bytes 6291464 | tf_op jit(solution)/shard_map/ppermute | solution.py:28
  66.9 13.7 %collective-permute-start.10 = (bf16[256,1024]{1,0:T(8,128)(2,1)}, bf16[256,1024]{1,0:T(8,128)(2,1)}, u32[]{:S(2)}, u32[]{:S(2)}) collective-permute-start(bf16[256,1024]{1,0:T(8,128)(2,1)} %get-tuple-element.38), channel_id=1, source_target_pairs={{0,1},{1,2},{2,3},{3,0},{4,5},{5,6},{6,7},{7,4},{8,9},{9,10},{10,1... | collective-permute-start | bytes 1572872 | tf_op jit(solution)/shard_map/ppermute | solution.py:23
  68.1 25.6 %collective-permute-start.11 = (bf16[256,1024]{1,0:T(8,128)(2,1)}, bf16[256,1024]{1,0:T(8,128)(2,1)}, u32[]{:S(2)}, u32[]{:S(2)}) collective-permute-start(bf16[256,1024]{1,0:T(8,128)(2,1)} %get-tuple-element.39), channel_id=1, source_target_pairs={{0,2},{1,3},{2,0},{3,1},{4,6},{5,7},{6,4},{7,5},{8,10},{9,11},{10,... | collective-permute-start | bytes 1572872 | tf_op jit(solution)/shard_map/ppermute | solution.py:23
  71.0 22.8 %collective-permute-start.12 = (bf16[256,1024]{1,0:T(8,128)(2,1)}, bf16[256,1024]{1,0:T(8,128)(2,1)}, u32[]{:S(2)}, u32[]{:S(2)}) collective-permute-start(bf16[256,1024]{1,0:T(8,128)(2,1)} %get-tuple-element.40), channel_id=1, source_target_pairs={{0,3},{1,0},{2,1},{3,2},{4,7},{5,4},{6,5},{7,6},{8,11},{9,8},{10,9... | collective-permute-start | bytes 1572872 | tf_op jit(solution)/shard_map/ppermute | solution.py:23
  111.1 2.2 %copy-start.2 = (bf16[1,256,8192]{2,1,0:T(8,128)(2,1)S(1)}, bf16[1,256,8192]{2,1,0:T(8,128)(2,1)}, u32[]{:S(2)}) copy-start(bf16[1,256,8192]{2,1,0:T(8,128)(2,1)} %param.7) | copy-start | bytes 12582916
  113.3 2.2 %copy-start.4 = (f32[1,1024,1024]{2,1,0:T(8,128)S(1)}, f32[1,1024,1024]{2,1,0:T(8,128)}, u32[]{:S(2)}) copy-start(f32[1,1024,1024]{2,1,0:T(8,128)} %param.9) | copy-start | bytes 12582916
  115.5 1.0 copy-start.9
  116.6 1.0 copy-start.13
  127.2 2.0 copy-start.5
  130.2 6.6 %collective-permute-start.17 = (bf16[8,64,1024]{2,1,0:T(8,128)(2,1)}, bf16[8,64,1024]{2,1,0:T(8,128)(2,1)}, u32[]{:S(2)}, u32[]{:S(2)}) collective-permute-start(bf16[8,64,1024]{2,1,0:T(8,128)(2,1)} %get-tuple-element.46), channel_id=1, source_target_pairs={{0,8},{8,0},{16,24},{24,16},{32,40},{40,32},{48,56},{56,48},{64,72... | collective-permute-start | bytes 3145736 | tf_op jit(solution)/shard_map/ppermute | solution.py:41
  136.8 1.2 copy-start.17
  140.2 11.2 %collective-permute-start.18 = (bf16[2,64,1024]{2,1,0:T(8,128)(2,1)}, bf16[2,64,1024]{2,1,0:T(8,128)(2,1)}, u32[]{:S(2)}, u32[]{:S(2)}) collective-permute-start(bf16[2,64,1024]{2,1,0:T(8,128)(2,1)} %get-tuple-element.48), channel_id=1, source_target_pairs={{0,16},{8,24},{16,32},{24,40},{32,48},{40,56},{48,0},{56,8},{64,80... | collective-permute-start | bytes 786440 | tf_op jit(solution)/shard_map/ppermute | solution.py:41
  141.5 14.4 %collective-permute-start.19 = (bf16[2,64,1024]{2,1,0:T(8,128)(2,1)}, bf16[2,64,1024]{2,1,0:T(8,128)(2,1)}, u32[]{:S(2)}, u32[]{:S(2)}) collective-permute-start(bf16[2,64,1024]{2,1,0:T(8,128)(2,1)} %get-tuple-element.49), channel_id=1, source_target_pairs={{0,32},{8,40},{16,48},{24,56},{32,0},{40,8},{48,16},{56,24},{64,96... | collective-permute-start | bytes 786440 | tf_op jit(solution)/shard_map/ppermute | solution.py:41
  143.9 13.7 %collective-permute-start.20 = (bf16[2,64,1024]{2,1,0:T(8,128)(2,1)}, bf16[2,64,1024]{2,1,0:T(8,128)(2,1)}, u32[]{:S(2)}, u32[]{:S(2)}) collective-permute-start(bf16[2,64,1024]{2,1,0:T(8,128)(2,1)} %get-tuple-element.50), channel_id=1, source_target_pairs={{0,48},{8,56},{16,0},{24,8},{32,16},{40,24},{48,32},{56,40},{64,11... | collective-permute-start | bytes 786440 | tf_op jit(solution)/shard_map/ppermute | solution.py:41
  145.1 1.0 copy-start.10
  147.1 13.2 %copy-start.11 = (bf16[256,1024]{1,0:T(8,128)(2,1)S(1)}, bf16[256,1024]{1,0:T(8,128)(2,1)}, u32[]{:S(2)}) copy-start(bf16[256,1024]{1,0:T(8,128)(2,1)} %copy-done.8) | copy-start | bytes 1572868
  147.1 13.2 %copy-start.15 = (bf16[256,1024]{1,0:T(8,128)(2,1)S(1)}, bf16[256,1024]{1,0:T(8,128)(2,1)}, u32[]{:S(2)}) copy-start(bf16[256,1024]{1,0:T(8,128)(2,1)} %copy-done.12) | copy-start | bytes 1572868
  150.4 21.6 %collective-permute-start.7 = (bf16[256,1024]{1,0:T(8,128)(2,1)S(1)}, bf16[256,1024]{1,0:T(8,128)(2,1)S(1)}, u32[]{:S(2)}, u32[]{:S(2)}) collective-permute-start(bf16[256,1024]{1,0:T(8,128)(2,1)S(1)} %get-tuple-element.35), channel_id=1, source_target_pairs={{0,1},{1,2},{2,3},{3,0},{4,5},{5,6},{6,7},{7,4},{8,9},{9,10},{10,1... | collective-permute-start | bytes 1572872 | tf_op jit(solution)/shard_map/ppermute | solution.py:23
  151.4 24.0 %collective-permute-start.8 = (bf16[256,1024]{1,0:T(8,128)(2,1)S(1)}, bf16[256,1024]{1,0:T(8,128)(2,1)S(1)}, u32[]{:S(2)}, u32[]{:S(2)}) collective-permute-start(bf16[256,1024]{1,0:T(8,128)(2,1)S(1)} %get-tuple-element.36), channel_id=1, source_target_pairs={{0,2},{1,3},{2,0},{3,1},{4,6},{5,7},{6,4},{7,5},{8,10},{9,11},{10,... | collective-permute-start | bytes 1572872 | tf_op jit(solution)/shard_map/ppermute | solution.py:23
  155.9 21.8 %collective-permute-start.9 = (bf16[256,1024]{1,0:T(8,128)(2,1)S(1)}, bf16[256,1024]{1,0:T(8,128)(2,1)S(1)}, u32[]{:S(2)}, u32[]{:S(2)}) collective-permute-start(bf16[256,1024]{1,0:T(8,128)(2,1)S(1)} %get-tuple-element.37), channel_id=1, source_target_pairs={{0,3},{1,0},{2,1},{3,2},{4,7},{5,4},{6,5},{7,6},{8,11},{9,8},{10,9... | collective-permute-start | bytes 1572872 | tf_op jit(solution)/shard_map/ppermute | solution.py:23
  158.9 6.1 %copy-start.18 = (f32[1,64,1024]{2,1,0:T(8,128)S(1)}, f32[1,64,1024]{2,1,0:T(8,128)}, u32[]{:S(2)}) copy-start(f32[1,64,1024]{2,1,0:T(8,128)} %param.12) | copy-start | bytes 786436
  158.9 6.1 %copy-start.19 = (f32[1,64,1024]{2,1,0:T(8,128)S(1)}, f32[1,64,1024]{2,1,0:T(8,128)}, u32[]{:S(2)}) copy-start(f32[1,64,1024]{2,1,0:T(8,128)} %param.13) | copy-start | bytes 786436
  158.9 6.1 %collective-permute-start.21 = (bf16[64,1024]{1,0:T(8,128)(2,1)S(1)}, bf16[64,1024]{1,0:T(8,128)(2,1)S(1)}, u32[]{:S(2)}, u32[]{:S(2)}) collective-permute-start(bf16[64,1024]{1,0:T(8,128)(2,1)S(1)} %get-tuple-element.52), channel_id=1, source_target_pairs={{0,64},{8,72},{16,80},{24,88},{32,96},{40,104},{48,112},{56,120},{... | collective-permute-start | bytes 393224 | tf_op jit(solution)/shard_map/ppermute | solution.py:41
  164.9 25.0 %collective-permute-start.4 = (bf16[256,1024]{1,0:T(8,128)(2,1)S(1)}, bf16[256,1024]{1,0:T(8,128)(2,1)S(1)}, u32[]{:S(2)}, u32[]{:S(2)}) collective-permute-start(bf16[256,1024]{1,0:T(8,128)(2,1)S(1)} %get-tuple-element.31), channel_id=1, source_target_pairs={{0,1},{1,2},{2,3},{3,0},{4,5},{5,6},{6,7},{7,4},{8,9},{9,10},{10,1... | collective-permute-start | bytes 1572872 | tf_op jit(solution)/shard_map/ppermute | solution.py:23
  165.9 4.1 %collective-permute-start.22 = (bf16[64,1024]{1,0:T(8,128)(2,1)S(1)}, bf16[64,1024]{1,0:T(8,128)(2,1)S(1)}, u32[]{:S(2)}, u32[]{:S(2)}) collective-permute-start(bf16[64,1024]{1,0:T(8,128)(2,1)S(1)} %get-tuple-element.53), channel_id=1, source_target_pairs={{0,64},{8,72},{16,80},{24,88},{32,96},{40,104},{48,112},{56,120},{... | collective-permute-start | bytes 393224 | tf_op jit(solution)/shard_map/ppermute | solution.py:41
  170.0 27.9 %collective-permute-start.5 = (bf16[256,1024]{1,0:T(8,128)(2,1)S(1)}, bf16[256,1024]{1,0:T(8,128)(2,1)S(1)}, u32[]{:S(2)}, u32[]{:S(2)}) collective-permute-start(bf16[256,1024]{1,0:T(8,128)(2,1)S(1)} %get-tuple-element.32), channel_id=1, source_target_pairs={{0,2},{1,3},{2,0},{3,1},{4,6},{5,7},{6,4},{7,5},{8,10},{9,11},{10,... | collective-permute-start | bytes 1572872 | tf_op jit(solution)/shard_map/ppermute | solution.py:23
  172.0 30.6 %collective-permute-start.6 = (bf16[256,1024]{1,0:T(8,128)(2,1)S(1)}, bf16[256,1024]{1,0:T(8,128)(2,1)S(1)}, u32[]{:S(2)}, u32[]{:S(2)}) collective-permute-start(bf16[256,1024]{1,0:T(8,128)(2,1)S(1)} %get-tuple-element.33), channel_id=1, source_target_pairs={{0,3},{1,0},{2,1},{3,2},{4,7},{5,4},{6,5},{7,6},{8,11},{9,8},{10,9... | collective-permute-start | bytes 1572872 | tf_op jit(solution)/shard_map/ppermute | solution.py:23
  175.4 24.6 %collective-permute-start.24 = (bf16[2,64,1024]{2,1,0:T(8,128)(2,1)S(1)}, bf16[2,64,1024]{2,1,0:T(8,128)(2,1)S(1)}, u32[]{:S(2)}, u32[]{:S(2)}) collective-permute-start(bf16[2,64,1024]{2,1,0:T(8,128)(2,1)S(1)} %pad_maximum_fusion.refs_0_), channel_id=1, source_target_pairs={{0,16},{8,24},{16,32},{24,40},{32,48},{40,56},{48,0},{56,8},{64,80... | collective-permute-start | bytes 786440 | tf_op jit(solution)/shard_map/ppermute | solution.py:41
  177.7 22.3 %collective-permute-start.26 = (bf16[2,64,1024]{2,1,0:T(8,128)(2,1)S(1)}, bf16[2,64,1024]{2,1,0:T(8,128)(2,1)S(1)}, u32[]{:S(2)}, u32[]{:S(2)}) collective-permute-start(bf16[2,64,1024]{2,1,0:T(8,128)(2,1)S(1)} %pad_maximum_fusion.refs_0_), channel_id=1, source_target_pairs={{0,32},{8,40},{16,48},{24,56},{32,0},{40,8},{48,16},{56,24},{64,96... | collective-permute-start | bytes 786440 | tf_op jit(solution)/shard_map/ppermute | solution.py:41
  189.9 10.7 %collective-permute-start.28 = (bf16[2,64,1024]{2,1,0:T(8,128)(2,1)S(1)}, bf16[2,64,1024]{2,1,0:T(8,128)(2,1)S(1)}, u32[]{:S(2)}, u32[]{:S(2)}) collective-permute-start(bf16[2,64,1024]{2,1,0:T(8,128)(2,1)S(1)} %pad_maximum_fusion.refs_0_), channel_id=1, source_target_pairs={{0,48},{8,56},{16,0},{24,8},{32,16},{40,24},{48,32},{56,40},{64,11... | collective-permute-start | bytes 786440 | tf_op jit(solution)/shard_map/ppermute | solution.py:41
  197.9 6.6 %collective-permute-start.23 = (bf16[2,64,1024]{2,1,0:T(8,128)(2,1)S(1)}, bf16[2,64,1024]{2,1,0:T(8,128)(2,1)S(1)}, u32[]{:S(2)}, u32[]{:S(2)}) collective-permute-start(bf16[2,64,1024]{2,1,0:T(8,128)(2,1)S(1)} %pad_maximum_fusion.refs_0_), channel_id=1, source_target_pairs={{0,8},{8,0},{16,24},{24,16},{32,40},{40,32},{48,56},{56,48},{64,72... | collective-permute-start | bytes 786440 | tf_op jit(solution)/shard_map/ppermute | solution.py:41
  200.1 4.5 %collective-permute-start.25 = (bf16[2,64,1024]{2,1,0:T(8,128)(2,1)S(1)}, bf16[2,64,1024]{2,1,0:T(8,128)(2,1)S(1)}, u32[]{:S(2)}, u32[]{:S(2)}) collective-permute-start(bf16[2,64,1024]{2,1,0:T(8,128)(2,1)S(1)} %collective-permute-done.24.refs_2_), channel_id=1, source_target_pairs={{0,8},{8,0},{16,24},{24,16},{32,40},{40,32},{48,56},{56,48},{64,72... | collective-permute-start | bytes 786440 | tf_op jit(solution)/shard_map/ppermute | solution.py:41
  200.1 4.5 %collective-permute-start.27 = (bf16[2,64,1024]{2,1,0:T(8,128)(2,1)S(1)}, bf16[2,64,1024]{2,1,0:T(8,128)(2,1)S(1)}, u32[]{:S(2)}, u32[]{:S(2)}) collective-permute-start(bf16[2,64,1024]{2,1,0:T(8,128)(2,1)S(1)} %collective-permute-done.26.refs_4_), channel_id=1, source_target_pairs={{0,8},{8,0},{16,24},{24,16},{32,40},{40,32},{48,56},{56,48},{64,72... | collective-permute-start | bytes 786440 | tf_op jit(solution)/shard_map/ppermute | solution.py:41
  200.6 4.0 %collective-permute-start.29 = (bf16[2,64,1024]{2,1,0:T(8,128)(2,1)S(1)}, bf16[2,64,1024]{2,1,0:T(8,128)(2,1)S(1)}, u32[]{:S(2)}, u32[]{:S(2)}) collective-permute-start(bf16[2,64,1024]{2,1,0:T(8,128)(2,1)S(1)} %collective-permute-done.28.refs_6_), channel_id=1, source_target_pairs={{0,8},{8,0},{16,24},{24,16},{32,40},{40,32},{48,56},{56,48},{64,72... | collective-permute-start | bytes 786440 | tf_op jit(solution)/shard_map/ppermute | solution.py:41
  202.6 2.9 %copy-start.6 = (f32[1024,1024]{1,0:T(8,128)S(1)}, f32[1024,1024]{1,0:T(8,128)}, u32[]{:S(2)}) copy-start(f32[1024,1024]{1,0:T(8,128)} %copy-done.5) | copy-start | bytes 12582916
  (2 other events, 2.0 us)

commit v2 on v0

v2 whole, which is shorter than its diff:
```python
import math

import jax
import jax.numpy as jnp
from jax import lax
from jax.experimental import pallas as pl
from jax.experimental.pallas import tpu as pltpu
from jax.sharding import PartitionSpec as P

STEP = 10
BF = jnp.bfloat16
F32 = jnp.float32
ROWS = 1024
HALF = 512
KV = 1024
TOK = 256
TILE = 256
MIB = 1 << 20
ANY = pl.BlockSpec(memory_space=pl.ANY)
VM = pl.BlockSpec(memory_space=pltpu.VMEM)
SM = pl.BlockSpec(memory_space=pltpu.SMEM)
HBM = pl.BlockSpec(memory_space=pltpu.HBM)
DIMS_T = (((0,), (0,)), ((), ()))
DIMS_N = (((1,), (1,)), ((), ()))


def f_index(zh, y):
    return (zh % 2) * 4 + y % 4


def along_y(array, step):
    pairs = [(f_index(z, y), f_index(z, y + step)) for z in range(2) for y in range(4)]
    return lax.ppermute(array, "fsdp", pairs)


def swap_z(array):
    pairs = [(f_index(z, y), f_index(z + 1, y)) for z in range(2) for y in range(4)]
    return lax.ppermute(array, "fsdp", pairs)


def island_shift(array, dz, dx, dc):
    def index(z, x, c):
        return ((z % 2) * 4 + x % 4) * 2 + c % 2

    pairs = [
        (index(z, x, c), index(z + dz, x + dx, c + dc))
        for z in range(2)
        for x in range(4)
        for c in range(2)
    ]
    return lax.ppermute(array, "island", pairs)


def cost(moved):
    return pl.CostEstimate(flops=0, bytes_accessed=moved, transcendentals=0)


def params(mib):
    return pltpu.CompilerParams(vmem_limit_bytes=mib * MIB)


def in_hbm(array):
    return pltpu.with_memory_space_constraint(array, pltpu.HBM)


def shape(*dims, dtype=BF):
    return jax.ShapeDtypeStruct(dims, dtype)


def gate(array, *earlier):
    def kernel(*refs):
        pass

    return pl.pallas_call(
        kernel,
        out_shape=shape(*array.shape, dtype=array.dtype),
        in_specs=[ANY] * (1 + len(earlier)),
        out_specs=ANY,
        input_output_aliases={0: 0},
        cost_estimate=cost(1),
        compiler_params=params(1),
        name="gate",
    )(array, *earlier)


def pack(place, acts, cot, master):
    tiles = ROWS // TILE

    def kernel(place_ref, acts_ref, cot_ref, w_ref, *refs):
        first, second, third, own, weight, wide, sems, w_sems = refs[:3], refs[3:6], refs[6:9], *refs[9:]
        zh, y = place_ref[0], place_ref[1]

        def columns(z, dy, start, width):
            block = z * 4 + lax.rem(y + dy, 4)
            return acts_ref.at[:, pl.ds(pl.multiple_of(block * ROWS + start, HALF), width)]

        loads = [
            pltpu.make_async_copy(w_ref.at[pl.ds(t * TILE, TILE)], wide.at[t], w_sems.at[t])
            for t in range(tiles)
        ]
        moves = []
        for n in range(3):
            moves.append((cot_ref, first[n].at[:, pl.ds(0, KV)]))
            moves.append((columns(1 - zh, n + 1, 0, HALF), first[n].at[:, pl.ds(KV, HALF)]))
            moves.append((columns(1 - zh, n + 1, HALF, HALF), second[n]))
            moves.append((columns(zh, n + 1, 0, ROWS), third[n]))
        moves.append((columns(1 - zh, 0, 0, ROWS), own.at[:, pl.ds(0, ROWS)]))
        moves.append((columns(zh, 0, 0, ROWS), own.at[:, pl.ds(ROWS, ROWS)]))
        copies = [pltpu.make_async_copy(a, b, sems.at[n]) for n, (a, b) in enumerate(moves)]
        for load in loads:
            load.start()
        for copy in copies:
            copy.start()
        for t, load in enumerate(loads):
            load.wait()
            weight[pl.ds(t * TILE, TILE), :] = wide[t].astype(BF)
        for copy in copies:
            copy.wait()

    outs = pl.pallas_call(
        kernel,
        out_shape=[shape(TOK, KV + HALF)] * 3
        + [shape(TOK, HALF)] * 3
        + [shape(TOK, ROWS)] * 3
        + [shape(TOK, 2 * ROWS), shape(ROWS, KV)],
        in_specs=[SM, HBM, HBM, HBM],
        out_specs=[VM] * 11,
        scratch_shapes=[
            pltpu.VMEM((tiles, TILE, KV), F32),
            pltpu.SemaphoreType.DMA((14,)),
            pltpu.SemaphoreType.DMA((tiles,)),
        ],
        cost_estimate=cost(1),
        compiler_params=params(16),
        name="pack",
    )(place, acts, cot, master)
    return outs[:3], outs[3:6], outs[6:9], *outs[9:]


def group_sums(dtype, acts, cots, earlier=()):
    def kernel(*refs):
        a, c, out = refs[:4], refs[4:8], refs[-1]
        total = None
        for k in range(4):
            term = lax.dot_general(a[k][...], c[k][...], DIMS_T, preferred_element_type=F32)
            total = term if total is None else total + term
        out[...] = total.astype(dtype)

    def strip(first):
        return pl.BlockSpec((TOK, TILE), lambda j: (0, first // TILE + j))

    whole = pl.BlockSpec((TOK, KV), lambda j: (0, 0))
    return pl.pallas_call(
        kernel,
        out_shape=shape(HALF, KV, dtype=dtype),
        grid=(HALF // TILE,),
        in_specs=[strip(first) for _, first in acts] + [whole] * 4 + [ANY] * len(earlier),
        out_specs=pl.BlockSpec((TILE, KV), lambda j: (j, 0)),
        cost_estimate=cost(1),
        compiler_params=params(16),
        name="group_sums",
    )(*[a for a, _ in acts], *cots, *earlier)


def adam(half, core, own, received, master, first, second, earlier):
    tile = 64
    count = HALF // tile
    from_one = 0.5 / (1.0 - 0.9**STEP)
    from_two = 1.0 / math.sqrt(1.0 - 0.95**STEP)

    def kernel(core_ref, g_ref, got_ref, w_ref, m1_ref, m2_ref, *refs):
        upd_ref, keep, send, g, got, w, m1, m2, upd, sems, out_sems = refs[-11:]
        pairs = ((g_ref, g, 0), (got_ref, got, 0), (w_ref, w, 1), (m1_ref, m1, 1), (m2_ref, m2, 1))
        loads = []
        for t in range(count):
            loads.append(
                [
                    pltpu.make_async_copy(
                        src.at[pl.ds(t * tile + far * half * HALF, tile)], dst.at[t], sems.at[n, t]
                    )
                    for n, (src, dst, far) in enumerate(pairs)
                ]
            )
        for row in loads:
            for load in row:
                load.start()
        stores = []
        for t, row in enumerate(loads):
            for load in row:
                load.wait()
            grad = g[t] + got[t].astype(F32)
            one = 0.9 * m1[t] + 0.1 * grad
            two = 0.95 * m2[t] + 0.05 * grad * grad
            root = two * lax.rsqrt(two)
            new = w[t] - from_one * one / (root * from_two + 1e-8)
            upd[t] = new

            @pl.when(core_ref[0] == t % 2)
            def _():
                keep[t // 2] = new.astype(BF)

            @pl.when(core_ref[0] != t % 2)
            def _():
                send[t // 2] = new.astype(BF)

            store = pltpu.make_async_copy(
                upd.at[t], upd_ref.at[pl.ds(t * tile, tile)], out_sems.at[t]
            )
            store.start()
            stores.append(store)
        for store in stores:
            store.wait()

    return pl.pallas_call(
        kernel,
        out_shape=[shape(HALF, KV, dtype=F32), shape(4, 64, KV), shape(4, 64, KV)],
        in_specs=[SM, ANY, ANY, HBM, HBM, HBM] + [ANY] * len(earlier),
        out_specs=[ANY, VM, VM],
        scratch_shapes=[
            pltpu.VMEM((count, tile, KV), F32),
            pltpu.VMEM((count, tile, KV), BF),
        ]
        + [pltpu.VMEM((count, tile, KV), F32)] * 4
        + [pltpu.SemaphoreType.DMA((5, count)), pltpu.SemaphoreType.DMA((count,))],
        cost_estimate=cost(1),
        compiler_params=params(20),
        name="adam_step",
    )(core, own, received, master, first, second, *earlier)


def input_blocks(weight, weight_got, cots, earlier):
    count = ROWS // TILE

    def kernel(w0, w1, c0, c1, c2, c3, *refs):
        outs, joined = refs[-5:-1], refs[-1]
        step = pl.program_id(0)

        @pl.when(step == 0)
        def _():
            for k, c in enumerate((c0, c1, c2, c3)):
                joined[pl.ds(k * TOK, TOK), :] = c[...]

        def fill(w):
            product = lax.dot_general(joined[...], w[...], DIMS_N, preferred_element_type=F32)
            for k, out in enumerate(outs):
                out[...] = product[k * TOK : (k + 1) * TOK].astype(BF)

        @pl.when(step < count)
        def _():
            fill(w0)

        @pl.when(step >= count)
        def _():
            fill(w1)

    def tile(start):
        return pl.BlockSpec((TILE, KV), lambda j: (jnp.clip(j - start, 0, count - 1), 0))

    whole = pl.BlockSpec((TOK, KV), lambda j: (0, 0))
    return pl.pallas_call(
        kernel,
        out_shape=[shape(TOK, 2 * ROWS)] * 4,
        grid=(2 * count,),
        in_specs=[tile(0), tile(count)] + [whole] * 4 + [ANY] * len(earlier),
        out_specs=[pl.BlockSpec((TOK, TILE), lambda j: (0, j))] * 4,
        scratch_shapes=[pltpu.VMEM((4 * TOK, KV), BF)],
        cost_estimate=cost(1),
        compiler_params=params(20),
        name="input_blocks",
    )(weight, weight_got, *cots, *earlier)


def assemble(place, blocks, earlier):
    def kernel(place_ref, *refs):
        ins, out, sems = refs[:4], refs[-2], refs[-1]
        zh, y = place_ref[0], place_ref[1]
        copies = []
        for k in range(4):
            for dz in range(2):
                block = lax.rem(zh + dz, 2) * 4 + lax.rem(y + 4 - k, 4)
                columns = pl.ds(pl.multiple_of(block * ROWS, ROWS), ROWS)
                part = ins[k].at[:, pl.ds(dz * ROWS, ROWS)]
                copies.append(
                    pltpu.make_async_copy(part, out.at[:, columns], sems.at[2 * k + dz])
                )
        for copy in copies:
            copy.start()
        for copy in copies:
            copy.wait()

    return pl.pallas_call(
        kernel,
        out_shape=shape(TOK, 8 * ROWS),
        in_specs=[SM] + [VM] * 4 + [ANY] * len(earlier),
        out_specs=ANY,
        scratch_shapes=[pltpu.SemaphoreType.DMA((8,))],
        cost_estimate=cost(1),
        compiler_params=params(8),
        name="assemble",
    )(place, *blocks, *earlier)


def core_sums(x_place, keep, received):
    def kernel(x_ref, keep_ref, got_ref, *outs):
        for dx in range(4):
            at = lax.rem(x_ref[0] + dx, 4)
            outs[dx][...] = (keep_ref[at].astype(F32) + got_ref[at].astype(F32)).astype(BF)

    return pl.pallas_call(
        kernel,
        out_shape=[shape(64, KV)] * 4,
        in_specs=[SM, VM, VM],
        out_specs=[VM] * 4,
        cost_estimate=cost(1),
        compiler_params=params(4),
        name="core_sums",
    )(x_place, keep, received)


def x_sums(half, zl, parts, anchor, momentum):
    def kernel(z_ref, p0, p1, p2, p3, w, m, wide, rounded):
        total = (p0[...].astype(F32) + p1[...].astype(F32)) + (
            p2[...].astype(F32) + p3[...].astype(F32)
        )
        wide[...] = total
        base = (16.0 / 1.33) * (-0.33 * w[...] - 0.567 * m[...])
        owner = jnp.broadcast_to(z_ref[0] == half, total.shape)
        rounded[...] = (total + jnp.where(owner, base, 0.0)).astype(BF)

    return pl.pallas_call(
        kernel,
        out_shape=[shape(64, KV, dtype=F32), shape(64, KV)],
        in_specs=[SM] + [VM] * 6,
        out_specs=[VM] * 2,
        cost_estimate=cost(1),
        compiler_params=params(4),
        name="x_sums",
    )(zl, *parts, anchor, momentum)


def outer_step(half, zl, mine, received, anchor, momentum, former):
    def kernel(z_ref, s, got, w, m, *refs):
        new_w, new_m, rounded = refs[-3:]
        total = s[...] + got[...].astype(F32)
        pseudo = w[...] - total / 16.0
        speed = 0.9 * m[...] + pseudo
        fresh = w[...] - 0.7 * (pseudo + 0.9 * speed)
        owner = jnp.broadcast_to(z_ref[0] == half, fresh.shape)
        rounded[...] = jnp.where(owner, fresh, (1.33 / 16.0) * total).astype(BF)
        if half:
            new_w[...] = jnp.where(owner, fresh, refs[0][...])
            new_m[...] = jnp.where(owner, speed, refs[1][...])
        else:
            new_w[...] = fresh
            new_m[...] = speed

    return pl.pallas_call(
        kernel,
        out_shape=[shape(64, KV, dtype=F32), shape(64, KV, dtype=F32), shape(64, KV)],
        in_specs=[SM] + [VM] * (4 + len(former)),
        out_specs=[VM] * 3,
        cost_estimate=cost(1),
        compiler_params=params(8),
        name="outer_step",
    )(zl, mine, received, anchor, momentum, *former)


def mix(half, place, updated, blocks, base):
    extra = [] if base is None else [base]

    def kernel(place_ref, upd, *refs):
        ins, out = refs[:8], refs[-1]
        dx = pl.program_id(0)
        for k in range(4):

            @pl.when(dx == k)
            def _():
                for dc in range(2):
                    core = lax.rem(place_ref[1] + dc, 2)
                    rows = pl.ds(pl.multiple_of(core * 64, 64), 64)
                    out[rows, :] = 0.5 * upd[rows, :] + 0.5 * ins[2 * k + dc][...].astype(F32)

    def here(dx, place):
        return (lax.rem(place[0] + 4 - dx, 4), 0)

    def there(dx, place):
        return (half * 4 + lax.rem(place[0] + 4 - dx, 4), 0)

    block = pl.BlockSpec((64, KV), lambda dx, place: (0, 0))
    return pl.pallas_call(
        kernel,
        out_shape=shape(ROWS, KV, dtype=F32),
        grid_spec=pltpu.PrefetchScalarGridSpec(
            num_scalar_prefetch=1,
            grid=(4,),
            in_specs=[pl.BlockSpec((128, KV), here)] + [block] * 8 + [ANY] * len(extra),
            out_specs=pl.BlockSpec((128, KV), there),
        ),
        input_output_aliases={10: 0} if extra else {},
        cost_estimate=cost(1),
        compiler_params=params(8),
        name="mix",
    )(place, updated, *blocks, *extra)


def shards(
    acts, cotangent, inner_weight, first_moment, second_moment, outer_weight, outer_momentum
):
    acts, cot, master = in_hbm(acts[0]), cotangent[0], in_hbm(inner_weight[0])
    moments = in_hbm(first_moment[0]), in_hbm(second_moment[0])
    anchor, momentum = outer_weight[0], outer_momentum[0]
    f, i = lax.axis_index("fsdp"), lax.axis_index("island")
    f_place = jnp.stack([f // 4, f % 4]).astype(jnp.int32)
    x_core = jnp.stack([(i // 2) % 4, i % 2]).astype(jnp.int32)
    zl, core = (i // 8).astype(jnp.int32)[None], (i % 2).astype(jnp.int32)[None]

    first, second, third, own, weight = pack(f_place, acts, in_hbm(cot), master)
    first = [along_y(a, k + 1) for k, a in enumerate(first)]
    weight_got = swap_z(weight)
    second = [along_y(gate(a, first[k]), k + 1) for k, a in enumerate(second)]
    third = [along_y(gate(a, second[k]), k + 1) for k, a in enumerate(third)]
    cots = [cot] + first

    partial_0 = group_sums(BF, [(own, 0)] + [(a, KV) for a in first], cots)
    got_0 = swap_z(partial_0)
    partial_1 = group_sums(
        BF, [(own, HALF)] + [(a, 0) for a in second], cots, [weight_got]
    )
    got_1 = swap_z(partial_1)
    blocks = input_blocks(weight, weight_got, cots, [partial_1])
    near = [along_y(gate(blocks[4 - k], *third), k) for k in (1, 3)]

    mine = [(own, ROWS)] + [(a, 0) for a in third]
    grad_0 = group_sums(F32, mine, cots, [blocks[0]])
    updated_0, keep_0, send_0 = adam(
        0, core, grad_0, got_0, master, *moments, []
    )
    grad_1 = group_sums(F32, [(a, c + HALF) for a, c in mine], cots, [send_0])

    def over_x(keep, send):
        sums = core_sums(x_core, keep, island_shift(send, 0, 0, 1))
        return [sums[0]] + [island_shift(sums[k], 0, k, 0) for k in (1, 2, 3)]

    def spread(fresh):
        lines = [fresh] + [island_shift(fresh, 0, k, 0) for k in (1, 2, 3)]
        return [part for line in lines for part in (line, island_shift(line, 0, 0, 1))]

    wide_0, rounded_0 = x_sums(0, zl, over_x(keep_0, send_0), anchor, momentum)
    updated_1, keep_1, send_1 = adam(
        1, core, grad_1, got_1, master, *moments, [rounded_0]
    )
    *former, fresh_0 = outer_step(
        0, zl, wide_0, island_shift(rounded_0, 1, 0, 0), anchor, momentum, []
    )
    sums_1 = over_x(keep_1, send_1)
    wide_1, rounded_1 = x_sums(1, zl, sums_1, anchor, momentum)
    far = along_y(gate(blocks[2], *near, sums_1[0]), 2)
    lines_0 = spread(gate(fresh_0, sums_1[1]))
    *former, fresh_1 = outer_step(
        1, zl, wide_1, island_shift(rounded_1, 1, 0, 0), anchor, momentum, former
    )
    lines_1 = spread(fresh_1)
    mixed = mix(0, x_core, gate(updated_0, rounded_1), lines_0, None)
    mixed = mix(1, x_core, updated_1, lines_1, mixed)
    input_grad = assemble(f_place, [blocks[0], near[0], far, near[1]], [lines_1[2]])
    new_outer, new_momentum = former
    return (input_grad[None], mixed[None], new_outer[None], new_momentum[None])


def solution(mesh):
    by_island = P("island", "fsdp", None)
    by_rows = P("fsdp", "island", None)
    return jax.shard_map(
        shards,
        mesh=mesh,
        in_specs=(by_island,) * 5 + (by_rows,) * 2,
        out_specs=(by_island, by_island, by_rows, by_rows),
        check_vma=False,
    )
```

time: 521 us -> 169 us (0.32)
  waiting for transfers between devices: 466 us -> 60.5 us
  starting transfers between devices: 0.16 us -> 53 us
  Pallas kernels: 0 us -> 45 us
  other arithmetic: 20.1 us -> 0.15 us
  matrix products: 19.9 us -> 0 us
  between operations: 13.8 us -> 1.06 us
  local copies, waits for them, and re-layouts: 1.01 us -> 9.25 us
    reduce_scatter x2 -> x0, waiting for transfers between devices: 252 us -> none  [the longest x1 194 us: shards(): lax.psum_scatter(lax.dot_general(local_acts, local_cot, (((0,), (0,)), ((...]
    all_gather x2 -> x0, waiting for transfers between devices: 214 us -> none  [the longest x1 189 us: shards(): lax.all_gather(weight_bf, 'fsdp', axis=0, tiled=True)]
    ppermute x0 -> x39, waiting for transfers between devices: none -> 60.5 us  [the longest x12 47.4 us: along_y(): return lax.ppermute(array, 'fsdp', pairs)]
    ppermute x0 -> x39, starting transfers between devices: none -> 53 us  [the longest x24 30.7 us: island_shift(): return lax.ppermute(array, 'island', pairs)]
    pallas_call x0 -> x28, Pallas kernels: none -> 45 us  [the longest x4 10.2 us: group_sums(): pl.pallas_call(kernel, out_shape=shape(HALF, KV, dtype=dtype), grid=(HALF...]
    dot_general x2 -> x0, matrix products: 19.9 us -> none  [the longest x1 10.4 us: shards(): lax.dot_general(local_acts, local_cot, (((0,), (0,)), ((), ())), preferre...]
    convert_element_type x2 -> x0, other arithmetic: 12.3 us -> none  [the longest x1 8.43 us: shards(): updated.astype(jnp.bfloat16)]
    unnamed x6 -> x40, local copies, waits for them, and re-layouts: 1.01 us -> 9.25 us
  transfers between devices with their start and end apart: 4 -> 39, of which waited for: 4 -> 15; matrix products, arithmetic and copies ran while one was open for 3% -> 0% of each run, Pallas kernels for 0% -> 21%
where the time goes in v2:
time: 169 us
  waiting for transfers between devices  60.5 us (36%)
  starting transfers between devices  53 us (31%)
  Pallas kernels  45 us (27%)
  local copies, waits for them, and re-layouts  9.25 us (5%)
    ppermute x12, waiting for transfers between devices, along_y(): return lax.ppermute(array, 'fsdp', pairs)  47.4 us
    ppermute x24, starting transfers between devices, island_shift(): return lax.ppermute(array, 'island', pairs)  30.7 us
    ppermute x12, starting transfers between devices, along_y(): return lax.ppermute(array, 'fsdp', pairs)  15 us
    ppermute x24, waiting for transfers between devices, island_shift(): return lax.ppermute(array, 'island', pairs)  13 us
    pallas_call x4, Pallas kernels, group_sums(): pl.pallas_call(kernel, out_shape=shape(HALF, KV, dtype=dtype), grid=(HALF...  10.2 us
    unnamed x40, local copies, waits for them, and re-layouts  9.25 us
    pallas_call x2, Pallas kernels, adam(): pl.pallas_call(kernel, out_shape=[shape(HALF, KV, dtype=F32), shape(4, 64...  8.38 us
    ppermute x3, starting transfers between devices, swap_z(): return lax.ppermute(array, 'fsdp', pairs)  7.38 us
  transfers between devices with their start and end apart: 39, of which 15 were waited for; matrix products, arithmetic and copies ran while one was open for 0% of the time, Pallas kernels for 21%

profile of v2, /device:TPU:1, one launch (start us, length us, event | category | flops | bytes accessed | tf_op | source)
XLA Modules:
  0.0 169.0 jit_solution(6923731529501511102)
XLA Ops:
  0.7 5.7 %pack.1 = (bf16[256,1536]{1,0:T(8,128)(2,1)S(1)}, bf16[256,1536]{1,0:T(8,128)(2,1)S(1)}, bf16[256,1536]{1,0:T(8,128)(2,1)S(1)}, bf16[256,512]{1,0:T(8,128)(2,1)S...) custom-call(s32[2]{0:T(128)S(1)} %pad_add_fusion.place_ref, ...), custom_call_target="tpu_custom_call" | custom-call | bytes 1 | tf_op jit(solution)/shard_map/pack/pallas_call | solution.py:120
  6.4 4.5 %collective-permute-start = (bf16[1024,1024]{1,0:T(8,128)(2,1)S(1)}, bf16[1024,1024]{1,0:T(8,128)(2,1)S(1)}, u32[]{:S(2)}, u32[]{:S(2)}) collective-permute-start(bf16[1024,1024]{1,0:T(8,128)(2,1)S(1)} %get-tuple-element.43.w0), channel_id=1, source_target_pairs={{0,4},{1,5},{2,6},{3,7},{4,0},{5,1},{6,2},{7,3},{8,12},{9,13},{10,... | collective-permute-start | bytes 6291464 | tf_op jit(solution)/shard_map/ppermute | solution.py:38
  10.9 1.3 collective-permute-start.1
  12.2 2.6 %collective-permute-start.2 = (bf16[256,1536]{1,0:T(8,128)(2,1)S(1)}, bf16[256,1536]{1,0:T(8,128)(2,1)S(1)}, u32[]{:S(2)}, u32[]{:S(2)}) collective-permute-start(bf16[256,1536]{1,0:T(8,128)(2,1)S(1)} %get-tuple-element.45), channel_id=1, source_target_pairs={{0,2},{1,3},{2,0},{3,1},{4,6},{5,7},{6,4},{7,5},{8,10},{9,11},{10,... | collective-permute-start | bytes 2359304 | tf_op jit(solution)/shard_map/ppermute | solution.py:33
  15.9 14.4 %collective-permute-done.1.refs_1_.refs_5_.c1 = bf16[256,1536]{1,0:T(8,128)(2,1)S(1)} collective-permute-done((bf16[256,1536]{1,0:T(8,128)(2,1)S(1)}, bf16[256,1536]{1,0:T(8,128)(2,1)S(1)}, u32[]{:S(2)}, u32[]{:S(2)}) %collective-permute-start.1) | collective-permute-done | bytes 786464 | tf_op jit(solution)/shard_map/ppermute | solution.py:33
  30.4 18.0 %collective-permute-done.2.refs_1_.refs_6_.c2.refs_2_ = bf16[256,1536]{1,0:T(8,128)(2,1)S(1)} collective-permute-done((bf16[256,1536]{1,0:T(8,128)(2,1)S(1)}, bf16[256,1536]{1,0:T(8,128)(2,1)S(1)}, u32[]{:S(2)}, u32[]{:S(2)}) %collective-permute-start.2) | collective-permute-done | bytes 786464 | tf_op jit(solution)/shard_map/ppermute | solution.py:33
  48.3 2.5 %group_sums.6 = bf16[512,1024]{1,0:T(8,128)(2,1)} custom-call(bf16[256,2048]{1,0:T(8,128)(2,1)S(1)} %get-tuple-element.47.refs_0_, bf16[256,1536]{1,0:T(8,128)(2,1)S(1)} %collective-permute-done.1.refs_1_.refs_5_.c1, bf16[256,1536]{1,0:T(8,128)(2,1)S(1)} %collective-permute-done.2.refs_1_.refs_6_.c2.refs_2_, ...), custom_call_target="tpu_custom_call" | custom-call | bytes 1 | tf_op jit(solution)/shard_map/group_sums/pallas_call | solution.py:153
  51.3 1.2 collective-permute-start.4
  52.5 2.9 %collective-permute-start.5 = (bf16[256,512]{1,0:T(8,128)(2,1)S(1)}, bf16[256,512]{1,0:T(8,128)(2,1)S(1)}, u32[]{:S(2)}, u32[]{:S(2)}) collective-permute-start(bf16[256,512]{1,0:T(8,128)(2,1)S(1)} %gate.12), channel_id=1, source_target_pairs={{0,2},{1,3},{2,0},{3,1},{4,6},{5,7},{6,4},{7,5},{8,10},{9,11},{10,... | collective-permute-start | bytes 786440 | tf_op jit(solution)/shard_map/ppermute | solution.py:33
  55.4 3.7 %collective-permute-done.4.refs_1_ = bf16[256,512]{1,0:T(8,128)(2,1)S(1)} collective-permute-done((bf16[256,512]{1,0:T(8,128)(2,1)S(1)}, bf16[256,512]{1,0:T(8,128)(2,1)S(1)}, u32[]{:S(2)}, u32[]{:S(2)}) %collective-permute-start.4) | collective-permute-done | bytes 262176 | tf_op jit(solution)/shard_map/ppermute | solution.py:33
  59.1 7.7 %collective-permute-done.5.refs_2_.refs_1_ = bf16[256,512]{1,0:T(8,128)(2,1)S(1)} collective-permute-done((bf16[256,512]{1,0:T(8,128)(2,1)S(1)}, bf16[256,512]{1,0:T(8,128)(2,1)S(1)}, u32[]{:S(2)}, u32[]{:S(2)}) %collective-permute-start.5) | collective-permute-done | bytes 262176 | tf_op jit(solution)/shard_map/ppermute | solution.py:33
  67.5 4.0 %collective-permute-start.9 = (bf16[256,1024]{1,0:T(8,128)(2,1)}, bf16[256,1024]{1,0:T(8,128)(2,1)}, u32[]{:S(2)}, u32[]{:S(2)}) collective-permute-start(bf16[256,1024]{1,0:T(8,128)(2,1)} %gate.16), channel_id=1, source_target_pairs={{0,3},{1,0},{2,1},{3,2},{4,7},{5,4},{6,5},{7,6},{8,11},{9,8},{10,9... | collective-permute-start | bytes 1572872 | tf_op jit(solution)/shard_map/ppermute | solution.py:33
  71.5 2.5 %group_sums.4.refs_0_ = bf16[512,1024]{1,0:T(8,128)(2,1)} custom-call(bf16[256,2048]{1,0:T(8,128)(2,1)S(1)} %get-tuple-element.47.refs_0_, bf16[256,512]{1,0:T(8,128)(2,1)S(1)} %collective-permute-done.4.refs_1_, bf16[256,512]{1,0:T(8,128)(2,1)S(1)} %collective-permute-done.5.refs_2_.refs_1_, bf16[256,512]{1,0:T(8,128)(2,1)S(1)} %collective-permute-done.6.refs_3_.refs_1_, ...), custom_call_target="tpu_custom_call" | custom-call | bytes 1 | tf_op jit(solution)/shard_map/group_sums/pallas_call | solution.py:153
  74.0 2.5 %collective-permute-start.13 = (bf16[512,1024]{1,0:T(8,128)(2,1)}, bf16[512,1024]{1,0:T(8,128)(2,1)}, u32[]{:S(2)}, u32[]{:S(2)}) collective-permute-start(bf16[512,1024]{1,0:T(8,128)(2,1)} %group_sums.4.refs_0_), channel_id=1, source_target_pairs={{0,4},{1,5},{2,6},{3,7},{4,0},{5,1},{6,2},{7,3},{8,12},{9,13},{10,... | collective-permute-start | bytes 3145736 | tf_op jit(solution)/shard_map/ppermute | solution.py:38
  76.5 1.6 copy-done.7
  78.1 1.6 copy-done.13
  79.7 7.4 %input_blocks.1 = (bf16[256,2048]{1,0:T(8,128)(2,1)S(1)}, bf16[256,2048]{1,0:T(8,128)(2,1)}, bf16[256,2048]{1,0:T(8,128)(2,1)S(1)}, bf16[256,2048]{1,0:T(8,128)(2,1)}) custom-call(bf16[1024,1024]{1,0:T(8,128)(2,1)S(1)} %copy-done.13, bf16[1024,1024]{1,0:T(8,128)(2,1)S(1)} %copy-done.7, bf16[256,1024]{1,0:T(8,128)(2,1)S(1)} %bitcast.19, ...), custom_call_target="tpu_custom_call" | custom-call | bytes 1 | tf_op jit(solution)/shard_map/input_blocks/pallas_call | solution.py:260
  88.0 1.2 collective-permute-done.8.refs_2_
  89.2 2.5 %group_sums.5.g_ref = f32[512,1024]{1,0:T(8,128)S(1)} custom-call(bf16[256,2048]{1,0:T(8,128)(2,1)S(1)} %copy-done.2, bf16[256,1024]{1,0:T(8,128)(2,1)S(1)} %collective-permute-done.7.refs_1_, bf16[256,1024]{1,0:T(8,128)(2,1)} %collective-permute-done.8.refs_2_, bf16[256,1024]{1,0:T(8,128)(2,1)} %collective-permute-done.9.refs_3_, ...), custom_call_target="tpu_custom_call" | custom-call | bytes 1 | tf_op jit(solution)/shard_map/group_sums/pallas_call | solution.py:153
  91.8 4.6 %adam_step.2 = (f32[512,1024]{1,0:T(8,128)S(1)}, bf16[4,64,1024]{2,1,0:T(8,128)(2,1)S(1)}, bf16[4,64,1024]{2,1,0:T(8,128)(2,1)}) custom-call(s32[1]{0:T(128)} %bitcast.6.core_ref, f32[512,1024]{1,0:T(8,128)S(1)} %group_sums.5.g_ref, bf16[512,1024]{1,0:T(8,128)(2,1)} %collective-permute-done.12.got_ref, f32[1024,1024]{1,0:T(8,128)} %bitcast.31, ...), custom_call_target="tpu_custom_call" | custom-call | bytes 1 | tf_op jit(solution)/shard_map/adam_step/pallas_call | solution.py:214
  96.4 1.3 copy-done.4
  98.5 1.7 collective-permute-start.14
  100.2 1.8 %collective-permute-start.11 = (bf16[256,2048]{1,0:T(8,128)(2,1)}, bf16[256,2048]{1,0:T(8,128)(2,1)}, u32[]{:S(2)}, u32[]{:S(2)}) collective-permute-start(bf16[256,2048]{1,0:T(8,128)(2,1)} %gate.18), channel_id=1, source_target_pairs={{0,3},{1,0},{2,1},{3,2},{4,7},{5,4},{6,5},{7,6},{8,11},{9,8},{10,9... | collective-permute-start | bytes 3145736 | tf_op jit(solution)/shard_map/ppermute | solution.py:33
  103.1 1.8 %core_sums.2 = (bf16[64,1024]{1,0:T(8,128)(2,1)S(1)}, bf16[64,1024]{1,0:T(8,128)(2,1)S(1)}, bf16[64,1024]{1,0:T(8,128)(2,1)}, bf16[64,1024]{1,0:T(8,128)(2,1)}) custom-call(s32[2]{0:T(128)S(1)} %pad_add_fusion.1.x_ref.place_ref, bf16[4,64,1024]{2,1,0:T(8,128)(2,1)S(1)} %copy-done.17, bf16[4,64,1024]{2,1,0:T(8,128)(2,1)} %collective-permute-done.14.got_ref), custom_call_target="tpu_custom_call" | custom-call | bytes 1 | tf_op jit(solution)/shard_map/core_sums/pallas_call | solution.py:309
  104.9 1.2 collective-permute-start.15
  106.2 2.4 %collective-permute-start.16 = (bf16[64,1024]{1,0:T(8,128)(2,1)}, bf16[64,1024]{1,0:T(8,128)(2,1)}, u32[]{:S(2)}, u32[]{:S(2)}) collective-permute-start(bf16[64,1024]{1,0:T(8,128)(2,1)} %get-tuple-element.62), channel_id=1, source_target_pairs={{0,32},{8,40},{16,48},{24,56},{32,0},{40,8},{48,16},{56,24},{64,96... | collective-permute-start | bytes 393224 | tf_op jit(solution)/shard_map/ppermute | solution.py:51
  108.6 2.4 %collective-permute-done.15.p1 = bf16[64,1024]{1,0:T(8,128)(2,1)S(1)} collective-permute-done((bf16[64,1024]{1,0:T(8,128)(2,1)S(1)}, bf16[64,1024]{1,0:T(8,128)(2,1)S(1)}, u32[]{:S(2)}, u32[]{:S(2)}) %collective-permute-start.15) | collective-permute-done | bytes 131104 | tf_op jit(solution)/shard_map/ppermute | solution.py:51
  111.7 1.3 collective-permute-start.17
  112.9 1.2 copy-done.3
  114.2 2.6 %group_sums.7.g_ref = f32[512,1024]{1,0:T(8,128)S(1)} custom-call(bf16[256,2048]{1,0:T(8,128)(2,1)S(1)} %copy-done.3, bf16[256,1024]{1,0:T(8,128)(2,1)S(1)} %collective-permute-done.7.refs_1_, bf16[256,1024]{1,0:T(8,128)(2,1)} %collective-permute-done.8.refs_2_, bf16[256,1024]{1,0:T(8,128)(2,1)} %collective-permute-done.9.refs_3_, ...), custom_call_target="tpu_custom_call" | custom-call | bytes 1 | tf_op jit(solution)/shard_map/group_sums/pallas_call | solution.py:153
  117.9 3.8 %adam_step.3 = (f32[512,1024]{1,0:T(8,128)S(1)}, bf16[4,64,1024]{2,1,0:T(8,128)(2,1)S(1)}, bf16[4,64,1024]{2,1,0:T(8,128)(2,1)S(1)}) custom-call(s32[1]{0:T(128)} %bitcast.6.core_ref, f32[512,1024]{1,0:T(8,128)S(1)} %group_sums.7.g_ref, bf16[512,1024]{1,0:T(8,128)(2,1)} %collective-permute-done.13.got_ref, f32[1024,1024]{1,0:T(8,128)} %bitcast.32, ...), custom_call_target="tpu_custom_call" | custom-call | bytes 1 | tf_op jit(solution)/shard_map/adam_step/pallas_call | solution.py:214
  121.8 2.2 %collective-permute-start.18 = (bf16[4,64,1024]{2,1,0:T(8,128)(2,1)S(1)}, bf16[4,64,1024]{2,1,0:T(8,128)(2,1)S(1)}, u32[]{:S(2)}, u32[]{:S(2)}) collective-permute-start(bf16[4,64,1024]{2,1,0:T(8,128)(2,1)S(1)} %get-tuple-element.66), channel_id=1, source_target_pairs={{0,8},{8,0},{16,24},{24,16},{32,40},{40,32},{48,56},{56,48},{64,72... | collective-permute-start | bytes 1572872 | tf_op jit(solution)/shard_map/ppermute | solution.py:51
  124.0 1.5 collective-permute-done.18.got_ref
  126.2 1.8 %collective-permute-done.10.refs_1_ = bf16[256,2048]{1,0:T(8,128)(2,1)} collective-permute-done((bf16[256,2048]{1,0:T(8,128)(2,1)}, bf16[256,2048]{1,0:T(8,128)(2,1)}, u32[]{:S(2)}, u32[]{:S(2)}) %collective-permute-start.10) | collective-permute-done | bytes 1048608 | tf_op jit(solution)/shard_map/ppermute | solution.py:33
  130.0 2.5 %collective-permute-start.21 = (bf16[64,1024]{1,0:T(8,128)(2,1)S(1)}, bf16[64,1024]{1,0:T(8,128)(2,1)S(1)}, u32[]{:S(2)}, u32[]{:S(2)}) collective-permute-start(bf16[64,1024]{1,0:T(8,128)(2,1)S(1)} %get-tuple-element.69), channel_id=1, source_target_pairs={{0,32},{8,40},{16,48},{24,56},{32,0},{40,8},{48,16},{56,24},{64,96... | collective-permute-start | bytes 393224 | tf_op jit(solution)/shard_map/ppermute | solution.py:51
  134.1 1.3 collective-permute-start.37
  135.9 1.4 collective-permute-done.21.p2
  138.5 2.0 %collective-permute-done.37.refs_6_ = bf16[64,1024]{1,0:T(8,128)(2,1)S(1)} collective-permute-done((bf16[64,1024]{1,0:T(8,128)(2,1)S(1)}, bf16[64,1024]{1,0:T(8,128)(2,1)S(1)}, u32[]{:S(2)}, u32[]{:S(2)}) %collective-permute-start.37) | collective-permute-done | bytes 131104 | tf_op jit(solution)/shard_map/ppermute | solution.py:51
  140.5 3.5 %collective-permute-start.32 = (bf16[64,1024]{1,0:T(8,128)(2,1)S(1)}, bf16[64,1024]{1,0:T(8,128)(2,1)S(1)}, u32[]{:S(2)}, u32[]{:S(2)}) collective-permute-start(bf16[64,1024]{1,0:T(8,128)(2,1)S(1)} %gate.21.refs_0_), channel_id=1, source_target_pairs={{0,8},{8,0},{16,24},{24,16},{32,40},{40,32},{48,56},{56,48},{64,72... | collective-permute-start | bytes 393224 | tf_op jit(solution)/shard_map/ppermute | solution.py:51
  144.0 1.4 collective-permute-start.38
  145.4 1.3 collective-permute-start.36
  147.7 2.2 %collective-permute-start.30 = (bf16[64,1024]{1,0:T(8,128)(2,1)S(1)}, bf16[64,1024]{1,0:T(8,128)(2,1)S(1)}, u32[]{:S(2)}, u32[]{:S(2)}) collective-permute-start(bf16[64,1024]{1,0:T(8,128)(2,1)S(1)} %get-tuple-element.76.refs_0_), channel_id=1, source_target_pairs={{0,48},{8,56},{16,0},{24,8},{32,16},{40,24},{48,32},{56,40},{64,11... | collective-permute-start | bytes 393224 | tf_op jit(solution)/shard_map/ppermute | solution.py:51
  152.1 3.4 %collective-permute-done.30.refs_6_ = bf16[64,1024]{1,0:T(8,128)(2,1)S(1)} collective-permute-done((bf16[64,1024]{1,0:T(8,128)(2,1)S(1)}, bf16[64,1024]{1,0:T(8,128)(2,1)S(1)}, u32[]{:S(2)}, u32[]{:S(2)}) %collective-permute-start.30) | collective-permute-done | bytes 131104 | tf_op jit(solution)/shard_map/ppermute | solution.py:51
  156.5 1.6 collective-permute-start.29
  158.1 1.6 collective-permute-done.25.refs_4_.refs_2_
  160.2 2.5 %mix.2.refs_8_ = f32[1024,1024]{1,0:T(8,128)} custom-call(s32[2]{0:T(128)S(1)} %pad_add_fusion.1.x_ref.place_ref, f32[512,1024]{1,0:T(8,128)S(1)} %gate.20.upd, bf16[64,1024]{1,0:T(8,128)(2,1)S(1)} %gate.21.refs_0_, bf16[64,1024]{1,0:T(8,128)(2,1)S(1)} %collective-permute-done.32.refs_1_, bf16[64,1024]{1,0:T(8,128)(2,1)S(1)} %collective-permute-done.33.refs_2_, ...), custom_call_target="tpu_custom_call" | custom-call | bytes 1 | tf_op jit(solution)/shard_map/mix/pallas_call | solution.py:390
  162.7 2.5 %mix.3 = f32[1024,1024]{1,0:T(8,128)} custom-call(s32[2]{0:T(128)S(1)} %pad_add_fusion.1.x_ref.place_ref, f32[512,1024]{1,0:T(8,128)S(1)} %get-tuple-element.77.upd, bf16[64,1024]{1,0:T(8,128)(2,1)S(1)} %get-tuple-element.76.refs_0_, bf16[64,1024]{1,0:T(8,128)(2,1)S(1)} %collective-permute-done.26.refs_1_, ...), custom_call_target="tpu_custom_call", output_to_operand_aliasing={{}: (10, {})} | custom-call | bytes 1 | tf_op jit(solution)/shard_map/mix/pallas_call | solution.py:390
  165.2 3.6 %assemble.1 = bf16[256,8192]{1,0:T(8,128)(2,1)} custom-call(s32[2]{0:T(128)S(1)} %pad_add_fusion.place_ref, bf16[256,2048]{1,0:T(8,128)(2,1)S(1)} %copy-done.9, bf16[256,2048]{1,0:T(8,128)(2,1)} %collective-permute-done.10.refs_1_, bf16[256,2048]{1,0:T(8,128)(2,1)S(1)} %collective-permute-done.19.refs_2_, ...), custom_call_target="tpu_custom_call" | custom-call | bytes 1 | tf_op jit(solution)/shard_map/assemble/pallas_call | solution.py:291
  (100 shorter events, 17.6 us)
Async XLA Ops:
  0.7 47.6 %copy-start = (bf16[1,256,1024]{2,1,0:T(8,128)(2,1)S(1)}, bf16[1,256,1024]{2,1,0:T(8,128)(2,1)}, u32[]{:S(2)}) copy-start(bf16[1,256,1024]{2,1,0:T(8,128)(2,1)} %param.8) | copy-start | bytes 1572868
  6.4 44.9 %copy-start.12 = (bf16[1024,1024]{1,0:T(8,128)(2,1)}, bf16[1024,1024]{1,0:T(8,128)(2,1)S(1)}, u32[]{:S(2)}) copy-start(bf16[1024,1024]{1,0:T(8,128)(2,1)S(1)} %get-tuple-element.43.w0) | copy-start | bytes 6291460
  6.4 65.1 %copy-start.1 = (bf16[256,2048]{1,0:T(8,128)(2,1)}, bf16[256,2048]{1,0:T(8,128)(2,1)S(1)}, u32[]{:S(2)}) copy-start(bf16[256,2048]{1,0:T(8,128)(2,1)S(1)} %get-tuple-element.47.refs_0_) | copy-start | bytes 3145732
  6.4 65.0 %collective-permute-start = (bf16[1024,1024]{1,0:T(8,128)(2,1)S(1)}, bf16[1024,1024]{1,0:T(8,128)(2,1)S(1)}, u32[]{:S(2)}, u32[]{:S(2)}) collective-permute-start(bf16[1024,1024]{1,0:T(8,128)(2,1)S(1)} %get-tuple-element.43.w0), channel_id=1, source_target_pairs={{0,4},{1,5},{2,6},{3,7},{4,0},{5,1},{6,2},{7,3},{8,12},{9,13},{10,... | collective-permute-start | bytes 6291464 | tf_op jit(solution)/shard_map/ppermute | solution.py:38
  10.9 19.4 %collective-permute-start.1 = (bf16[256,1536]{1,0:T(8,128)(2,1)S(1)}, bf16[256,1536]{1,0:T(8,128)(2,1)S(1)}, u32[]{:S(2)}, u32[]{:S(2)}) collective-permute-start(bf16[256,1536]{1,0:T(8,128)(2,1)S(1)} %get-tuple-element.44), channel_id=1, source_target_pairs={{0,1},{1,2},{2,3},{3,0},{4,5},{5,6},{6,7},{7,4},{8,9},{9,10},{10,1... | collective-permute-start | bytes 2359304 | tf_op jit(solution)/shard_map/ppermute | solution.py:33
  12.2 36.1 %collective-permute-start.2 = (bf16[256,1536]{1,0:T(8,128)(2,1)S(1)}, bf16[256,1536]{1,0:T(8,128)(2,1)S(1)}, u32[]{:S(2)}, u32[]{:S(2)}) collective-permute-start(bf16[256,1536]{1,0:T(8,128)(2,1)S(1)} %get-tuple-element.45), channel_id=1, source_target_pairs={{0,2},{1,3},{2,0},{3,1},{4,6},{5,7},{6,4},{7,5},{8,10},{9,11},{10,... | collective-permute-start | bytes 2359304 | tf_op jit(solution)/shard_map/ppermute | solution.py:33
  14.9 33.5 %collective-permute-start.3 = (bf16[256,1536]{1,0:T(8,128)(2,1)S(1)}, bf16[256,1536]{1,0:T(8,128)(2,1)S(1)}, u32[]{:S(2)}, u32[]{:S(2)}) collective-permute-start(bf16[256,1536]{1,0:T(8,128)(2,1)S(1)} %get-tuple-element.46), channel_id=1, source_target_pairs={{0,3},{1,0},{2,1},{3,2},{4,7},{5,4},{6,5},{7,6},{8,11},{9,8},{10,9... | collective-permute-start | bytes 2359304 | tf_op jit(solution)/shard_map/ppermute | solution.py:33
  50.9 40.9 %collective-permute-start.12 = (bf16[512,1024]{1,0:T(8,128)(2,1)}, bf16[512,1024]{1,0:T(8,128)(2,1)}, u32[]{:S(2)}, u32[]{:S(2)}) collective-permute-start(bf16[512,1024]{1,0:T(8,128)(2,1)} %group_sums.6), channel_id=1, source_target_pairs={{0,4},{1,5},{2,6},{3,7},{4,0},{5,1},{6,2},{7,3},{8,12},{9,13},{10,... | collective-permute-start | bytes 3145736 | tf_op jit(solution)/shard_map/ppermute | solution.py:38
  51.3 7.8 %collective-permute-start.4 = (bf16[256,512]{1,0:T(8,128)(2,1)S(1)}, bf16[256,512]{1,0:T(8,128)(2,1)S(1)}, u32[]{:S(2)}, u32[]{:S(2)}) collective-permute-start(bf16[256,512]{1,0:T(8,128)(2,1)S(1)} %gate.11), channel_id=1, source_target_pairs={{0,1},{1,2},{2,3},{3,0},{4,5},{5,6},{6,7},{7,4},{8,9},{9,10},{10,1... | collective-permute-start | bytes 786440 | tf_op jit(solution)/shard_map/ppermute | solution.py:33
  52.5 14.2 %collective-permute-start.5 = (bf16[256,512]{1,0:T(8,128)(2,1)S(1)}, bf16[256,512]{1,0:T(8,128)(2,1)S(1)}, u32[]{:S(2)}, u32[]{:S(2)}) collective-permute-start(bf16[256,512]{1,0:T(8,128)(2,1)S(1)} %gate.12), channel_id=1, source_target_pairs={{0,2},{1,3},{2,0},{3,1},{4,6},{5,7},{6,4},{7,5},{8,10},{9,11},{10,... | collective-permute-start | bytes 786440 | tf_op jit(solution)/shard_map/ppermute | solution.py:33
  55.4 12.0 %collective-permute-start.6 = (bf16[256,512]{1,0:T(8,128)(2,1)S(1)}, bf16[256,512]{1,0:T(8,128)(2,1)S(1)}, u32[]{:S(2)}, u32[]{:S(2)}) collective-permute-start(bf16[256,512]{1,0:T(8,128)(2,1)S(1)} %gate.13), channel_id=1, source_target_pairs={{0,3},{1,0},{2,1},{3,2},{4,7},{5,4},{6,5},{7,6},{8,11},{9,8},{10,9... | collective-permute-start | bytes 786440 | tf_op jit(solution)/shard_map/ppermute | solution.py:33
  59.1 28.9 %collective-permute-start.7 = (bf16[256,1024]{1,0:T(8,128)(2,1)}, bf16[256,1024]{1,0:T(8,128)(2,1)S(1)}, u32[]{:S(2)}, u32[]{:S(2)}) collective-permute-start(bf16[256,1024]{1,0:T(8,128)(2,1)} %gate.14), channel_id=1, source_target_pairs={{0,1},{1,2},{2,3},{3,0},{4,5},{5,6},{6,7},{7,4},{8,9},{9,10},{10,1... | collective-permute-start | bytes 1572872 | tf_op jit(solution)/shard_map/ppermute | solution.py:33
  66.8 22.5 %collective-permute-start.8 = (bf16[256,1024]{1,0:T(8,128)(2,1)}, bf16[256,1024]{1,0:T(8,128)(2,1)}, u32[]{:S(2)}, u32[]{:S(2)}) collective-permute-start(bf16[256,1024]{1,0:T(8,128)(2,1)} %gate.15), channel_id=1, source_target_pairs={{0,2},{1,3},{2,0},{3,1},{4,6},{5,7},{6,4},{7,5},{8,10},{9,11},{10,... | collective-permute-start | bytes 1572872 | tf_op jit(solution)/shard_map/ppermute | solution.py:33
  67.5 21.8 %collective-permute-start.9 = (bf16[256,1024]{1,0:T(8,128)(2,1)}, bf16[256,1024]{1,0:T(8,128)(2,1)}, u32[]{:S(2)}, u32[]{:S(2)}) collective-permute-start(bf16[256,1024]{1,0:T(8,128)(2,1)} %gate.16), channel_id=1, source_target_pairs={{0,3},{1,0},{2,1},{3,2},{4,7},{5,4},{6,5},{7,6},{8,11},{9,8},{10,9... | collective-permute-start | bytes 1572872 | tf_op jit(solution)/shard_map/ppermute | solution.py:33
  74.0 43.9 %collective-permute-start.13 = (bf16[512,1024]{1,0:T(8,128)(2,1)}, bf16[512,1024]{1,0:T(8,128)(2,1)}, u32[]{:S(2)}, u32[]{:S(2)}) collective-permute-start(bf16[512,1024]{1,0:T(8,128)(2,1)} %group_sums.4.refs_0_), channel_id=1, source_target_pairs={{0,4},{1,5},{2,6},{3,7},{4,0},{5,1},{6,2},{7,3},{8,12},{9,13},{10,... | collective-permute-start | bytes 3145736 | tf_op jit(solution)/shard_map/ppermute | solution.py:38
  79.7 9.6 %copy-start.2 = (bf16[256,2048]{1,0:T(8,128)(2,1)S(1)}, bf16[256,2048]{1,0:T(8,128)(2,1)}, u32[]{:S(2)}) copy-start(bf16[256,2048]{1,0:T(8,128)(2,1)} %copy-done.1) | copy-start | bytes 3145732
  88.0 3.8 %copy-start.8 = (bf16[256,2048]{1,0:T(8,128)(2,1)}, bf16[256,2048]{1,0:T(8,128)(2,1)S(1)}, u32[]{:S(2)}) copy-start(bf16[256,2048]{1,0:T(8,128)(2,1)S(1)} %get-tuple-element.51.refs_8_.refs_0_) | copy-start | bytes 3145732
  98.5 3.6 %collective-permute-start.14 = (bf16[4,64,1024]{2,1,0:T(8,128)(2,1)}, bf16[4,64,1024]{2,1,0:T(8,128)(2,1)}, u32[]{:S(2)}, u32[]{:S(2)}) collective-permute-start(bf16[4,64,1024]{2,1,0:T(8,128)(2,1)} %get-tuple-element.58.refs_8_), channel_id=1, source_target_pairs={{0,8},{8,0},{16,24},{24,16},{32,40},{40,32},{48,56},{56,48},{64,72... | collective-permute-start | bytes 1572872 | tf_op jit(solution)/shard_map/ppermute | solution.py:51
  100.2 26.0 %collective-permute-start.11 = (bf16[256,2048]{1,0:T(8,128)(2,1)}, bf16[256,2048]{1,0:T(8,128)(2,1)}, u32[]{:S(2)}, u32[]{:S(2)}) collective-permute-start(bf16[256,2048]{1,0:T(8,128)(2,1)} %gate.18), channel_id=1, source_target_pairs={{0,3},{1,0},{2,1},{3,2},{4,7},{5,4},{6,5},{7,6},{8,11},{9,8},{10,9... | collective-permute-start | bytes 3145736 | tf_op jit(solution)/shard_map/ppermute | solution.py:33
  102.0 25.9 %collective-permute-start.10 = (bf16[256,2048]{1,0:T(8,128)(2,1)}, bf16[256,2048]{1,0:T(8,128)(2,1)}, u32[]{:S(2)}, u32[]{:S(2)}) collective-permute-start(bf16[256,2048]{1,0:T(8,128)(2,1)} %gate.17), channel_id=1, source_target_pairs={{0,1},{1,2},{2,3},{3,0},{4,5},{5,6},{6,7},{7,4},{8,9},{9,10},{10,1... | collective-permute-start | bytes 3145736 | tf_op jit(solution)/shard_map/ppermute | solution.py:33
  104.9 6.1 %collective-permute-start.15 = (bf16[64,1024]{1,0:T(8,128)(2,1)S(1)}, bf16[64,1024]{1,0:T(8,128)(2,1)S(1)}, u32[]{:S(2)}, u32[]{:S(2)}) collective-permute-start(bf16[64,1024]{1,0:T(8,128)(2,1)S(1)} %get-tuple-element.61), channel_id=1, source_target_pairs={{0,16},{8,24},{16,32},{24,40},{32,48},{40,56},{48,0},{56,8},{64,80... | collective-permute-start | bytes 393224 | tf_op jit(solution)/shard_map/ppermute | solution.py:51
  106.2 10.6 %collective-permute-start.16 = (bf16[64,1024]{1,0:T(8,128)(2,1)}, bf16[64,1024]{1,0:T(8,128)(2,1)}, u32[]{:S(2)}, u32[]{:S(2)}) collective-permute-start(bf16[64,1024]{1,0:T(8,128)(2,1)} %get-tuple-element.62), channel_id=1, source_target_pairs={{0,32},{8,40},{16,48},{24,56},{32,0},{40,8},{48,16},{56,24},{64,96... | collective-permute-start | bytes 393224 | tf_op jit(solution)/shard_map/ppermute | solution.py:51
  111.7 5.1 %collective-permute-start.17 = (bf16[64,1024]{1,0:T(8,128)(2,1)}, bf16[64,1024]{1,0:T(8,128)(2,1)}, u32[]{:S(2)}, u32[]{:S(2)}) collective-permute-start(bf16[64,1024]{1,0:T(8,128)(2,1)} %get-tuple-element.63), channel_id=1, source_target_pairs={{0,48},{8,56},{16,0},{24,8},{32,16},{40,24},{48,32},{56,40},{64,11... | collective-permute-start | bytes 393224 | tf_op jit(solution)/shard_map/ppermute | solution.py:51
  114.2 2.6 %copy-start.11 = (f32[1,64,1024]{2,1,0:T(8,128)S(1)}, f32[1,64,1024]{2,1,0:T(8,128)}, u32[]{:S(2)}) copy-start(f32[1,64,1024]{2,1,0:T(8,128)} %param.13) | copy-start | bytes 786436
  114.2 2.6 %copy-start.19 = (bf16[64,1024]{1,0:T(8,128)(2,1)S(1)}, bf16[64,1024]{1,0:T(8,128)(2,1)}, u32[]{:S(2)}) copy-start(bf16[64,1024]{1,0:T(8,128)(2,1)} %copy-done.18) | copy-start | bytes 393220
  117.9 10.0 %copy-start.15 = (bf16[256,2048]{1,0:T(8,128)(2,1)S(1)}, bf16[256,2048]{1,0:T(8,128)(2,1)}, u32[]{:S(2)}) copy-start(bf16[256,2048]{1,0:T(8,128)(2,1)} %copy-done.14) | copy-start | bytes 3145732
  121.8 3.7 %collective-permute-start.18 = (bf16[4,64,1024]{2,1,0:T(8,128)(2,1)S(1)}, bf16[4,64,1024]{2,1,0:T(8,128)(2,1)S(1)}, u32[]{:S(2)}, u32[]{:S(2)}) collective-permute-start(bf16[4,64,1024]{2,1,0:T(8,128)(2,1)S(1)} %get-tuple-element.66), channel_id=1, source_target_pairs={{0,8},{8,0},{16,24},{24,16},{32,40},{40,32},{48,56},{56,48},{64,72... | collective-permute-start | bytes 1572872 | tf_op jit(solution)/shard_map/ppermute | solution.py:51
  126.2 34.0 %copy-start.5 = (f32[512,1024]{1,0:T(8,128)S(1)}, f32[512,1024]{1,0:T(8,128)}, u32[]{:S(2)}) copy-start(f32[512,1024]{1,0:T(8,128)} %copy-done.4) | copy-start | bytes 6291460
  128.0 37.3 %collective-permute-start.19 = (bf16[256,2048]{1,0:T(8,128)(2,1)S(1)}, bf16[256,2048]{1,0:T(8,128)(2,1)S(1)}, u32[]{:S(2)}, u32[]{:S(2)}) collective-permute-start(bf16[256,2048]{1,0:T(8,128)(2,1)S(1)} %gate.19), channel_id=1, source_target_pairs={{0,2},{1,3},{2,0},{3,1},{4,6},{5,7},{6,4},{7,5},{8,10},{9,11},{10,... | collective-permute-start | bytes 3145736 | tf_op jit(solution)/shard_map/ppermute | solution.py:33
  128.0 5.7 %collective-permute-start.24 = (bf16[64,1024]{1,0:T(8,128)(2,1)S(1)}, bf16[64,1024]{1,0:T(8,128)(2,1)S(1)}, u32[]{:S(2)}, u32[]{:S(2)}) collective-permute-start(bf16[64,1024]{1,0:T(8,128)(2,1)S(1)} %get-tuple-element.64.refs_0_), channel_id=1, source_target_pairs={{0,64},{8,72},{16,80},{24,88},{32,96},{40,104},{48,112},{56,120},{... | collective-permute-start | bytes 393224 | tf_op jit(solution)/shard_map/ppermute | solution.py:51
  128.8 5.3 %collective-permute-start.20 = (bf16[64,1024]{1,0:T(8,128)(2,1)S(1)}, bf16[64,1024]{1,0:T(8,128)(2,1)S(1)}, u32[]{:S(2)}, u32[]{:S(2)}) collective-permute-start(bf16[64,1024]{1,0:T(8,128)(2,1)S(1)} %get-tuple-element.68), channel_id=1, source_target_pairs={{0,16},{8,24},{16,32},{24,40},{32,48},{40,56},{48,0},{56,8},{64,80... | collective-permute-start | bytes 393224 | tf_op jit(solution)/shard_map/ppermute | solution.py:51
  130.0 7.3 %collective-permute-start.21 = (bf16[64,1024]{1,0:T(8,128)(2,1)S(1)}, bf16[64,1024]{1,0:T(8,128)(2,1)S(1)}, u32[]{:S(2)}, u32[]{:S(2)}) collective-permute-start(bf16[64,1024]{1,0:T(8,128)(2,1)S(1)} %get-tuple-element.69), channel_id=1, source_target_pairs={{0,32},{8,40},{16,48},{24,56},{32,0},{40,8},{48,16},{56,24},{64,96... | collective-permute-start | bytes 393224 | tf_op jit(solution)/shard_map/ppermute | solution.py:51
  132.5 5.2 %collective-permute-start.22 = (bf16[64,1024]{1,0:T(8,128)(2,1)S(1)}, bf16[64,1024]{1,0:T(8,128)(2,1)S(1)}, u32[]{:S(2)}, u32[]{:S(2)}) collective-permute-start(bf16[64,1024]{1,0:T(8,128)(2,1)S(1)} %get-tuple-element.70), channel_id=1, source_target_pairs={{0,48},{8,56},{16,0},{24,8},{32,16},{40,24},{48,32},{56,40},{64,11... | collective-permute-start | bytes 393224 | tf_op jit(solution)/shard_map/ppermute | solution.py:51
  134.1 6.4 %collective-permute-start.37 = (bf16[64,1024]{1,0:T(8,128)(2,1)S(1)}, bf16[64,1024]{1,0:T(8,128)(2,1)S(1)}, u32[]{:S(2)}, u32[]{:S(2)}) collective-permute-start(bf16[64,1024]{1,0:T(8,128)(2,1)S(1)} %gate.21.refs_0_), channel_id=1, source_target_pairs={{0,48},{8,56},{16,0},{24,8},{32,16},{40,24},{48,32},{56,40},{64,11... | collective-permute-start | bytes 393224 | tf_op jit(solution)/shard_map/ppermute | solution.py:51
  135.4 8.6 %collective-permute-start.35 = (bf16[64,1024]{1,0:T(8,128)(2,1)S(1)}, bf16[64,1024]{1,0:T(8,128)(2,1)S(1)}, u32[]{:S(2)}, u32[]{:S(2)}) collective-permute-start(bf16[64,1024]{1,0:T(8,128)(2,1)S(1)} %gate.21.refs_0_), channel_id=1, source_target_pairs={{0,32},{8,40},{16,48},{24,56},{32,0},{40,8},{48,16},{56,24},{64,96... | collective-permute-start | bytes 393224 | tf_op jit(solution)/shard_map/ppermute | solution.py:51
  137.4 8.1 %collective-permute-start.33 = (bf16[64,1024]{1,0:T(8,128)(2,1)S(1)}, bf16[64,1024]{1,0:T(8,128)(2,1)S(1)}, u32[]{:S(2)}, u32[]{:S(2)}) collective-permute-start(bf16[64,1024]{1,0:T(8,128)(2,1)S(1)} %gate.21.refs_0_), channel_id=1, source_target_pairs={{0,16},{8,24},{16,32},{24,40},{32,48},{40,56},{48,0},{56,8},{64,80... | collective-permute-start | bytes 393224 | tf_op jit(solution)/shard_map/ppermute | solution.py:51
  137.8 9.0 %collective-permute-start.23 = (bf16[64,1024]{1,0:T(8,128)(2,1)S(1)}, bf16[64,1024]{1,0:T(8,128)(2,1)S(1)}, u32[]{:S(2)}, u32[]{:S(2)}) collective-permute-start(bf16[64,1024]{1,0:T(8,128)(2,1)S(1)} %get-tuple-element.72.refs_1_), channel_id=1, source_target_pairs={{0,64},{8,72},{16,80},{24,88},{32,96},{40,104},{48,112},{56,120},{... | collective-permute-start | bytes 393224 | tf_op jit(solution)/shard_map/ppermute | solution.py:51
  140.5 7.2 %collective-permute-start.32 = (bf16[64,1024]{1,0:T(8,128)(2,1)S(1)}, bf16[64,1024]{1,0:T(8,128)(2,1)S(1)}, u32[]{:S(2)}, u32[]{:S(2)}) collective-permute-start(bf16[64,1024]{1,0:T(8,128)(2,1)S(1)} %gate.21.refs_0_), channel_id=1, source_target_pairs={{0,8},{8,0},{16,24},{24,16},{32,40},{40,32},{48,56},{56,48},{64,72... | collective-permute-start | bytes 393224 | tf_op jit(solution)/shard_map/ppermute | solution.py:51
  144.0 5.9 %collective-permute-start.38 = (bf16[64,1024]{1,0:T(8,128)(2,1)S(1)}, bf16[64,1024]{1,0:T(8,128)(2,1)S(1)}, u32[]{:S(2)}, u32[]{:S(2)}) collective-permute-start(bf16[64,1024]{1,0:T(8,128)(2,1)S(1)} %collective-permute-done.37.refs_6_), channel_id=1, source_target_pairs={{0,8},{8,0},{16,24},{24,16},{32,40},{40,32},{48,56},{56,48},{64,72... | collective-permute-start | bytes 393224 | tf_op jit(solution)/shard_map/ppermute | solution.py:51
  145.4 5.0 %collective-permute-start.36 = (bf16[64,1024]{1,0:T(8,128)(2,1)S(1)}, bf16[64,1024]{1,0:T(8,128)(2,1)S(1)}, u32[]{:S(2)}, u32[]{:S(2)}) collective-permute-start(bf16[64,1024]{1,0:T(8,128)(2,1)S(1)} %collective-permute-done.35.refs_4_), channel_id=1, source_target_pairs={{0,8},{8,0},{16,24},{24,16},{32,40},{40,32},{48,56},{56,48},{64,72... | collective-permute-start | bytes 393224 | tf_op jit(solution)/shard_map/ppermute | solution.py:51
  146.8 4.5 %collective-permute-start.34 = (bf16[64,1024]{1,0:T(8,128)(2,1)S(1)}, bf16[64,1024]{1,0:T(8,128)(2,1)S(1)}, u32[]{:S(2)}, u32[]{:S(2)}) collective-permute-start(bf16[64,1024]{1,0:T(8,128)(2,1)S(1)} %collective-permute-done.33.refs_2_), channel_id=1, source_target_pairs={{0,8},{8,0},{16,24},{24,16},{32,40},{40,32},{48,56},{56,48},{64,72... | collective-permute-start | bytes 393224 | tf_op jit(solution)/shard_map/ppermute | solution.py:51
  147.7 7.8 %collective-permute-start.30 = (bf16[64,1024]{1,0:T(8,128)(2,1)S(1)}, bf16[64,1024]{1,0:T(8,128)(2,1)S(1)}, u32[]{:S(2)}, u32[]{:S(2)}) collective-permute-start(bf16[64,1024]{1,0:T(8,128)(2,1)S(1)} %get-tuple-element.76.refs_0_), channel_id=1, source_target_pairs={{0,48},{8,56},{16,0},{24,8},{32,16},{40,24},{48,32},{56,40},{64,11... | collective-permute-start | bytes 393224 | tf_op jit(solution)/shard_map/ppermute | solution.py:51
  149.9 6.6 %collective-permute-start.28 = (bf16[64,1024]{1,0:T(8,128)(2,1)S(1)}, bf16[64,1024]{1,0:T(8,128)(2,1)S(1)}, u32[]{:S(2)}, u32[]{:S(2)}) collective-permute-start(bf16[64,1024]{1,0:T(8,128)(2,1)S(1)} %get-tuple-element.76.refs_0_), channel_id=1, source_target_pairs={{0,32},{8,40},{16,48},{24,56},{32,0},{40,8},{48,16},{56,24},{64,96... | collective-permute-start | bytes 393224 | tf_op jit(solution)/shard_map/ppermute | solution.py:51
  150.5 9.2 %collective-permute-start.25 = (bf16[64,1024]{1,0:T(8,128)(2,1)S(1)}, bf16[64,1024]{1,0:T(8,128)(2,1)S(1)}, u32[]{:S(2)}, u32[]{:S(2)}) collective-permute-start(bf16[64,1024]{1,0:T(8,128)(2,1)S(1)} %get-tuple-element.76.refs_0_), channel_id=1, source_target_pairs={{0,16},{8,24},{16,32},{24,40},{32,48},{40,56},{48,0},{56,8},{64,80... | collective-permute-start | bytes 393224 | tf_op jit(solution)/shard_map/ppermute | solution.py:51
  151.3 11.4 %collective-permute-start.26 = (bf16[64,1024]{1,0:T(8,128)(2,1)S(1)}, bf16[64,1024]{1,0:T(8,128)(2,1)S(1)}, u32[]{:S(2)}, u32[]{:S(2)}) collective-permute-start(bf16[64,1024]{1,0:T(8,128)(2,1)S(1)} %get-tuple-element.76.refs_0_), channel_id=1, source_target_pairs={{0,8},{8,0},{16,24},{24,16},{32,40},{40,32},{48,56},{56,48},{64,72... | collective-permute-start | bytes 393224 | tf_op jit(solution)/shard_map/ppermute | solution.py:51
  155.5 7.2 %collective-permute-start.31 = (bf16[64,1024]{1,0:T(8,128)(2,1)S(1)}, bf16[64,1024]{1,0:T(8,128)(2,1)S(1)}, u32[]{:S(2)}, u32[]{:S(2)}) collective-permute-start(bf16[64,1024]{1,0:T(8,128)(2,1)S(1)} %collective-permute-done.30.refs_6_), channel_id=1, source_target_pairs={{0,8},{8,0},{16,24},{24,16},{32,40},{40,32},{48,56},{56,48},{64,72... | collective-permute-start | bytes 393224 | tf_op jit(solution)/shard_map/ppermute | solution.py:51
  156.5 6.2 %collective-permute-start.29 = (bf16[64,1024]{1,0:T(8,128)(2,1)S(1)}, bf16[64,1024]{1,0:T(8,128)(2,1)S(1)}, u32[]{:S(2)}, u32[]{:S(2)}) collective-permute-start(bf16[64,1024]{1,0:T(8,128)(2,1)S(1)} %collective-permute-done.28.refs_4_), channel_id=1, source_target_pairs={{0,8},{8,0},{16,24},{24,16},{32,40},{40,32},{48,56},{56,48},{64,72... | collective-permute-start | bytes 393224 | tf_op jit(solution)/shard_map/ppermute | solution.py:51
  159.7 3.0 %collective-permute-start.27 = (bf16[64,1024]{1,0:T(8,128)(2,1)S(1)}, bf16[64,1024]{1,0:T(8,128)(2,1)S(1)}, u32[]{:S(2)}, u32[]{:S(2)}) collective-permute-start(bf16[64,1024]{1,0:T(8,128)(2,1)S(1)} %collective-permute-done.25.refs_4_.refs_2_), channel_id=1, source_target_pairs={{0,8},{8,0},{16,24},{24,16},{32,40},{40,32},{48,56},{56,48},{64,72... | collective-permute-start | bytes 393224 | tf_op jit(solution)/shard_map/ppermute | solution.py:51
  (11 other events, 16.9 us)

commit v3 on v2

--- a/solution.py
+++ b/solution.py
@@ -259,7 +259,7 @@
     whole = pl.BlockSpec((TOK, KV), lambda j: (0, 0))
     return pl.pallas_call(
         kernel,
-        out_shape=[shape(TOK, 2 * ROWS)] * 4,
+        out_shape=[pltpu.HBM((TOK, 2 * ROWS), BF)] * 4,
         grid=(2 * count,),
         in_specs=[tile(0), tile(count)] + [whole] * 4 + [ANY] * len(earlier),
         out_specs=[pl.BlockSpec((TOK, TILE), lambda j: (0, j))] * 4,
@@ -427,25 +427,25 @@
         BF, [(own, HALF)] + [(a, 0) for a in second], cots, [weight_got]
     )
     got_1 = swap_z(partial_1)
-    blocks = input_blocks(weight, weight_got, cots, [partial_1])
-    near = [along_y(gate(blocks[4 - k], *third), k) for k in (1, 3)]
+    blocks = [in_hbm(b) for b in input_blocks(weight, weight_got, cots, [partial_1])]
+    far = along_y(gate(blocks[2], *third), 2)
 
     mine = [(own, ROWS)] + [(a, 0) for a in third]
+    mine = [(in_hbm(a), c) for a, c in mine]
+    cots = [in_hbm(c) for c in cots]
     grad_0 = group_sums(F32, mine, cots, [blocks[0]])
-    updated_0, keep_0, send_0 = adam(
-        0, core, grad_0, got_0, master, *moments, []
-    )
-    grad_1 = group_sums(F32, [(a, c + HALF) for a, c in mine], cots, [send_0])
+    updated_0, keep_0, send_0 = adam(0, core, grad_0, got_0, master, *moments, [])
 
     def over_x(keep, send):
         sums = core_sums(x_core, keep, island_shift(send, 0, 0, 1))
         return [sums[0]] + [island_shift(sums[k], 0, k, 0) for k in (1, 2, 3)]
 
-    def spread(fresh):
-        lines = [fresh] + [island_shift(fresh, 0, k, 0) for k in (1, 2, 3)]
+    def with_other_core(lines):
         return [part for line in lines for part in (line, island_shift(line, 0, 0, 1))]
 
-    wide_0, rounded_0 = x_sums(0, zl, over_x(keep_0, send_0), anchor, momentum)
+    sums_0 = over_x(keep_0, send_0)
+    grad_1 = group_sums(F32, [(a, c + HALF) for a, c in mine], cots)
+    wide_0, rounded_0 = x_sums(0, zl, sums_0, anchor, momentum)
     updated_1, keep_1, send_1 = adam(
         1, core, grad_1, got_1, master, *moments, [rounded_0]
     )
@@ -454,15 +454,17 @@
     )
     sums_1 = over_x(keep_1, send_1)
     wide_1, rounded_1 = x_sums(1, zl, sums_1, anchor, momentum)
-    far = along_y(gate(blocks[2], *near, sums_1[0]), 2)
-    lines_0 = spread(gate(fresh_0, sums_1[1]))
+    near = [along_y(gate(blocks[4 - k], far, rounded_0), k) for k in (1, 3)]
+    fresh_0 = gate(fresh_0, sums_1[1])
+    lines_0 = with_other_core([fresh_0] + [island_shift(fresh_0, 0, k, 0) for k in (1, 2, 3)])
     *former, fresh_1 = outer_step(
         1, zl, wide_1, island_shift(rounded_1, 1, 0, 0), anchor, momentum, former
     )
-    lines_1 = spread(fresh_1)
+    lines_1 = [island_shift(fresh_1, 0, k, 0) for k in (1, 2, 3)]
     mixed = mix(0, x_core, gate(updated_0, rounded_1), lines_0, None)
-    mixed = mix(1, x_core, updated_1, lines_1, mixed)
-    input_grad = assemble(f_place, [blocks[0], near[0], far, near[1]], [lines_1[2]])
+    input_grad = assemble(f_place, [blocks[0], near[0], far, near[1]], [fresh_1])
+    lines_1[1] = gate(lines_1[1], in_hbm(input_grad))
+    mixed = mix(1, x_core, updated_1, with_other_core([fresh_1] + lines_1), mixed)
     new_outer, new_momentum = former
     return (input_grad[None], mixed[None], new_outer[None], new_momentum[None])
 

time: 169 us -> 160 us (0.947)
  local copies, waits for them, and re-layouts: 9.25 us -> 3.45 us
  starting transfers between devices: 53 us -> 50.2 us
    unnamed x40 -> x24, local copies, waits for them, and re-layouts: 9.25 us -> 3.45 us
    ppermute x24, starting transfers between devices: 30.7 us -> 27.8 us  [island_shift(): return lax.ppermute(array, 'island', pairs)]
    ppermute x12, starting transfers between devices: 15 us -> 17.9 us  [along_y(): return lax.ppermute(array, 'fsdp', pairs)]
    ppermute x3, starting transfers between devices: 7.38 us -> 4.51 us  [swap_z(): return lax.ppermute(array, 'fsdp', pairs)]
  transfers between devices with their start and end apart: 39 -> 39, of which waited for: 15 -> 16; matrix products, arithmetic and copies ran while one was open for 0% -> 0% of each run, Pallas kernels for 21% -> 24%
where the time goes in v3:
time: 160 us
  waiting for transfers between devices  59.8 us (37%)
  starting transfers between devices  50.2 us (31%)
  Pallas kernels  45.3 us (28%)
  local copies, waits for them, and re-layouts  3.45 us (2%)
    ppermute x12, waiting for transfers between devices, along_y(): return lax.ppermute(array, 'fsdp', pairs)  45.8 us
    ppermute x24, starting transfers between devices, island_shift(): return lax.ppermute(array, 'island', pairs)  27.8 us
    ppermute x12, starting transfers between devices, along_y(): return lax.ppermute(array, 'fsdp', pairs)  17.9 us
    ppermute x24, waiting for transfers between devices, island_shift(): return lax.ppermute(array, 'island', pairs)  14 us
    pallas_call x4, Pallas kernels, group_sums(): pl.pallas_call(kernel, out_shape=shape(HALF, KV, dtype=dtype), grid=(HALF...  11.8 us
    pallas_call x2, Pallas kernels, adam(): pl.pallas_call(kernel, out_shape=[shape(HALF, KV, dtype=F32), shape(4, 64...  8.33 us
    pallas_call x1, Pallas kernels, input_blocks(): pl.pallas_call(kernel, out_shape=[pltpu.HBM((TOK, 2 * ROWS), BF)] * 4, gr...  7.38 us
    pallas_call x2, Pallas kernels, mix(): pl.pallas_call(kernel, out_shape=shape(ROWS, KV, dtype=F32), grid_spec=pl...  5.03 us
  transfers between devices with their start and end apart: 39, of which 16 were waited for; matrix products, arithmetic and copies ran while one was open for 0% of the time, Pallas kernels for 24%

profile of v3, /device:TPU:1, one launch (start us, length us, event | category | flops | bytes accessed | tf_op | source)
XLA Modules:
  0.0 159.7 jit_solution(14810095124030823103)
XLA Ops:
  0.7 4.5 %pack.1 = (bf16[256,1536]{1,0:T(8,128)(2,1)S(1)}, bf16[256,1536]{1,0:T(8,128)(2,1)S(1)}, bf16[256,1536]{1,0:T(8,128)(2,1)S(1)}, bf16[256,512]{1,0:T(8,128)(2,1)S...) custom-call(s32[2]{0:T(128)S(1)} %pad_add_fusion.place_ref, ...), custom_call_target="tpu_custom_call" | custom-call | bytes 1 | tf_op jit(solution)/shard_map/pack/pallas_call | solution.py:120
  5.3 4.5 %collective-permute-start = (bf16[1024,1024]{1,0:T(8,128)(2,1)S(1)}, bf16[1024,1024]{1,0:T(8,128)(2,1)S(1)}, u32[]{:S(2)}, u32[]{:S(2)}) collective-permute-start(bf16[1024,1024]{1,0:T(8,128)(2,1)S(1)} %get-tuple-element.43.w0), channel_id=1, source_target_pairs={{0,4},{1,5},{2,6},{3,7},{4,0},{5,1},{6,2},{7,3},{8,12},{9,13},{10,... | collective-permute-start | bytes 6291464 | tf_op jit(solution)/shard_map/ppermute | solution.py:38
  9.8 1.3 collective-permute-start.1
  11.1 2.6 %collective-permute-start.2 = (bf16[256,1536]{1,0:T(8,128)(2,1)S(1)}, bf16[256,1536]{1,0:T(8,128)(2,1)S(1)}, u32[]{:S(2)}, u32[]{:S(2)}) collective-permute-start(bf16[256,1536]{1,0:T(8,128)(2,1)S(1)} %get-tuple-element.45), channel_id=1, source_target_pairs={{0,2},{1,3},{2,0},{3,1},{4,6},{5,7},{6,4},{7,5},{8,10},{9,11},{10,... | collective-permute-start | bytes 2359304 | tf_op jit(solution)/shard_map/ppermute | solution.py:33
  13.7 1.1 collective-permute-start.3
  14.8 14.4 %collective-permute-done.1.refs_1_.refs_5_.c1 = bf16[256,1536]{1,0:T(8,128)(2,1)S(1)} collective-permute-done((bf16[256,1536]{1,0:T(8,128)(2,1)S(1)}, bf16[256,1536]{1,0:T(8,128)(2,1)S(1)}, u32[]{:S(2)}, u32[]{:S(2)}) %collective-permute-start.1) | collective-permute-done | bytes 786464 | tf_op jit(solution)/shard_map/ppermute | solution.py:33
  29.2 18.0 %collective-permute-done.2.refs_1_.refs_6_.c2.refs_2_ = bf16[256,1536]{1,0:T(8,128)(2,1)S(1)} collective-permute-done((bf16[256,1536]{1,0:T(8,128)(2,1)S(1)}, bf16[256,1536]{1,0:T(8,128)(2,1)S(1)}, u32[]{:S(2)}, u32[]{:S(2)}) %collective-permute-start.2) | collective-permute-done | bytes 786464 | tf_op jit(solution)/shard_map/ppermute | solution.py:33
  48.0 3.9 %collective-permute-start.6 = (bf16[256,512]{1,0:T(8,128)(2,1)S(1)}, bf16[256,512]{1,0:T(8,128)(2,1)S(1)}, u32[]{:S(2)}, u32[]{:S(2)}) collective-permute-start(bf16[256,512]{1,0:T(8,128)(2,1)S(1)} %gate.14), channel_id=1, source_target_pairs={{0,3},{1,0},{2,1},{3,2},{4,7},{5,4},{6,5},{7,6},{8,11},{9,8},{10,9... | collective-permute-start | bytes 786440 | tf_op jit(solution)/shard_map/ppermute | solution.py:33
  51.9 2.5 %group_sums.6 = bf16[512,1024]{1,0:T(8,128)(2,1)} custom-call(bf16[256,2048]{1,0:T(8,128)(2,1)S(1)} %get-tuple-element.47.refs_0_, bf16[256,1536]{1,0:T(8,128)(2,1)S(1)} %collective-permute-done.1.refs_1_.refs_5_.c1, bf16[256,1536]{1,0:T(8,128)(2,1)S(1)} %collective-permute-done.2.refs_1_.refs_6_.c2.refs_2_, ...), custom_call_target="tpu_custom_call" | custom-call | bytes 1 | tf_op jit(solution)/shard_map/group_sums/pallas_call | solution.py:153
  55.3 3.2 %collective-permute-done.5.refs_2_.refs_1_ = bf16[256,512]{1,0:T(8,128)(2,1)S(1)} collective-permute-done((bf16[256,512]{1,0:T(8,128)(2,1)S(1)}, bf16[256,512]{1,0:T(8,128)(2,1)S(1)}, u32[]{:S(2)}, u32[]{:S(2)}) %collective-permute-start.5) | collective-permute-done | bytes 262176 | tf_op jit(solution)/shard_map/ppermute | solution.py:33
  58.9 3.1 %collective-permute-start.9 = (bf16[256,1024]{1,0:T(8,128)(2,1)S(1)}, bf16[256,1024]{1,0:T(8,128)(2,1)S(1)}, u32[]{:S(2)}, u32[]{:S(2)}) collective-permute-start(bf16[256,1024]{1,0:T(8,128)(2,1)S(1)} %gate.17), channel_id=1, source_target_pairs={{0,3},{1,0},{2,1},{3,2},{4,7},{5,4},{6,5},{7,6},{8,11},{9,8},{10,9... | collective-permute-start | bytes 1572872 | tf_op jit(solution)/shard_map/ppermute | solution.py:33
  62.0 2.5 %group_sums.4.refs_0_ = bf16[512,1024]{1,0:T(8,128)(2,1)} custom-call(bf16[256,2048]{1,0:T(8,128)(2,1)S(1)} %get-tuple-element.47.refs_0_, bf16[256,512]{1,0:T(8,128)(2,1)S(1)} %collective-permute-done.4.refs_1_, bf16[256,512]{1,0:T(8,128)(2,1)S(1)} %collective-permute-done.5.refs_2_.refs_1_, bf16[256,512]{1,0:T(8,128)(2,1)S(1)} %collective-permute-done.6.refs_3_.refs_1_, ...), custom_call_target="tpu_custom_call" | custom-call | bytes 1 | tf_op jit(solution)/shard_map/group_sums/pallas_call | solution.py:153
  64.6 7.4 %input_blocks.1 = (bf16[256,2048]{1,0:T(8,128)(2,1)}, bf16[256,2048]{1,0:T(8,128)(2,1)}, bf16[256,2048]{1,0:T(8,128)(2,1)}, bf16[256,2048]{1,0:T(8,128)(2,1)}) custom-call(bf16[1024,1024]{1,0:T(8,128)(2,1)S(1)} %get-tuple-element.43.w0, bf16[1024,1024]{1,0:T(8,128)(2,1)S(1)} %collective-permute-done.refs_8_.w1, bf16[256,1024]{1,0:T(8,128)(2,1)S(1)} %bitcast.21, ...), custom_call_target="tpu_custom_call" | custom-call | bytes 1 | tf_op jit(solution)/shard_map/input_blocks/pallas_call | solution.py:260
  72.5 8.3 %collective-permute-done.8.refs_2_ = bf16[256,1024]{1,0:T(8,128)(2,1)S(1)} collective-permute-done((bf16[256,1024]{1,0:T(8,128)(2,1)S(1)}, bf16[256,1024]{1,0:T(8,128)(2,1)S(1)}, u32[]{:S(2)}, u32[]{:S(2)}) %collective-permute-start.8) | collective-permute-done | bytes 524320 | tf_op jit(solution)/shard_map/ppermute | solution.py:33
  82.4 2.4 %collective-permute-start.10 = (bf16[256,2048]{1,0:T(8,128)(2,1)}, bf16[256,2048]{1,0:T(8,128)(2,1)S(1)}, u32[]{:S(2)}, u32[]{:S(2)}) collective-permute-start(bf16[256,2048]{1,0:T(8,128)(2,1)} %gate.18), channel_id=1, source_target_pairs={{0,2},{1,3},{2,0},{3,1},{4,6},{5,7},{6,4},{7,5},{8,10},{9,11},{10,... | collective-permute-start | bytes 3145736 | tf_op jit(solution)/shard_map/ppermute | solution.py:33
  84.8 3.4 %group_sums.5.g_ref = f32[512,1024]{1,0:T(8,128)S(1)} custom-call(bf16[256,2048]{1,0:T(8,128)(2,1)} %copy-done.4, bf16[256,1024]{1,0:T(8,128)(2,1)} %copy-done.5, bf16[256,1024]{1,0:T(8,128)(2,1)} %copy-done.6, bf16[256,1024]{1,0:T(8,128)(2,1)} %copy-done.7, bf16[256,1024]{1,0:T(8,128)(2,1)} %bitcast.17, bf16[256,1536]{1,0:T(8,128)(2,1)} %copy-done, ...), custom_call_target="tpu_custom_call" | custom-call | bytes 1 | tf_op jit(solution)/shard_map/group_sums/pallas_call | solution.py:153
  88.2 4.6 %adam_step.2 = (f32[512,1024]{1,0:T(8,128)S(1)}, bf16[4,64,1024]{2,1,0:T(8,128)(2,1)S(1)}, bf16[4,64,1024]{2,1,0:T(8,128)(2,1)}) custom-call(s32[1]{0:T(128)} %bitcast.7.core_ref, f32[512,1024]{1,0:T(8,128)S(1)} %group_sums.5.g_ref, bf16[512,1024]{1,0:T(8,128)(2,1)} %collective-permute-done.11.got_ref, f32[1024,1024]{1,0:T(8,128)} %bitcast.31, ...), custom_call_target="tpu_custom_call" | custom-call | bytes 1 | tf_op jit(solution)/shard_map/adam_step/pallas_call | solution.py:214
  93.6 2.2 %collective-permute-start.12 = (bf16[4,64,1024]{2,1,0:T(8,128)(2,1)}, bf16[4,64,1024]{2,1,0:T(8,128)(2,1)}, u32[]{:S(2)}, u32[]{:S(2)}) collective-permute-start(bf16[4,64,1024]{2,1,0:T(8,128)(2,1)} %get-tuple-element.58), channel_id=1, source_target_pairs={{0,8},{8,0},{16,24},{24,16},{32,40},{40,32},{48,56},{56,48},{64,72... | collective-permute-start | bytes 1572872 | tf_op jit(solution)/shard_map/ppermute | solution.py:51
  95.9 1.8 %collective-permute-done.12.got_ref = bf16[4,64,1024]{2,1,0:T(8,128)(2,1)} collective-permute-done((bf16[4,64,1024]{2,1,0:T(8,128)(2,1)}, bf16[4,64,1024]{2,1,0:T(8,128)(2,1)}, u32[]{:S(2)}, u32[]{:S(2)}) %collective-permute-start.12) | collective-permute-done | bytes 524320 | tf_op jit(solution)/shard_map/ppermute | solution.py:51
  97.7 1.0 copy-done.11
  98.7 1.9 %core_sums.2 = (bf16[64,1024]{1,0:T(8,128)(2,1)S(1)}, bf16[64,1024]{1,0:T(8,128)(2,1)}, bf16[64,1024]{1,0:T(8,128)(2,1)}, bf16[64,1024]{1,0:T(8,128)(2,1)}) custom-call(s32[2]{0:T(128)S(1)} %pad_add_fusion.1.x_ref.place_ref, bf16[4,64,1024]{2,1,0:T(8,128)(2,1)S(1)} %copy-done.11, bf16[4,64,1024]{2,1,0:T(8,128)(2,1)} %collective-permute-done.12.got_ref), custom_call_target="tpu_custom_call" | custom-call | bytes 1 | tf_op jit(solution)/shard_map/core_sums/pallas_call | solution.py:309
  100.6 1.2 collective-permute-start.13
  101.8 2.5 %collective-permute-start.14 = (bf16[64,1024]{1,0:T(8,128)(2,1)}, bf16[64,1024]{1,0:T(8,128)(2,1)}, u32[]{:S(2)}, u32[]{:S(2)}) collective-permute-start(bf16[64,1024]{1,0:T(8,128)(2,1)} %get-tuple-element.61), channel_id=1, source_target_pairs={{0,32},{8,40},{16,48},{24,56},{32,0},{40,8},{48,16},{56,24},{64,96... | collective-permute-start | bytes 393224 | tf_op jit(solution)/shard_map/ppermute | solution.py:51
  104.3 1.2 collective-permute-start.15
  105.4 3.4 %group_sums.7.g_ref = f32[512,1024]{1,0:T(8,128)S(1)} custom-call(bf16[256,2048]{1,0:T(8,128)(2,1)} %copy-done.4, bf16[256,1024]{1,0:T(8,128)(2,1)} %copy-done.5, bf16[256,1024]{1,0:T(8,128)(2,1)} %copy-done.6, bf16[256,1024]{1,0:T(8,128)(2,1)} %copy-done.7, bf16[256,1024]{1,0:T(8,128)(2,1)} %bitcast.18, bf16[256,1536]{1,0:T(8,128)(2,1)} %copy-done, ...), custom_call_target="tpu_custom_call" | custom-call | bytes 1 | tf_op jit(solution)/shard_map/group_sums/pallas_call | solution.py:153
  108.8 1.8 %collective-permute-done.14.p2 = bf16[64,1024]{1,0:T(8,128)(2,1)} collective-permute-done((bf16[64,1024]{1,0:T(8,128)(2,1)}, bf16[64,1024]{1,0:T(8,128)(2,1)}, u32[]{:S(2)}, u32[]{:S(2)}) %collective-permute-start.14) | collective-permute-done | bytes 131104 | tf_op jit(solution)/shard_map/ppermute | solution.py:51
  110.7 1.2 x_sums.2
  111.8 3.8 %adam_step.3 = (f32[512,1024]{1,0:T(8,128)S(1)}, bf16[4,64,1024]{2,1,0:T(8,128)(2,1)S(1)}, bf16[4,64,1024]{2,1,0:T(8,128)(2,1)S(1)}) custom-call(s32[1]{0:T(128)} %bitcast.7.core_ref, f32[512,1024]{1,0:T(8,128)S(1)} %group_sums.7.g_ref, bf16[512,1024]{1,0:T(8,128)(2,1)} %collective-permute-done.18.got_ref, f32[1024,1024]{1,0:T(8,128)} %bitcast.32, ...), custom_call_target="tpu_custom_call" | custom-call | bytes 1 | tf_op jit(solution)/shard_map/adam_step/pallas_call | solution.py:214
  115.6 1.3 collective-permute-start.19
  117.6 1.9 %collective-permute-start.17 = (bf16[256,2048]{1,0:T(8,128)(2,1)}, bf16[256,2048]{1,0:T(8,128)(2,1)S(1)}, u32[]{:S(2)}, u32[]{:S(2)}) collective-permute-start(bf16[256,2048]{1,0:T(8,128)(2,1)} %gate.20), channel_id=1, source_target_pairs={{0,3},{1,0},{2,1},{3,2},{4,7},{5,4},{6,5},{7,6},{8,11},{9,8},{10,9... | collective-permute-start | bytes 3145736 | tf_op jit(solution)/shard_map/ppermute | solution.py:33
  120.3 1.1 collective-permute-start.20
  121.4 2.1 %collective-permute-start.21 = (bf16[64,1024]{1,0:T(8,128)(2,1)S(1)}, bf16[64,1024]{1,0:T(8,128)(2,1)S(1)}, u32[]{:S(2)}, u32[]{:S(2)}) collective-permute-start(bf16[64,1024]{1,0:T(8,128)(2,1)S(1)} %get-tuple-element.69), channel_id=1, source_target_pairs={{0,32},{8,40},{16,48},{24,56},{32,0},{40,8},{48,16},{56,24},{64,96... | collective-permute-start | bytes 393224 | tf_op jit(solution)/shard_map/ppermute | solution.py:51
  123.5 1.3 collective-permute-start.22
  124.8 1.2 collective-permute-done.20.p1.refs_1_
  126.7 2.6 %collective-permute-done.21.p2 = bf16[64,1024]{1,0:T(8,128)(2,1)S(1)} collective-permute-done((bf16[64,1024]{1,0:T(8,128)(2,1)S(1)}, bf16[64,1024]{1,0:T(8,128)(2,1)S(1)}, u32[]{:S(2)}, u32[]{:S(2)}) %collective-permute-start.21) | collective-permute-done | bytes 131104 | tf_op jit(solution)/shard_map/ppermute | solution.py:51
  129.4 0.8 collective-permute-start.23
  130.3 3.4 %collective-permute-start.32 = (bf16[64,1024]{1,0:T(8,128)(2,1)S(1)}, bf16[64,1024]{1,0:T(8,128)(2,1)S(1)}, u32[]{:S(2)}, u32[]{:S(2)}) collective-permute-start(bf16[64,1024]{1,0:T(8,128)(2,1)S(1)} %gate.23.refs_0_), channel_id=1, source_target_pairs={{0,8},{8,0},{16,24},{24,16},{32,40},{40,32},{48,56},{56,48},{64,72... | collective-permute-start | bytes 393224 | tf_op jit(solution)/shard_map/ppermute | solution.py:51
  134.1 1.9 %collective-permute-start.35 = (bf16[64,1024]{1,0:T(8,128)(2,1)S(1)}, bf16[64,1024]{1,0:T(8,128)(2,1)S(1)}, u32[]{:S(2)}, u32[]{:S(2)}) collective-permute-start(bf16[64,1024]{1,0:T(8,128)(2,1)S(1)} %gate.23.refs_0_), channel_id=1, source_target_pairs={{0,32},{8,40},{16,48},{24,56},{32,0},{40,8},{48,16},{56,24},{64,96... | collective-permute-start | bytes 393224 | tf_op jit(solution)/shard_map/ppermute | solution.py:51
  135.9 0.9 outer_step.3
  136.8 1.1 collective-permute-start.28
  137.9 2.6 %collective-permute-done.33.refs_2_ = bf16[64,1024]{1,0:T(8,128)(2,1)S(1)} collective-permute-done((bf16[64,1024]{1,0:T(8,128)(2,1)S(1)}, bf16[64,1024]{1,0:T(8,128)(2,1)S(1)}, u32[]{:S(2)}, u32[]{:S(2)}) %collective-permute-start.33) | collective-permute-done | bytes 131104 | tf_op jit(solution)/shard_map/ppermute | solution.py:51
  140.5 1.6 collective-permute-done.35.refs_4_
  142.1 2.0 %collective-permute-done.28.refs_0_ = bf16[64,1024]{1,0:T(8,128)(2,1)S(1)} collective-permute-done((bf16[64,1024]{1,0:T(8,128)(2,1)S(1)}, bf16[64,1024]{1,0:T(8,128)(2,1)S(1)}, u32[]{:S(2)}, u32[]{:S(2)}) %collective-permute-start.28) | collective-permute-done | bytes 131104 | tf_op jit(solution)/shard_map/ppermute | solution.py:51
  144.0 2.0 %collective-permute-start.30 = (bf16[64,1024]{1,0:T(8,128)(2,1)S(1)}, bf16[64,1024]{1,0:T(8,128)(2,1)S(1)}, u32[]{:S(2)}, u32[]{:S(2)}) collective-permute-start(bf16[64,1024]{1,0:T(8,128)(2,1)S(1)} %get-tuple-element.76.refs_4_.refs_0_), channel_id=1, source_target_pairs={{0,48},{8,56},{16,0},{24,8},{32,16},{40,24},{48,32},{56,40},{64,11... | collective-permute-start | bytes 393224 | tf_op jit(solution)/shard_map/ppermute | solution.py:51
  146.0 3.4 %collective-permute-start.34 = (bf16[64,1024]{1,0:T(8,128)(2,1)S(1)}, bf16[64,1024]{1,0:T(8,128)(2,1)S(1)}, u32[]{:S(2)}, u32[]{:S(2)}) collective-permute-start(bf16[64,1024]{1,0:T(8,128)(2,1)S(1)} %collective-permute-done.33.refs_2_), channel_id=1, source_target_pairs={{0,8},{8,0},{16,24},{24,16},{32,40},{40,32},{48,56},{56,48},{64,72... | collective-permute-start | bytes 393224 | tf_op jit(solution)/shard_map/ppermute | solution.py:51
  149.5 3.3 %assemble.1.refs_1_ = bf16[256,8192]{1,0:T(8,128)(2,1)} custom-call(s32[2]{0:T(128)S(1)} %pad_add_fusion.place_ref, bf16[256,2048]{1,0:T(8,128)(2,1)} %get-tuple-element.51.refs_8_.refs_0_, bf16[256,2048]{1,0:T(8,128)(2,1)S(1)} %collective-permute-done.16.refs_1_, bf16[256,2048]{1,0:T(8,128)(2,1)S(1)} %collective-permute-done.10.refs_1_.refs_2_, ...), custom_call_target="tpu_custom_call" | custom-call | bytes 1 | tf_op jit(solution)/shard_map/assemble/pallas_call | solution.py:291
  154.7 2.5 %mix.2.refs_8_ = f32[1024,1024]{1,0:T(8,128)} custom-call(s32[2]{0:T(128)S(1)} %pad_add_fusion.1.x_ref.place_ref, f32[512,1024]{1,0:T(8,128)S(1)} %gate.22.upd, bf16[64,1024]{1,0:T(8,128)(2,1)S(1)} %gate.23.refs_0_, bf16[64,1024]{1,0:T(8,128)(2,1)S(1)} %collective-permute-done.32.refs_1_, bf16[64,1024]{1,0:T(8,128)(2,1)S(1)} %collective-permute-done.33.refs_2_, ...), custom_call_target="tpu_custom_call" | custom-call | bytes 1 | tf_op jit(solution)/shard_map/mix/pallas_call | solution.py:390
  157.2 2.5 %mix.3 = f32[1024,1024]{1,0:T(8,128)} custom-call(s32[2]{0:T(128)S(1)} %pad_add_fusion.1.x_ref.place_ref, f32[512,1024]{1,0:T(8,128)S(1)} %get-tuple-element.77.upd, bf16[64,1024]{1,0:T(8,128)(2,1)S(1)} %get-tuple-element.76.refs_4_.refs_0_, bf16[64,1024]{1,0:T(8,128)(2,1)S(1)} %collective-permute-done.25.refs_1_, ...), custom_call_target="tpu_custom_call", output_to_operand_aliasing={{}: (10, {})} | custom-call | bytes 1 | tf_op jit(solution)/shard_map/mix/pallas_call | solution.py:390
  (85 shorter events, 9.8 us)
Async XLA Ops:
  5.3 56.8 %copy-start.4 = (bf16[256,2048]{1,0:T(8,128)(2,1)}, bf16[256,2048]{1,0:T(8,128)(2,1)S(1)}, u32[]{:S(2)}) copy-start(bf16[256,2048]{1,0:T(8,128)(2,1)S(1)} %get-tuple-element.47.refs_0_) | copy-start | bytes 3145732
  5.3 46.6 %copy-start.3 = (bf16[1,256,1024]{2,1,0:T(8,128)(2,1)S(1)}, bf16[1,256,1024]{2,1,0:T(8,128)(2,1)}, u32[]{:S(2)}) copy-start(bf16[1,256,1024]{2,1,0:T(8,128)(2,1)} %param.8) | copy-start | bytes 1572868
  5.3 56.7 %collective-permute-start = (bf16[1024,1024]{1,0:T(8,128)(2,1)S(1)}, bf16[1024,1024]{1,0:T(8,128)(2,1)S(1)}, u32[]{:S(2)}, u32[]{:S(2)}) collective-permute-start(bf16[1024,1024]{1,0:T(8,128)(2,1)S(1)} %get-tuple-element.43.w0), channel_id=1, source_target_pairs={{0,4},{1,5},{2,6},{3,7},{4,0},{5,1},{6,2},{7,3},{8,12},{9,13},{10,... | collective-permute-start | bytes 6291464 | tf_op jit(solution)/shard_map/ppermute | solution.py:38
  9.8 19.4 %collective-permute-start.1 = (bf16[256,1536]{1,0:T(8,128)(2,1)S(1)}, bf16[256,1536]{1,0:T(8,128)(2,1)S(1)}, u32[]{:S(2)}, u32[]{:S(2)}) collective-permute-start(bf16[256,1536]{1,0:T(8,128)(2,1)S(1)} %get-tuple-element.44), channel_id=1, source_target_pairs={{0,1},{1,2},{2,3},{3,0},{4,5},{5,6},{6,7},{7,4},{8,9},{9,10},{10,1... | collective-permute-start | bytes 2359304 | tf_op jit(solution)/shard_map/ppermute | solution.py:33
  11.1 36.1 %collective-permute-start.2 = (bf16[256,1536]{1,0:T(8,128)(2,1)S(1)}, bf16[256,1536]{1,0:T(8,128)(2,1)S(1)}, u32[]{:S(2)}, u32[]{:S(2)}) collective-permute-start(bf16[256,1536]{1,0:T(8,128)(2,1)S(1)} %get-tuple-element.45), channel_id=1, source_target_pairs={{0,2},{1,3},{2,0},{3,1},{4,6},{5,7},{6,4},{7,5},{8,10},{9,11},{10,... | collective-permute-start | bytes 2359304 | tf_op jit(solution)/shard_map/ppermute | solution.py:33
  13.7 34.3 %collective-permute-start.3 = (bf16[256,1536]{1,0:T(8,128)(2,1)S(1)}, bf16[256,1536]{1,0:T(8,128)(2,1)S(1)}, u32[]{:S(2)}, u32[]{:S(2)}) collective-permute-start(bf16[256,1536]{1,0:T(8,128)(2,1)S(1)} %get-tuple-element.46), channel_id=1, source_target_pairs={{0,3},{1,0},{2,1},{3,2},{4,7},{5,4},{6,5},{7,6},{8,11},{9,8},{10,9... | collective-permute-start | bytes 2359304 | tf_op jit(solution)/shard_map/ppermute | solution.py:33
  29.2 35.3 %copy-start = (bf16[256,1536]{1,0:T(8,128)(2,1)}, bf16[256,1536]{1,0:T(8,128)(2,1)S(1)}, u32[]{:S(2)}) copy-start(bf16[256,1536]{1,0:T(8,128)(2,1)S(1)} %collective-permute-done.1.refs_1_.refs_5_.c1) | copy-start | bytes 2359300
  29.2 26.0 %collective-permute-start.4 = (bf16[256,512]{1,0:T(8,128)(2,1)S(1)}, bf16[256,512]{1,0:T(8,128)(2,1)S(1)}, u32[]{:S(2)}, u32[]{:S(2)}) collective-permute-start(bf16[256,512]{1,0:T(8,128)(2,1)S(1)} %gate.12), channel_id=1, source_target_pairs={{0,1},{1,2},{2,3},{3,0},{4,5},{5,6},{6,7},{7,4},{8,9},{9,10},{10,1... | collective-permute-start | bytes 786440 | tf_op jit(solution)/shard_map/ppermute | solution.py:33
  47.2 17.3 %copy-start.1 = (bf16[256,1536]{1,0:T(8,128)(2,1)}, bf16[256,1536]{1,0:T(8,128)(2,1)S(1)}, u32[]{:S(2)}) copy-start(bf16[256,1536]{1,0:T(8,128)(2,1)S(1)} %collective-permute-done.2.refs_1_.refs_6_.c2.refs_2_) | copy-start | bytes 2359300
  47.2 11.2 %collective-permute-start.5 = (bf16[256,512]{1,0:T(8,128)(2,1)S(1)}, bf16[256,512]{1,0:T(8,128)(2,1)S(1)}, u32[]{:S(2)}, u32[]{:S(2)}) collective-permute-start(bf16[256,512]{1,0:T(8,128)(2,1)S(1)} %gate.13), channel_id=1, source_target_pairs={{0,2},{1,3},{2,0},{3,1},{4,6},{5,7},{6,4},{7,5},{8,10},{9,11},{10,... | collective-permute-start | bytes 786440 | tf_op jit(solution)/shard_map/ppermute | solution.py:33
  48.0 16.5 %copy-start.2 = (bf16[256,1536]{1,0:T(8,128)(2,1)}, bf16[256,1536]{1,0:T(8,128)(2,1)S(1)}, u32[]{:S(2)}) copy-start(bf16[256,1536]{1,0:T(8,128)(2,1)S(1)} %collective-permute-done.3.refs_1_.refs_7_.c3.refs_3_) | copy-start | bytes 2359300
  48.0 10.9 %collective-permute-start.6 = (bf16[256,512]{1,0:T(8,128)(2,1)S(1)}, bf16[256,512]{1,0:T(8,128)(2,1)S(1)}, u32[]{:S(2)}, u32[]{:S(2)}) collective-permute-start(bf16[256,512]{1,0:T(8,128)(2,1)S(1)} %gate.14), channel_id=1, source_target_pairs={{0,3},{1,0},{2,1},{3,2},{4,7},{5,4},{6,5},{7,6},{8,11},{9,8},{10,9... | collective-permute-start | bytes 786440 | tf_op jit(solution)/shard_map/ppermute | solution.py:33
  54.5 33.7 %collective-permute-start.11 = (bf16[512,1024]{1,0:T(8,128)(2,1)}, bf16[512,1024]{1,0:T(8,128)(2,1)}, u32[]{:S(2)}, u32[]{:S(2)}) collective-permute-start(bf16[512,1024]{1,0:T(8,128)(2,1)} %group_sums.6), channel_id=1, source_target_pairs={{0,4},{1,5},{2,6},{3,7},{4,0},{5,1},{6,2},{7,3},{8,12},{9,13},{10,... | collective-permute-start | bytes 3145736 | tf_op jit(solution)/shard_map/ppermute | solution.py:38
  55.2 17.2 %collective-permute-start.7 = (bf16[256,1024]{1,0:T(8,128)(2,1)S(1)}, bf16[256,1024]{1,0:T(8,128)(2,1)S(1)}, u32[]{:S(2)}, u32[]{:S(2)}) collective-permute-start(bf16[256,1024]{1,0:T(8,128)(2,1)S(1)} %gate.15), channel_id=1, source_target_pairs={{0,1},{1,2},{2,3},{3,0},{4,5},{5,6},{6,7},{7,4},{8,9},{9,10},{10,1... | collective-permute-start | bytes 1572872 | tf_op jit(solution)/shard_map/ppermute | solution.py:33
  58.5 22.3 %collective-permute-start.8 = (bf16[256,1024]{1,0:T(8,128)(2,1)S(1)}, bf16[256,1024]{1,0:T(8,128)(2,1)S(1)}, u32[]{:S(2)}, u32[]{:S(2)}) collective-permute-start(bf16[256,1024]{1,0:T(8,128)(2,1)S(1)} %gate.16), channel_id=1, source_target_pairs={{0,2},{1,3},{2,0},{3,1},{4,6},{5,7},{6,4},{7,5},{8,10},{9,11},{10,... | collective-permute-start | bytes 1572872 | tf_op jit(solution)/shard_map/ppermute | solution.py:33
  58.9 21.9 %collective-permute-start.9 = (bf16[256,1024]{1,0:T(8,128)(2,1)S(1)}, bf16[256,1024]{1,0:T(8,128)(2,1)S(1)}, u32[]{:S(2)}, u32[]{:S(2)}) collective-permute-start(bf16[256,1024]{1,0:T(8,128)(2,1)S(1)} %gate.17), channel_id=1, source_target_pairs={{0,3},{1,0},{2,1},{3,2},{4,7},{5,4},{6,5},{7,6},{8,11},{9,8},{10,9... | collective-permute-start | bytes 1572872 | tf_op jit(solution)/shard_map/ppermute | solution.py:33
  64.5 47.3 %collective-permute-start.18 = (bf16[512,1024]{1,0:T(8,128)(2,1)}, bf16[512,1024]{1,0:T(8,128)(2,1)}, u32[]{:S(2)}, u32[]{:S(2)}) collective-permute-start(bf16[512,1024]{1,0:T(8,128)(2,1)} %group_sums.4.refs_0_), channel_id=1, source_target_pairs={{0,4},{1,5},{2,6},{3,7},{4,0},{5,1},{6,2},{7,3},{8,12},{9,13},{10,... | collective-permute-start | bytes 3145736 | tf_op jit(solution)/shard_map/ppermute | solution.py:38
  72.5 12.3 %copy-start.5 = (bf16[256,1024]{1,0:T(8,128)(2,1)}, bf16[256,1024]{1,0:T(8,128)(2,1)S(1)}, u32[]{:S(2)}) copy-start(bf16[256,1024]{1,0:T(8,128)(2,1)S(1)} %collective-permute-done.7.refs_1_) | copy-start | bytes 1572868
  82.4 34.5 %collective-permute-start.10 = (bf16[256,2048]{1,0:T(8,128)(2,1)}, bf16[256,2048]{1,0:T(8,128)(2,1)S(1)}, u32[]{:S(2)}, u32[]{:S(2)}) collective-permute-start(bf16[256,2048]{1,0:T(8,128)(2,1)} %gate.18), channel_id=1, source_target_pairs={{0,2},{1,3},{2,0},{3,1},{4,6},{5,7},{6,4},{7,5},{8,10},{9,11},{10,... | collective-permute-start | bytes 3145736 | tf_op jit(solution)/shard_map/ppermute | solution.py:33
  93.6 4.1 %collective-permute-start.12 = (bf16[4,64,1024]{2,1,0:T(8,128)(2,1)}, bf16[4,64,1024]{2,1,0:T(8,128)(2,1)}, u32[]{:S(2)}, u32[]{:S(2)}) collective-permute-start(bf16[4,64,1024]{2,1,0:T(8,128)(2,1)} %get-tuple-element.58), channel_id=1, source_target_pairs={{0,8},{8,0},{16,24},{24,16},{32,40},{40,32},{48,56},{56,48},{64,72... | collective-permute-start | bytes 1572872 | tf_op jit(solution)/shard_map/ppermute | solution.py:51
  97.7 1.0 copy-start.11
  98.7 11.9 %copy-start.8 = (f32[1,64,1024]{2,1,0:T(8,128)S(1)}, f32[1,64,1024]{2,1,0:T(8,128)}, u32[]{:S(2)}) copy-start(f32[1,64,1024]{2,1,0:T(8,128)} %param.12) | copy-start | bytes 786436
  100.6 8.2 %collective-permute-start.13 = (bf16[64,1024]{1,0:T(8,128)(2,1)}, bf16[64,1024]{1,0:T(8,128)(2,1)}, u32[]{:S(2)}, u32[]{:S(2)}) collective-permute-start(bf16[64,1024]{1,0:T(8,128)(2,1)} %get-tuple-element.60), channel_id=1, source_target_pairs={{0,16},{8,24},{16,32},{24,40},{32,48},{40,56},{48,0},{56,8},{64,80... | collective-permute-start | bytes 393224 | tf_op jit(solution)/shard_map/ppermute | solution.py:51
  101.8 8.8 %collective-permute-start.14 = (bf16[64,1024]{1,0:T(8,128)(2,1)}, bf16[64,1024]{1,0:T(8,128)(2,1)}, u32[]{:S(2)}, u32[]{:S(2)}) collective-permute-start(bf16[64,1024]{1,0:T(8,128)(2,1)} %get-tuple-element.61), channel_id=1, source_target_pairs={{0,32},{8,40},{16,48},{24,56},{32,0},{40,8},{48,16},{56,24},{64,96... | collective-permute-start | bytes 393224 | tf_op jit(solution)/shard_map/ppermute | solution.py:51
  104.3 6.4 %collective-permute-start.15 = (bf16[64,1024]{1,0:T(8,128)(2,1)}, bf16[64,1024]{1,0:T(8,128)(2,1)}, u32[]{:S(2)}, u32[]{:S(2)}) collective-permute-start(bf16[64,1024]{1,0:T(8,128)(2,1)} %get-tuple-element.62), channel_id=1, source_target_pairs={{0,48},{8,56},{16,0},{24,8},{32,16},{40,24},{48,32},{56,40},{64,11... | collective-permute-start | bytes 393224 | tf_op jit(solution)/shard_map/ppermute | solution.py:51
  105.4 5.2 %copy-start.9 = (f32[1,64,1024]{2,1,0:T(8,128)S(1)}, f32[1,64,1024]{2,1,0:T(8,128)}, u32[]{:S(2)}) copy-start(f32[1,64,1024]{2,1,0:T(8,128)} %param.13) | copy-start | bytes 786436
  115.6 4.0 %collective-permute-start.19 = (bf16[4,64,1024]{2,1,0:T(8,128)(2,1)S(1)}, bf16[4,64,1024]{2,1,0:T(8,128)(2,1)S(1)}, u32[]{:S(2)}, u32[]{:S(2)}) collective-permute-start(bf16[4,64,1024]{2,1,0:T(8,128)(2,1)S(1)} %get-tuple-element.66), channel_id=1, source_target_pairs={{0,8},{8,0},{16,24},{24,16},{32,40},{40,32},{48,56},{56,48},{64,72... | collective-permute-start | bytes 1572872 | tf_op jit(solution)/shard_map/ppermute | solution.py:51
  116.9 29.1 %collective-permute-start.16 = (bf16[256,2048]{1,0:T(8,128)(2,1)}, bf16[256,2048]{1,0:T(8,128)(2,1)S(1)}, u32[]{:S(2)}, u32[]{:S(2)}) collective-permute-start(bf16[256,2048]{1,0:T(8,128)(2,1)} %gate.19), channel_id=1, source_target_pairs={{0,1},{1,2},{2,3},{3,0},{4,5},{5,6},{6,7},{7,4},{8,9},{9,10},{10,1... | collective-permute-start | bytes 3145736 | tf_op jit(solution)/shard_map/ppermute | solution.py:33
  117.6 31.7 %collective-permute-start.17 = (bf16[256,2048]{1,0:T(8,128)(2,1)}, bf16[256,2048]{1,0:T(8,128)(2,1)S(1)}, u32[]{:S(2)}, u32[]{:S(2)}) collective-permute-start(bf16[256,2048]{1,0:T(8,128)(2,1)} %gate.20), channel_id=1, source_target_pairs={{0,3},{1,0},{2,1},{3,2},{4,7},{5,4},{6,5},{7,6},{8,11},{9,8},{10,9... | collective-permute-start | bytes 3145736 | tf_op jit(solution)/shard_map/ppermute | solution.py:33
  120.3 5.7 %collective-permute-start.20 = (bf16[64,1024]{1,0:T(8,128)(2,1)S(1)}, bf16[64,1024]{1,0:T(8,128)(2,1)S(1)}, u32[]{:S(2)}, u32[]{:S(2)}) collective-permute-start(bf16[64,1024]{1,0:T(8,128)(2,1)S(1)} %get-tuple-element.68), channel_id=1, source_target_pairs={{0,16},{8,24},{16,32},{24,40},{32,48},{40,56},{48,0},{56,8},{64,80... | collective-permute-start | bytes 393224 | tf_op jit(solution)/shard_map/ppermute | solution.py:51
  121.4 7.9 %collective-permute-start.21 = (bf16[64,1024]{1,0:T(8,128)(2,1)S(1)}, bf16[64,1024]{1,0:T(8,128)(2,1)S(1)}, u32[]{:S(2)}, u32[]{:S(2)}) collective-permute-start(bf16[64,1024]{1,0:T(8,128)(2,1)S(1)} %get-tuple-element.69), channel_id=1, source_target_pairs={{0,32},{8,40},{16,48},{24,56},{32,0},{40,8},{48,16},{56,24},{64,96... | collective-permute-start | bytes 393224 | tf_op jit(solution)/shard_map/ppermute | solution.py:51
  123.5 5.7 %collective-permute-start.22 = (bf16[64,1024]{1,0:T(8,128)(2,1)S(1)}, bf16[64,1024]{1,0:T(8,128)(2,1)S(1)}, u32[]{:S(2)}, u32[]{:S(2)}) collective-permute-start(bf16[64,1024]{1,0:T(8,128)(2,1)S(1)} %get-tuple-element.70), channel_id=1, source_target_pairs={{0,48},{8,56},{16,0},{24,8},{32,16},{40,24},{48,32},{56,40},{64,11... | collective-permute-start | bytes 393224 | tf_op jit(solution)/shard_map/ppermute | solution.py:51
  125.9 4.3 %collective-permute-start.24 = (bf16[64,1024]{1,0:T(8,128)(2,1)S(1)}, bf16[64,1024]{1,0:T(8,128)(2,1)S(1)}, u32[]{:S(2)}, u32[]{:S(2)}) collective-permute-start(bf16[64,1024]{1,0:T(8,128)(2,1)S(1)} %get-tuple-element.63.refs_2_.refs_0_), channel_id=1, source_target_pairs={{0,64},{8,72},{16,80},{24,88},{32,96},{40,104},{48,112},{56,120},{... | collective-permute-start | bytes 393224 | tf_op jit(solution)/shard_map/ppermute | solution.py:51
  129.4 4.7 %collective-permute-start.23 = (bf16[64,1024]{1,0:T(8,128)(2,1)S(1)}, bf16[64,1024]{1,0:T(8,128)(2,1)S(1)}, u32[]{:S(2)}, u32[]{:S(2)}) collective-permute-start(bf16[64,1024]{1,0:T(8,128)(2,1)S(1)} %get-tuple-element.72.refs_1_), channel_id=1, source_target_pairs={{0,64},{8,72},{16,80},{24,88},{32,96},{40,104},{48,112},{56,120},{... | collective-permute-start | bytes 393224 | tf_op jit(solution)/shard_map/ppermute | solution.py:51
  130.3 6.5 %collective-permute-start.32 = (bf16[64,1024]{1,0:T(8,128)(2,1)S(1)}, bf16[64,1024]{1,0:T(8,128)(2,1)S(1)}, u32[]{:S(2)}, u32[]{:S(2)}) collective-permute-start(bf16[64,1024]{1,0:T(8,128)(2,1)S(1)} %gate.23.refs_0_), channel_id=1, source_target_pairs={{0,8},{8,0},{16,24},{24,16},{32,40},{40,32},{48,56},{56,48},{64,72... | collective-permute-start | bytes 393224 | tf_op jit(solution)/shard_map/ppermute | solution.py:51
  133.7 6.7 %collective-permute-start.33 = (bf16[64,1024]{1,0:T(8,128)(2,1)S(1)}, bf16[64,1024]{1,0:T(8,128)(2,1)S(1)}, u32[]{:S(2)}, u32[]{:S(2)}) collective-permute-start(bf16[64,1024]{1,0:T(8,128)(2,1)S(1)} %gate.23.refs_0_), channel_id=1, source_target_pairs={{0,16},{8,24},{16,32},{24,40},{32,48},{40,56},{48,0},{56,8},{64,80... | collective-permute-start | bytes 393224 | tf_op jit(solution)/shard_map/ppermute | solution.py:51
  134.1 8.0 %collective-permute-start.35 = (bf16[64,1024]{1,0:T(8,128)(2,1)S(1)}, bf16[64,1024]{1,0:T(8,128)(2,1)S(1)}, u32[]{:S(2)}, u32[]{:S(2)}) collective-permute-start(bf16[64,1024]{1,0:T(8,128)(2,1)S(1)} %gate.23.refs_0_), channel_id=1, source_target_pairs={{0,32},{8,40},{16,48},{24,56},{32,0},{40,8},{48,16},{56,24},{64,96... | collective-permute-start | bytes 393224 | tf_op jit(solution)/shard_map/ppermute | solution.py:51
  136.8 7.2 %collective-permute-start.28 = (bf16[64,1024]{1,0:T(8,128)(2,1)S(1)}, bf16[64,1024]{1,0:T(8,128)(2,1)S(1)}, u32[]{:S(2)}, u32[]{:S(2)}) collective-permute-start(bf16[64,1024]{1,0:T(8,128)(2,1)S(1)} %get-tuple-element.76.refs_4_.refs_0_), channel_id=1, source_target_pairs={{0,32},{8,40},{16,48},{24,56},{32,0},{40,8},{48,16},{56,24},{64,96... | collective-permute-start | bytes 393224 | tf_op jit(solution)/shard_map/ppermute | solution.py:51
  140.5 12.3 %collective-permute-start.37 = (bf16[64,1024]{1,0:T(8,128)(2,1)S(1)}, bf16[64,1024]{1,0:T(8,128)(2,1)S(1)}, u32[]{:S(2)}, u32[]{:S(2)}) collective-permute-start(bf16[64,1024]{1,0:T(8,128)(2,1)S(1)} %gate.23.refs_0_), channel_id=1, source_target_pairs={{0,48},{8,56},{16,0},{24,8},{32,16},{40,24},{48,32},{56,40},{64,11... | collective-permute-start | bytes 393224 | tf_op jit(solution)/shard_map/ppermute | solution.py:51
  142.1 11.3 %collective-permute-start.26 = (bf16[64,1024]{1,0:T(8,128)(2,1)S(1)}, bf16[64,1024]{1,0:T(8,128)(2,1)S(1)}, u32[]{:S(2)}, u32[]{:S(2)}) collective-permute-start(bf16[64,1024]{1,0:T(8,128)(2,1)S(1)} %get-tuple-element.76.refs_4_.refs_0_), channel_id=1, source_target_pairs={{0,16},{8,24},{16,32},{24,40},{32,48},{40,56},{48,0},{56,8},{64,80... | collective-permute-start | bytes 393224 | tf_op jit(solution)/shard_map/ppermute | solution.py:51
  144.0 9.4 %collective-permute-start.30 = (bf16[64,1024]{1,0:T(8,128)(2,1)S(1)}, bf16[64,1024]{1,0:T(8,128)(2,1)S(1)}, u32[]{:S(2)}, u32[]{:S(2)}) collective-permute-start(bf16[64,1024]{1,0:T(8,128)(2,1)S(1)} %get-tuple-element.76.refs_4_.refs_0_), channel_id=1, source_target_pairs={{0,48},{8,56},{16,0},{24,8},{32,16},{40,24},{48,32},{56,40},{64,11... | collective-permute-start | bytes 393224 | tf_op jit(solution)/shard_map/ppermute | solution.py:51
  146.0 7.8 %collective-permute-start.34 = (bf16[64,1024]{1,0:T(8,128)(2,1)S(1)}, bf16[64,1024]{1,0:T(8,128)(2,1)S(1)}, u32[]{:S(2)}, u32[]{:S(2)}) collective-permute-start(bf16[64,1024]{1,0:T(8,128)(2,1)S(1)} %collective-permute-done.33.refs_2_), channel_id=1, source_target_pairs={{0,8},{8,0},{16,24},{24,16},{32,40},{40,32},{48,56},{56,48},{64,72... | collective-permute-start | bytes 393224 | tf_op jit(solution)/shard_map/ppermute | solution.py:51
  149.4 4.6 %collective-permute-start.36 = (bf16[64,1024]{1,0:T(8,128)(2,1)S(1)}, bf16[64,1024]{1,0:T(8,128)(2,1)S(1)}, u32[]{:S(2)}, u32[]{:S(2)}) collective-permute-start(bf16[64,1024]{1,0:T(8,128)(2,1)S(1)} %collective-permute-done.35.refs_4_), channel_id=1, source_target_pairs={{0,8},{8,0},{16,24},{24,16},{32,40},{40,32},{48,56},{56,48},{64,72... | collective-permute-start | bytes 393224 | tf_op jit(solution)/shard_map/ppermute | solution.py:51
  152.8 4.4 %collective-permute-start.25 = (bf16[64,1024]{1,0:T(8,128)(2,1)S(1)}, bf16[64,1024]{1,0:T(8,128)(2,1)S(1)}, u32[]{:S(2)}, u32[]{:S(2)}) collective-permute-start(bf16[64,1024]{1,0:T(8,128)(2,1)S(1)} %get-tuple-element.76.refs_4_.refs_0_), channel_id=1, source_target_pairs={{0,8},{8,0},{16,24},{24,16},{32,40},{40,32},{48,56},{56,48},{64,72... | collective-permute-start | bytes 393224 | tf_op jit(solution)/shard_map/ppermute | solution.py:51
  153.3 1.3 collective-permute-start.38
  153.4 3.8 %collective-permute-start.27 = (bf16[64,1024]{1,0:T(8,128)(2,1)S(1)}, bf16[64,1024]{1,0:T(8,128)(2,1)S(1)}, u32[]{:S(2)}, u32[]{:S(2)}) collective-permute-start(bf16[64,1024]{1,0:T(8,128)(2,1)S(1)} %collective-permute-done.26.refs_2_), channel_id=1, source_target_pairs={{0,8},{8,0},{16,24},{24,16},{32,40},{40,32},{48,56},{56,48},{64,72... | collective-permute-start | bytes 393224 | tf_op jit(solution)/shard_map/ppermute | solution.py:51
  153.8 3.4 %collective-permute-start.31 = (bf16[64,1024]{1,0:T(8,128)(2,1)S(1)}, bf16[64,1024]{1,0:T(8,128)(2,1)S(1)}, u32[]{:S(2)}, u32[]{:S(2)}) collective-permute-start(bf16[64,1024]{1,0:T(8,128)(2,1)S(1)} %collective-permute-done.30.refs_6_), channel_id=1, source_target_pairs={{0,8},{8,0},{16,24},{24,16},{32,40},{40,32},{48,56},{56,48},{64,72... | collective-permute-start | bytes 393224 | tf_op jit(solution)/shard_map/ppermute | solution.py:51
  153.9 3.3 %collective-permute-start.29 = (bf16[64,1024]{1,0:T(8,128)(2,1)S(1)}, bf16[64,1024]{1,0:T(8,128)(2,1)S(1)}, u32[]{:S(2)}, u32[]{:S(2)}) collective-permute-start(bf16[64,1024]{1,0:T(8,128)(2,1)S(1)} %gate.21.refs_4_), channel_id=1, source_target_pairs={{0,8},{8,0},{16,24},{24,16},{32,40},{40,32},{48,56},{56,48},{64,72... | collective-permute-start | bytes 393224 | tf_op jit(solution)/shard_map/ppermute | solution.py:51
  (3 other events, 2.4 us)

commit v4 on v3

--- a/solution.py
+++ b/solution.py
@@ -419,7 +419,10 @@
     weight_got = swap_z(weight)
     second = [along_y(gate(a, first[k]), k + 1) for k, a in enumerate(second)]
     third = [along_y(gate(a, second[k]), k + 1) for k, a in enumerate(third)]
-    cots = [cot] + first
+    first = [in_hbm(a) for a in first]
+    second = [in_hbm(a) for a in second]
+    own = in_hbm(own)
+    cots = [in_hbm(cot)] + first
 
     partial_0 = group_sums(BF, [(own, 0)] + [(a, KV) for a in first], cots)
     got_0 = swap_z(partial_0)

time: 160 us -> 159 us (level)
  Pallas kernels: 45.3 us -> 50.1 us
  waiting for transfers between devices: 59.8 us -> 56.2 us
    ppermute x12, waiting for transfers between devices: 45.8 us -> 42.2 us  [along_y(): return lax.ppermute(array, 'fsdp', pairs)]
    pallas_call x4, Pallas kernels: 11.8 us -> 15.1 us  [group_sums(): pl.pallas_call(kernel, out_shape=shape(HALF, KV, dtype=dtype), grid=(HALF...]
    unnamed x24 -> x28, local copies, waits for them, and re-layouts: 3.45 us -> 1.9 us
  transfers between devices with their start and end apart: 39 -> 39, of which waited for: 16 -> 15; matrix products, arithmetic and copies ran while one was open for 0% -> 0% of each run, Pallas kernels for 24% -> 27%
where the time goes in v4:
time: 159 us; the launch traced here: 158 us
  waiting for transfers between devices  56.2 us (35%)
  Pallas kernels  50.1 us (32%)
  starting transfers between devices  48.9 us (31%)
  local copies, waits for them, and re-layouts  1.9 us (1%)
    ppermute x12, waiting for transfers between devices, along_y(): return lax.ppermute(array, 'fsdp', pairs)  42.2 us
    ppermute x24, starting transfers between devices, island_shift(): return lax.ppermute(array, 'island', pairs)  27.4 us
    ppermute x12, starting transfers between devices, along_y(): return lax.ppermute(array, 'fsdp', pairs)  17 us
    pallas_call x4, Pallas kernels, group_sums(): pl.pallas_call(kernel, out_shape=shape(HALF, KV, dtype=dtype), grid=(HALF...  15.1 us
    ppermute x24, waiting for transfers between devices, island_shift(): return lax.ppermute(array, 'island', pairs)  14 us
    pallas_call x1, Pallas kernels, input_blocks(): pl.pallas_call(kernel, out_shape=[pltpu.HBM((TOK, 2 * ROWS), BF)] * 4, gr...  8.89 us
    pallas_call x2, Pallas kernels, adam(): pl.pallas_call(kernel, out_shape=[shape(HALF, KV, dtype=F32), shape(4, 64...  8.32 us
    pallas_call x2, Pallas kernels, mix(): pl.pallas_call(kernel, out_shape=shape(ROWS, KV, dtype=F32), grid_spec=pl...  5.03 us
  transfers between devices with their start and end apart: 39, of which 15 were waited for; matrix products, arithmetic and copies ran while one was open for 0% of the time, Pallas kernels for 27%

profile of v4, /device:TPU:1, one launch (start us, length us, event | category | flops | bytes accessed | tf_op | source)
XLA Modules:
  0.0 158.2 jit_solution(13973263294535330081)
XLA Ops:
  0.7 4.5 %pack.1 = (bf16[256,1536]{1,0:T(8,128)(2,1)S(1)}, bf16[256,1536]{1,0:T(8,128)(2,1)S(1)}, bf16[256,1536]{1,0:T(8,128)(2,1)S(1)}, bf16[256,512]{1,0:T(8,128)(2,1)S...) custom-call(s32[2]{0:T(128)S(1)} %pad_add_fusion.place_ref, ...), custom_call_target="tpu_custom_call" | custom-call | bytes 1 | tf_op jit(solution)/shard_map/pack/pallas_call | solution.py:120
  5.3 4.5 %collective-permute-start = (bf16[1024,1024]{1,0:T(8,128)(2,1)S(1)}, bf16[1024,1024]{1,0:T(8,128)(2,1)S(1)}, u32[]{:S(2)}, u32[]{:S(2)}) collective-permute-start(bf16[1024,1024]{1,0:T(8,128)(2,1)S(1)} %get-tuple-element.43.w0), channel_id=1, source_target_pairs={{0,4},{1,5},{2,6},{3,7},{4,0},{5,1},{6,2},{7,3},{8,12},{9,13},{10,... | collective-permute-start | bytes 6291464 | tf_op jit(solution)/shard_map/ppermute | solution.py:38
  9.8 1.3 collective-permute-start.1
  11.1 2.6 %collective-permute-start.2 = (bf16[256,1536]{1,0:T(8,128)(2,1)S(1)}, bf16[256,1536]{1,0:T(8,128)(2,1)S(1)}, u32[]{:S(2)}, u32[]{:S(2)}) collective-permute-start(bf16[256,1536]{1,0:T(8,128)(2,1)S(1)} %get-tuple-element.45), channel_id=1, source_target_pairs={{0,2},{1,3},{2,0},{3,1},{4,6},{5,7},{6,4},{7,5},{8,10},{9,11},{10,... | collective-permute-start | bytes 2359304 | tf_op jit(solution)/shard_map/ppermute | solution.py:33
  13.7 1.1 collective-permute-start.3
  14.8 14.4 %collective-permute-done.1.refs_1_.refs_5_.c1 = bf16[256,1536]{1,0:T(8,128)(2,1)S(1)} collective-permute-done((bf16[256,1536]{1,0:T(8,128)(2,1)S(1)}, bf16[256,1536]{1,0:T(8,128)(2,1)S(1)}, u32[]{:S(2)}, u32[]{:S(2)}) %collective-permute-start.1) | collective-permute-done | bytes 786464 | tf_op jit(solution)/shard_map/ppermute | solution.py:33
  29.2 18.0 %collective-permute-done.2.refs_1_.refs_6_.c2.refs_2_ = bf16[256,1536]{1,0:T(8,128)(2,1)S(1)} collective-permute-done((bf16[256,1536]{1,0:T(8,128)(2,1)S(1)}, bf16[256,1536]{1,0:T(8,128)(2,1)S(1)}, u32[]{:S(2)}, u32[]{:S(2)}) %collective-permute-start.2) | collective-permute-done | bytes 786464 | tf_op jit(solution)/shard_map/ppermute | solution.py:33
  48.0 3.9 %collective-permute-start.6 = (bf16[256,512]{1,0:T(8,128)(2,1)S(1)}, bf16[256,512]{1,0:T(8,128)(2,1)S(1)}, u32[]{:S(2)}, u32[]{:S(2)}) collective-permute-start(bf16[256,512]{1,0:T(8,128)(2,1)S(1)} %gate.14), channel_id=1, source_target_pairs={{0,3},{1,0},{2,1},{3,2},{4,7},{5,4},{6,5},{7,6},{8,11},{9,8},{10,9... | collective-permute-start | bytes 786440 | tf_op jit(solution)/shard_map/ppermute | solution.py:33
  51.9 4.2 %group_sums.6 = bf16[512,1024]{1,0:T(8,128)(2,1)} custom-call(bf16[256,2048]{1,0:T(8,128)(2,1)} %copy-done.3, bf16[256,1536]{1,0:T(8,128)(2,1)} %copy-done, bf16[256,1536]{1,0:T(8,128)(2,1)} %copy-done.1, bf16[256,1536]{1,0:T(8,128)(2,1)} %copy-done.2, bf16[256,1024]{1,0:T(8,128)(2,1)} %bitcast.28, bf16[256,1536]{1,0:T(8,128)(2,1)} %copy-done, ...), custom_call_target="tpu_custom_call" | custom-call | bytes 1 | tf_op jit(solution)/shard_map/group_sums/pallas_call | solution.py:153
  56.2 2.2 %collective-permute-done.5.refs_2_.refs_1_ = bf16[256,512]{1,0:T(8,128)(2,1)S(1)} collective-permute-done((bf16[256,512]{1,0:T(8,128)(2,1)S(1)}, bf16[256,512]{1,0:T(8,128)(2,1)S(1)}, u32[]{:S(2)}, u32[]{:S(2)}) %collective-permute-start.5) | collective-permute-done | bytes 262176 | tf_op jit(solution)/shard_map/ppermute | solution.py:33
  58.8 3.1 %collective-permute-start.9 = (bf16[256,1024]{1,0:T(8,128)(2,1)S(1)}, bf16[256,1024]{1,0:T(8,128)(2,1)S(1)}, u32[]{:S(2)}, u32[]{:S(2)}) collective-permute-start(bf16[256,1024]{1,0:T(8,128)(2,1)S(1)} %gate.17), channel_id=1, source_target_pairs={{0,3},{1,0},{2,1},{3,2},{4,7},{5,4},{6,5},{7,6},{8,11},{9,8},{10,9... | collective-permute-start | bytes 1572872 | tf_op jit(solution)/shard_map/ppermute | solution.py:33
  61.9 4.2 %group_sums.4.refs_0_ = bf16[512,1024]{1,0:T(8,128)(2,1)} custom-call(bf16[256,2048]{1,0:T(8,128)(2,1)} %copy-done.3, bf16[256,512]{1,0:T(8,128)(2,1)} %copy-done.9, bf16[256,512]{1,0:T(8,128)(2,1)} %copy-done.10, bf16[256,512]{1,0:T(8,128)(2,1)} %copy-done.11, bf16[256,1024]{1,0:T(8,128)(2,1)} %bitcast.29, bf16[256,1536]{1,0:T(8,128)(2,1)} %copy-done, ...), custom_call_target="tpu_custom_call" | custom-call | bytes 1 | tf_op jit(solution)/shard_map/group_sums/pallas_call | solution.py:153
  66.1 8.9 %input_blocks.1 = (bf16[256,2048]{1,0:T(8,128)(2,1)}, bf16[256,2048]{1,0:T(8,128)(2,1)}, bf16[256,2048]{1,0:T(8,128)(2,1)}, bf16[256,2048]{1,0:T(8,128)(2,1)}) custom-call(bf16[1024,1024]{1,0:T(8,128)(2,1)S(1)} %get-tuple-element.43.w0, bf16[1024,1024]{1,0:T(8,128)(2,1)S(1)} %collective-permute-done.refs_8_.w1, bf16[256,1024]{1,0:T(8,128)(2,1)} %bitcast.30, ...), custom_call_target="tpu_custom_call" | custom-call | bytes 1 | tf_op jit(solution)/shard_map/input_blocks/pallas_call | solution.py:260
  75.0 5.9 %collective-permute-done.8.refs_2_ = bf16[256,1024]{1,0:T(8,128)(2,1)S(1)} collective-permute-done((bf16[256,1024]{1,0:T(8,128)(2,1)S(1)}, bf16[256,1024]{1,0:T(8,128)(2,1)S(1)}, u32[]{:S(2)}, u32[]{:S(2)}) %collective-permute-start.8) | collective-permute-done | bytes 524320 | tf_op jit(solution)/shard_map/ppermute | solution.py:33
  80.9 1.2 collective-permute-done.9.refs_3_
  82.1 1.5 collective-permute-start.10
  83.6 3.4 %group_sums.5.g_ref = f32[512,1024]{1,0:T(8,128)S(1)} custom-call(bf16[256,2048]{1,0:T(8,128)(2,1)} %copy-done.3, bf16[256,1024]{1,0:T(8,128)(2,1)} %copy-done.4, bf16[256,1024]{1,0:T(8,128)(2,1)} %copy-done.5, bf16[256,1024]{1,0:T(8,128)(2,1)} %copy-done.6, bf16[256,1024]{1,0:T(8,128)(2,1)} %bitcast.31, bf16[256,1536]{1,0:T(8,128)(2,1)} %copy-done, ...), custom_call_target="tpu_custom_call" | custom-call | bytes 1 | tf_op jit(solution)/shard_map/group_sums/pallas_call | solution.py:153
  87.0 4.6 %adam_step.2 = (f32[512,1024]{1,0:T(8,128)S(1)}, bf16[4,64,1024]{2,1,0:T(8,128)(2,1)S(1)}, bf16[4,64,1024]{2,1,0:T(8,128)(2,1)}) custom-call(s32[1]{0:T(128)} %bitcast.7.core_ref, f32[512,1024]{1,0:T(8,128)S(1)} %group_sums.5.g_ref, bf16[512,1024]{1,0:T(8,128)(2,1)} %collective-permute-done.11.got_ref, f32[1024,1024]{1,0:T(8,128)} %bitcast.25, ...), custom_call_target="tpu_custom_call" | custom-call | bytes 1 | tf_op jit(solution)/shard_map/adam_step/pallas_call | solution.py:214
  92.4 1.8 %collective-permute-start.12 = (bf16[4,64,1024]{2,1,0:T(8,128)(2,1)}, bf16[4,64,1024]{2,1,0:T(8,128)(2,1)}, u32[]{:S(2)}, u32[]{:S(2)}) collective-permute-start(bf16[4,64,1024]{2,1,0:T(8,128)(2,1)} %get-tuple-element.58), channel_id=1, source_target_pairs={{0,8},{8,0},{16,24},{24,16},{32,40},{40,32},{48,56},{56,48},{64,72... | collective-permute-start | bytes 1572872 | tf_op jit(solution)/shard_map/ppermute | solution.py:51
  94.3 1.8 %collective-permute-done.12.got_ref = bf16[4,64,1024]{2,1,0:T(8,128)(2,1)} collective-permute-done((bf16[4,64,1024]{2,1,0:T(8,128)(2,1)}, bf16[4,64,1024]{2,1,0:T(8,128)(2,1)}, u32[]{:S(2)}, u32[]{:S(2)}) %collective-permute-start.12) | collective-permute-done | bytes 524320 | tf_op jit(solution)/shard_map/ppermute | solution.py:51
  96.1 1.0 copy-done.13
  97.2 1.9 %core_sums.2 = (bf16[64,1024]{1,0:T(8,128)(2,1)S(1)}, bf16[64,1024]{1,0:T(8,128)(2,1)}, bf16[64,1024]{1,0:T(8,128)(2,1)}, bf16[64,1024]{1,0:T(8,128)(2,1)}) custom-call(s32[2]{0:T(128)S(1)} %pad_add_fusion.1.x_ref.place_ref, bf16[4,64,1024]{2,1,0:T(8,128)(2,1)S(1)} %copy-done.13, bf16[4,64,1024]{2,1,0:T(8,128)(2,1)} %collective-permute-done.12.got_ref), custom_call_target="tpu_custom_call" | custom-call | bytes 1 | tf_op jit(solution)/shard_map/core_sums/pallas_call | solution.py:309
  99.0 1.2 collective-permute-start.13
  100.3 2.5 %collective-permute-start.14 = (bf16[64,1024]{1,0:T(8,128)(2,1)}, bf16[64,1024]{1,0:T(8,128)(2,1)}, u32[]{:S(2)}, u32[]{:S(2)}) collective-permute-start(bf16[64,1024]{1,0:T(8,128)(2,1)} %get-tuple-element.61), channel_id=1, source_target_pairs={{0,32},{8,40},{16,48},{24,56},{32,0},{40,8},{48,16},{56,24},{64,96... | collective-permute-start | bytes 393224 | tf_op jit(solution)/shard_map/ppermute | solution.py:51
  102.7 1.2 collective-permute-start.15
  103.9 3.4 %group_sums.7.g_ref = f32[512,1024]{1,0:T(8,128)S(1)} custom-call(bf16[256,2048]{1,0:T(8,128)(2,1)} %copy-done.3, bf16[256,1024]{1,0:T(8,128)(2,1)} %copy-done.4, bf16[256,1024]{1,0:T(8,128)(2,1)} %copy-done.5, bf16[256,1024]{1,0:T(8,128)(2,1)} %copy-done.6, bf16[256,1024]{1,0:T(8,128)(2,1)} %bitcast.32, bf16[256,1536]{1,0:T(8,128)(2,1)} %copy-done, ...), custom_call_target="tpu_custom_call" | custom-call | bytes 1 | tf_op jit(solution)/shard_map/group_sums/pallas_call | solution.py:153
  107.3 1.8 %collective-permute-done.14.p2 = bf16[64,1024]{1,0:T(8,128)(2,1)} collective-permute-done((bf16[64,1024]{1,0:T(8,128)(2,1)}, bf16[64,1024]{1,0:T(8,128)(2,1)}, u32[]{:S(2)}, u32[]{:S(2)}) %collective-permute-start.14) | collective-permute-done | bytes 131104 | tf_op jit(solution)/shard_map/ppermute | solution.py:51
  109.1 1.2 x_sums.2
  110.3 3.8 %adam_step.3 = (f32[512,1024]{1,0:T(8,128)S(1)}, bf16[4,64,1024]{2,1,0:T(8,128)(2,1)S(1)}, bf16[4,64,1024]{2,1,0:T(8,128)(2,1)S(1)}) custom-call(s32[1]{0:T(128)} %bitcast.7.core_ref, f32[512,1024]{1,0:T(8,128)S(1)} %group_sums.7.g_ref, bf16[512,1024]{1,0:T(8,128)(2,1)} %collective-permute-done.18.got_ref, f32[1024,1024]{1,0:T(8,128)} %bitcast.26, ...), custom_call_target="tpu_custom_call" | custom-call | bytes 1 | tf_op jit(solution)/shard_map/adam_step/pallas_call | solution.py:214
  114.0 1.3 collective-permute-start.19
  115.3 1.4 collective-permute-start.16
  116.8 1.3 collective-permute-start.17
  118.7 1.1 collective-permute-start.20
  119.8 2.1 %collective-permute-start.21 = (bf16[64,1024]{1,0:T(8,128)(2,1)S(1)}, bf16[64,1024]{1,0:T(8,128)(2,1)S(1)}, u32[]{:S(2)}, u32[]{:S(2)}) collective-permute-start(bf16[64,1024]{1,0:T(8,128)(2,1)S(1)} %get-tuple-element.69), channel_id=1, source_target_pairs={{0,32},{8,40},{16,48},{24,56},{32,0},{40,8},{48,16},{56,24},{64,96... | collective-permute-start | bytes 393224 | tf_op jit(solution)/shard_map/ppermute | solution.py:51
  121.9 1.3 collective-permute-start.22
  123.2 1.2 collective-permute-done.20.p1.refs_1_
  125.1 2.6 %collective-permute-done.21.p2 = bf16[64,1024]{1,0:T(8,128)(2,1)S(1)} collective-permute-done((bf16[64,1024]{1,0:T(8,128)(2,1)S(1)}, bf16[64,1024]{1,0:T(8,128)(2,1)S(1)}, u32[]{:S(2)}, u32[]{:S(2)}) %collective-permute-start.21) | collective-permute-done | bytes 131104 | tf_op jit(solution)/shard_map/ppermute | solution.py:51
  128.8 3.4 %collective-permute-start.32 = (bf16[64,1024]{1,0:T(8,128)(2,1)S(1)}, bf16[64,1024]{1,0:T(8,128)(2,1)S(1)}, u32[]{:S(2)}, u32[]{:S(2)}) collective-permute-start(bf16[64,1024]{1,0:T(8,128)(2,1)S(1)} %gate.23.refs_0_), channel_id=1, source_target_pairs={{0,8},{8,0},{16,24},{24,16},{32,40},{40,32},{48,56},{56,48},{64,72... | collective-permute-start | bytes 393224 | tf_op jit(solution)/shard_map/ppermute | solution.py:51
  132.5 1.9 %collective-permute-start.35 = (bf16[64,1024]{1,0:T(8,128)(2,1)S(1)}, bf16[64,1024]{1,0:T(8,128)(2,1)S(1)}, u32[]{:S(2)}, u32[]{:S(2)}) collective-permute-start(bf16[64,1024]{1,0:T(8,128)(2,1)S(1)} %gate.23.refs_0_), channel_id=1, source_target_pairs={{0,32},{8,40},{16,48},{24,56},{32,0},{40,8},{48,16},{56,24},{64,96... | collective-permute-start | bytes 393224 | tf_op jit(solution)/shard_map/ppermute | solution.py:51
  135.3 1.1 collective-permute-start.28
  136.4 2.6 %collective-permute-done.33.refs_2_ = bf16[64,1024]{1,0:T(8,128)(2,1)S(1)} collective-permute-done((bf16[64,1024]{1,0:T(8,128)(2,1)S(1)}, bf16[64,1024]{1,0:T(8,128)(2,1)S(1)}, u32[]{:S(2)}, u32[]{:S(2)}) %collective-permute-start.33) | collective-permute-done | bytes 131104 | tf_op jit(solution)/shard_map/ppermute | solution.py:51
  138.9 1.5 collective-permute-done.35.refs_4_
  140.5 2.0 %collective-permute-done.28.refs_0_ = bf16[64,1024]{1,0:T(8,128)(2,1)S(1)} collective-permute-done((bf16[64,1024]{1,0:T(8,128)(2,1)S(1)}, bf16[64,1024]{1,0:T(8,128)(2,1)S(1)}, u32[]{:S(2)}, u32[]{:S(2)}) %collective-permute-start.28) | collective-permute-done | bytes 131104 | tf_op jit(solution)/shard_map/ppermute | solution.py:51
  142.4 2.0 %collective-permute-start.30 = (bf16[64,1024]{1,0:T(8,128)(2,1)S(1)}, bf16[64,1024]{1,0:T(8,128)(2,1)S(1)}, u32[]{:S(2)}, u32[]{:S(2)}) collective-permute-start(bf16[64,1024]{1,0:T(8,128)(2,1)S(1)} %get-tuple-element.76.refs_4_.refs_0_), channel_id=1, source_target_pairs={{0,48},{8,56},{16,0},{24,8},{32,16},{40,24},{48,32},{56,40},{64,11... | collective-permute-start | bytes 393224 | tf_op jit(solution)/shard_map/ppermute | solution.py:51
  144.5 3.4 %collective-permute-start.34 = (bf16[64,1024]{1,0:T(8,128)(2,1)S(1)}, bf16[64,1024]{1,0:T(8,128)(2,1)S(1)}, u32[]{:S(2)}, u32[]{:S(2)}) collective-permute-start(bf16[64,1024]{1,0:T(8,128)(2,1)S(1)} %collective-permute-done.33.refs_2_), channel_id=1, source_target_pairs={{0,8},{8,0},{16,24},{24,16},{32,40},{40,32},{48,56},{56,48},{64,72... | collective-permute-start | bytes 393224 | tf_op jit(solution)/shard_map/ppermute | solution.py:51
  147.9 3.3 %assemble.1.refs_1_ = bf16[256,8192]{1,0:T(8,128)(2,1)} custom-call(s32[2]{0:T(128)S(1)} %pad_add_fusion.place_ref, bf16[256,2048]{1,0:T(8,128)(2,1)} %get-tuple-element.51.refs_8_.refs_0_, bf16[256,2048]{1,0:T(8,128)(2,1)S(1)} %collective-permute-done.16.refs_1_, bf16[256,2048]{1,0:T(8,128)(2,1)S(1)} %collective-permute-done.10.refs_1_.refs_2_, ...), custom_call_target="tpu_custom_call" | custom-call | bytes 1 | tf_op jit(solution)/shard_map/assemble/pallas_call | solution.py:291
  153.1 2.5 %mix.2.refs_8_ = f32[1024,1024]{1,0:T(8,128)} custom-call(s32[2]{0:T(128)S(1)} %pad_add_fusion.1.x_ref.place_ref, f32[512,1024]{1,0:T(8,128)S(1)} %gate.22.upd, bf16[64,1024]{1,0:T(8,128)(2,1)S(1)} %gate.23.refs_0_, bf16[64,1024]{1,0:T(8,128)(2,1)S(1)} %collective-permute-done.32.refs_1_, bf16[64,1024]{1,0:T(8,128)(2,1)S(1)} %collective-permute-done.33.refs_2_, ...), custom_call_target="tpu_custom_call" | custom-call | bytes 1 | tf_op jit(solution)/shard_map/mix/pallas_call | solution.py:390
  155.6 2.5 %mix.3 = f32[1024,1024]{1,0:T(8,128)} custom-call(s32[2]{0:T(128)S(1)} %pad_add_fusion.1.x_ref.place_ref, f32[512,1024]{1,0:T(8,128)S(1)} %get-tuple-element.77.upd, bf16[64,1024]{1,0:T(8,128)(2,1)S(1)} %get-tuple-element.76.refs_4_.refs_0_, bf16[64,1024]{1,0:T(8,128)(2,1)S(1)} %collective-permute-done.25.refs_1_, ...), custom_call_target="tpu_custom_call", output_to_operand_aliasing={{}: (10, {})} | custom-call | bytes 1 | tf_op jit(solution)/shard_map/mix/pallas_call | solution.py:390
  (89 shorter events, 7.9 us)
Async XLA Ops:
  5.3 46.6 %copy-start.3 = (bf16[256,2048]{1,0:T(8,128)(2,1)}, bf16[256,2048]{1,0:T(8,128)(2,1)S(1)}, u32[]{:S(2)}) copy-start(bf16[256,2048]{1,0:T(8,128)(2,1)S(1)} %get-tuple-element.47.refs_0_) | copy-start | bytes 3145732
  5.3 56.6 %collective-permute-start = (bf16[1024,1024]{1,0:T(8,128)(2,1)S(1)}, bf16[1024,1024]{1,0:T(8,128)(2,1)S(1)}, u32[]{:S(2)}, u32[]{:S(2)}) collective-permute-start(bf16[1024,1024]{1,0:T(8,128)(2,1)S(1)} %get-tuple-element.43.w0), channel_id=1, source_target_pairs={{0,4},{1,5},{2,6},{3,7},{4,0},{5,1},{6,2},{7,3},{8,12},{9,13},{10,... | collective-permute-start | bytes 6291464 | tf_op jit(solution)/shard_map/ppermute | solution.py:38
  9.8 19.4 %collective-permute-start.1 = (bf16[256,1536]{1,0:T(8,128)(2,1)S(1)}, bf16[256,1536]{1,0:T(8,128)(2,1)S(1)}, u32[]{:S(2)}, u32[]{:S(2)}) collective-permute-start(bf16[256,1536]{1,0:T(8,128)(2,1)S(1)} %get-tuple-element.44), channel_id=1, source_target_pairs={{0,1},{1,2},{2,3},{3,0},{4,5},{5,6},{6,7},{7,4},{8,9},{9,10},{10,1... | collective-permute-start | bytes 2359304 | tf_op jit(solution)/shard_map/ppermute | solution.py:33
  11.1 36.1 %collective-permute-start.2 = (bf16[256,1536]{1,0:T(8,128)(2,1)S(1)}, bf16[256,1536]{1,0:T(8,128)(2,1)S(1)}, u32[]{:S(2)}, u32[]{:S(2)}) collective-permute-start(bf16[256,1536]{1,0:T(8,128)(2,1)S(1)} %get-tuple-element.45), channel_id=1, source_target_pairs={{0,2},{1,3},{2,0},{3,1},{4,6},{5,7},{6,4},{7,5},{8,10},{9,11},{10,... | collective-permute-start | bytes 2359304 | tf_op jit(solution)/shard_map/ppermute | solution.py:33
  13.7 34.3 %collective-permute-start.3 = (bf16[256,1536]{1,0:T(8,128)(2,1)S(1)}, bf16[256,1536]{1,0:T(8,128)(2,1)S(1)}, u32[]{:S(2)}, u32[]{:S(2)}) collective-permute-start(bf16[256,1536]{1,0:T(8,128)(2,1)S(1)} %get-tuple-element.46), channel_id=1, source_target_pairs={{0,3},{1,0},{2,1},{3,2},{4,7},{5,4},{6,5},{7,6},{8,11},{9,8},{10,9... | collective-permute-start | bytes 2359304 | tf_op jit(solution)/shard_map/ppermute | solution.py:33
  29.2 22.7 %copy-start = (bf16[256,1536]{1,0:T(8,128)(2,1)}, bf16[256,1536]{1,0:T(8,128)(2,1)S(1)}, u32[]{:S(2)}) copy-start(bf16[256,1536]{1,0:T(8,128)(2,1)S(1)} %collective-permute-done.1.refs_1_.refs_5_.c1) | copy-start | bytes 2359300
  29.2 26.9 %collective-permute-start.4 = (bf16[256,512]{1,0:T(8,128)(2,1)S(1)}, bf16[256,512]{1,0:T(8,128)(2,1)S(1)}, u32[]{:S(2)}, u32[]{:S(2)}) collective-permute-start(bf16[256,512]{1,0:T(8,128)(2,1)S(1)} %gate.12), channel_id=1, source_target_pairs={{0,1},{1,2},{2,3},{3,0},{4,5},{5,6},{6,7},{7,4},{8,9},{9,10},{10,1... | collective-permute-start | bytes 786440 | tf_op jit(solution)/shard_map/ppermute | solution.py:33
  47.2 4.7 %copy-start.1 = (bf16[256,1536]{1,0:T(8,128)(2,1)}, bf16[256,1536]{1,0:T(8,128)(2,1)S(1)}, u32[]{:S(2)}) copy-start(bf16[256,1536]{1,0:T(8,128)(2,1)S(1)} %collective-permute-done.2.refs_1_.refs_6_.c2.refs_2_) | copy-start | bytes 2359300
  47.2 11.2 %collective-permute-start.5 = (bf16[256,512]{1,0:T(8,128)(2,1)S(1)}, bf16[256,512]{1,0:T(8,128)(2,1)S(1)}, u32[]{:S(2)}, u32[]{:S(2)}) collective-permute-start(bf16[256,512]{1,0:T(8,128)(2,1)S(1)} %gate.13), channel_id=1, source_target_pairs={{0,2},{1,3},{2,0},{3,1},{4,6},{5,7},{6,4},{7,5},{8,10},{9,11},{10,... | collective-permute-start | bytes 786440 | tf_op jit(solution)/shard_map/ppermute | solution.py:33
  48.0 3.9 %copy-start.2 = (bf16[256,1536]{1,0:T(8,128)(2,1)}, bf16[256,1536]{1,0:T(8,128)(2,1)S(1)}, u32[]{:S(2)}) copy-start(bf16[256,1536]{1,0:T(8,128)(2,1)S(1)} %collective-permute-done.3.refs_1_.refs_7_.c3.refs_3_) | copy-start | bytes 2359300
  48.0 10.8 %collective-permute-start.6 = (bf16[256,512]{1,0:T(8,128)(2,1)S(1)}, bf16[256,512]{1,0:T(8,128)(2,1)S(1)}, u32[]{:S(2)}, u32[]{:S(2)}) collective-permute-start(bf16[256,512]{1,0:T(8,128)(2,1)S(1)} %gate.14), channel_id=1, source_target_pairs={{0,3},{1,0},{2,1},{3,2},{4,7},{5,4},{6,5},{7,6},{8,11},{9,8},{10,9... | collective-permute-start | bytes 786440 | tf_op jit(solution)/shard_map/ppermute | solution.py:33
  56.1 30.9 %collective-permute-start.11 = (bf16[512,1024]{1,0:T(8,128)(2,1)}, bf16[512,1024]{1,0:T(8,128)(2,1)}, u32[]{:S(2)}, u32[]{:S(2)}) collective-permute-start(bf16[512,1024]{1,0:T(8,128)(2,1)} %group_sums.6), channel_id=1, source_target_pairs={{0,4},{1,5},{2,6},{3,7},{4,0},{5,1},{6,2},{7,3},{8,12},{9,13},{10,... | collective-permute-start | bytes 3145736 | tf_op jit(solution)/shard_map/ppermute | solution.py:38
  56.1 5.8 %copy-start.9 = (bf16[256,512]{1,0:T(8,128)(2,1)}, bf16[256,512]{1,0:T(8,128)(2,1)S(1)}, u32[]{:S(2)}) copy-start(bf16[256,512]{1,0:T(8,128)(2,1)S(1)} %collective-permute-done.4.refs_1_) | copy-start | bytes 786436
  56.1 18.8 %collective-permute-start.7 = (bf16[256,1024]{1,0:T(8,128)(2,1)S(1)}, bf16[256,1024]{1,0:T(8,128)(2,1)S(1)}, u32[]{:S(2)}, u32[]{:S(2)}) collective-permute-start(bf16[256,1024]{1,0:T(8,128)(2,1)S(1)} %gate.15), channel_id=1, source_target_pairs={{0,1},{1,2},{2,3},{3,0},{4,5},{5,6},{6,7},{7,4},{8,9},{9,10},{10,1... | collective-permute-start | bytes 1572872 | tf_op jit(solution)/shard_map/ppermute | solution.py:33
  58.5 3.4 %copy-start.10 = (bf16[256,512]{1,0:T(8,128)(2,1)}, bf16[256,512]{1,0:T(8,128)(2,1)S(1)}, u32[]{:S(2)}) copy-start(bf16[256,512]{1,0:T(8,128)(2,1)S(1)} %collective-permute-done.5.refs_2_.refs_1_) | copy-start | bytes 786436
  58.5 22.4 %collective-permute-start.8 = (bf16[256,1024]{1,0:T(8,128)(2,1)S(1)}, bf16[256,1024]{1,0:T(8,128)(2,1)S(1)}, u32[]{:S(2)}, u32[]{:S(2)}) collective-permute-start(bf16[256,1024]{1,0:T(8,128)(2,1)S(1)} %gate.16), channel_id=1, source_target_pairs={{0,2},{1,3},{2,0},{3,1},{4,6},{5,7},{6,4},{7,5},{8,10},{9,11},{10,... | collective-permute-start | bytes 1572872 | tf_op jit(solution)/shard_map/ppermute | solution.py:33
  58.8 23.2 %collective-permute-start.9 = (bf16[256,1024]{1,0:T(8,128)(2,1)S(1)}, bf16[256,1024]{1,0:T(8,128)(2,1)S(1)}, u32[]{:S(2)}, u32[]{:S(2)}) collective-permute-start(bf16[256,1024]{1,0:T(8,128)(2,1)S(1)} %gate.17), channel_id=1, source_target_pairs={{0,3},{1,0},{2,1},{3,2},{4,7},{5,4},{6,5},{7,6},{8,11},{9,8},{10,9... | collective-permute-start | bytes 1572872 | tf_op jit(solution)/shard_map/ppermute | solution.py:33
  66.1 44.2 %collective-permute-start.18 = (bf16[512,1024]{1,0:T(8,128)(2,1)}, bf16[512,1024]{1,0:T(8,128)(2,1)}, u32[]{:S(2)}, u32[]{:S(2)}) collective-permute-start(bf16[512,1024]{1,0:T(8,128)(2,1)} %group_sums.4.refs_0_), channel_id=1, source_target_pairs={{0,4},{1,5},{2,6},{3,7},{4,0},{5,1},{6,2},{7,3},{8,12},{9,13},{10,... | collective-permute-start | bytes 3145736 | tf_op jit(solution)/shard_map/ppermute | solution.py:38
  75.0 8.6 %copy-start.4 = (bf16[256,1024]{1,0:T(8,128)(2,1)}, bf16[256,1024]{1,0:T(8,128)(2,1)S(1)}, u32[]{:S(2)}) copy-start(bf16[256,1024]{1,0:T(8,128)(2,1)S(1)} %collective-permute-done.7.refs_1_) | copy-start | bytes 1572868
  82.1 33.2 %collective-permute-start.10 = (bf16[256,2048]{1,0:T(8,128)(2,1)}, bf16[256,2048]{1,0:T(8,128)(2,1)S(1)}, u32[]{:S(2)}, u32[]{:S(2)}) collective-permute-start(bf16[256,2048]{1,0:T(8,128)(2,1)} %gate.18), channel_id=1, source_target_pairs={{0,2},{1,3},{2,0},{3,1},{4,6},{5,7},{6,4},{7,5},{8,10},{9,11},{10,... | collective-permute-start | bytes 3145736 | tf_op jit(solution)/shard_map/ppermute | solution.py:33
  92.4 3.7 %collective-permute-start.12 = (bf16[4,64,1024]{2,1,0:T(8,128)(2,1)}, bf16[4,64,1024]{2,1,0:T(8,128)(2,1)}, u32[]{:S(2)}, u32[]{:S(2)}) collective-permute-start(bf16[4,64,1024]{2,1,0:T(8,128)(2,1)} %get-tuple-element.58), channel_id=1, source_target_pairs={{0,8},{8,0},{16,24},{24,16},{32,40},{40,32},{48,56},{56,48},{64,72... | collective-permute-start | bytes 1572872 | tf_op jit(solution)/shard_map/ppermute | solution.py:51
  97.2 11.9 %copy-start.7 = (f32[1,64,1024]{2,1,0:T(8,128)S(1)}, f32[1,64,1024]{2,1,0:T(8,128)}, u32[]{:S(2)}) copy-start(f32[1,64,1024]{2,1,0:T(8,128)} %param.12) | copy-start | bytes 786436
  99.0 8.2 %collective-permute-start.13 = (bf16[64,1024]{1,0:T(8,128)(2,1)}, bf16[64,1024]{1,0:T(8,128)(2,1)}, u32[]{:S(2)}, u32[]{:S(2)}) collective-permute-start(bf16[64,1024]{1,0:T(8,128)(2,1)} %get-tuple-element.60), channel_id=1, source_target_pairs={{0,16},{8,24},{16,32},{24,40},{32,48},{40,56},{48,0},{56,8},{64,80... | collective-permute-start | bytes 393224 | tf_op jit(solution)/shard_map/ppermute | solution.py:51
  100.3 8.8 %collective-permute-start.14 = (bf16[64,1024]{1,0:T(8,128)(2,1)}, bf16[64,1024]{1,0:T(8,128)(2,1)}, u32[]{:S(2)}, u32[]{:S(2)}) collective-permute-start(bf16[64,1024]{1,0:T(8,128)(2,1)} %get-tuple-element.61), channel_id=1, source_target_pairs={{0,32},{8,40},{16,48},{24,56},{32,0},{40,8},{48,16},{56,24},{64,96... | collective-permute-start | bytes 393224 | tf_op jit(solution)/shard_map/ppermute | solution.py:51
  102.7 6.4 %collective-permute-start.15 = (bf16[64,1024]{1,0:T(8,128)(2,1)}, bf16[64,1024]{1,0:T(8,128)(2,1)}, u32[]{:S(2)}, u32[]{:S(2)}) collective-permute-start(bf16[64,1024]{1,0:T(8,128)(2,1)} %get-tuple-element.62), channel_id=1, source_target_pairs={{0,48},{8,56},{16,0},{24,8},{32,16},{40,24},{48,32},{56,40},{64,11... | collective-permute-start | bytes 393224 | tf_op jit(solution)/shard_map/ppermute | solution.py:51
  103.9 5.2 %copy-start.8 = (f32[1,64,1024]{2,1,0:T(8,128)S(1)}, f32[1,64,1024]{2,1,0:T(8,128)}, u32[]{:S(2)}) copy-start(f32[1,64,1024]{2,1,0:T(8,128)} %param.13) | copy-start | bytes 786436
  114.0 4.0 %collective-permute-start.19 = (bf16[4,64,1024]{2,1,0:T(8,128)(2,1)S(1)}, bf16[4,64,1024]{2,1,0:T(8,128)(2,1)S(1)}, u32[]{:S(2)}, u32[]{:S(2)}) collective-permute-start(bf16[4,64,1024]{2,1,0:T(8,128)(2,1)S(1)} %get-tuple-element.66), channel_id=1, source_target_pairs={{0,8},{8,0},{16,24},{24,16},{32,40},{40,32},{48,56},{56,48},{64,72... | collective-permute-start | bytes 1572872 | tf_op jit(solution)/shard_map/ppermute | solution.py:51
  115.3 29.1 %collective-permute-start.16 = (bf16[256,2048]{1,0:T(8,128)(2,1)}, bf16[256,2048]{1,0:T(8,128)(2,1)S(1)}, u32[]{:S(2)}, u32[]{:S(2)}) collective-permute-start(bf16[256,2048]{1,0:T(8,128)(2,1)} %gate.19), channel_id=1, source_target_pairs={{0,1},{1,2},{2,3},{3,0},{4,5},{5,6},{6,7},{7,4},{8,9},{9,10},{10,1... | collective-permute-start | bytes 3145736 | tf_op jit(solution)/shard_map/ppermute | solution.py:33
  116.8 31.1 %collective-permute-start.17 = (bf16[256,2048]{1,0:T(8,128)(2,1)}, bf16[256,2048]{1,0:T(8,128)(2,1)S(1)}, u32[]{:S(2)}, u32[]{:S(2)}) collective-permute-start(bf16[256,2048]{1,0:T(8,128)(2,1)} %gate.20), channel_id=1, source_target_pairs={{0,3},{1,0},{2,1},{3,2},{4,7},{5,4},{6,5},{7,6},{8,11},{9,8},{10,9... | collective-permute-start | bytes 3145736 | tf_op jit(solution)/shard_map/ppermute | solution.py:33
  118.7 5.7 %collective-permute-start.20 = (bf16[64,1024]{1,0:T(8,128)(2,1)S(1)}, bf16[64,1024]{1,0:T(8,128)(2,1)S(1)}, u32[]{:S(2)}, u32[]{:S(2)}) collective-permute-start(bf16[64,1024]{1,0:T(8,128)(2,1)S(1)} %get-tuple-element.68), channel_id=1, source_target_pairs={{0,16},{8,24},{16,32},{24,40},{32,48},{40,56},{48,0},{56,8},{64,80... | collective-permute-start | bytes 393224 | tf_op jit(solution)/shard_map/ppermute | solution.py:51
  119.8 7.9 %collective-permute-start.21 = (bf16[64,1024]{1,0:T(8,128)(2,1)S(1)}, bf16[64,1024]{1,0:T(8,128)(2,1)S(1)}, u32[]{:S(2)}, u32[]{:S(2)}) collective-permute-start(bf16[64,1024]{1,0:T(8,128)(2,1)S(1)} %get-tuple-element.69), channel_id=1, source_target_pairs={{0,32},{8,40},{16,48},{24,56},{32,0},{40,8},{48,16},{56,24},{64,96... | collective-permute-start | bytes 393224 | tf_op jit(solution)/shard_map/ppermute | solution.py:51
  121.9 5.7 %collective-permute-start.22 = (bf16[64,1024]{1,0:T(8,128)(2,1)S(1)}, bf16[64,1024]{1,0:T(8,128)(2,1)S(1)}, u32[]{:S(2)}, u32[]{:S(2)}) collective-permute-start(bf16[64,1024]{1,0:T(8,128)(2,1)S(1)} %get-tuple-element.70), channel_id=1, source_target_pairs={{0,48},{8,56},{16,0},{24,8},{32,16},{40,24},{48,32},{56,40},{64,11... | collective-permute-start | bytes 393224 | tf_op jit(solution)/shard_map/ppermute | solution.py:51
  124.4 4.3 %collective-permute-start.24 = (bf16[64,1024]{1,0:T(8,128)(2,1)S(1)}, bf16[64,1024]{1,0:T(8,128)(2,1)S(1)}, u32[]{:S(2)}, u32[]{:S(2)}) collective-permute-start(bf16[64,1024]{1,0:T(8,128)(2,1)S(1)} %get-tuple-element.63.refs_2_.refs_0_), channel_id=1, source_target_pairs={{0,64},{8,72},{16,80},{24,88},{32,96},{40,104},{48,112},{56,120},{... | collective-permute-start | bytes 393224 | tf_op jit(solution)/shard_map/ppermute | solution.py:51
  127.8 4.7 %collective-permute-start.23 = (bf16[64,1024]{1,0:T(8,128)(2,1)S(1)}, bf16[64,1024]{1,0:T(8,128)(2,1)S(1)}, u32[]{:S(2)}, u32[]{:S(2)}) collective-permute-start(bf16[64,1024]{1,0:T(8,128)(2,1)S(1)} %get-tuple-element.72.refs_1_), channel_id=1, source_target_pairs={{0,64},{8,72},{16,80},{24,88},{32,96},{40,104},{48,112},{56,120},{... | collective-permute-start | bytes 393224 | tf_op jit(solution)/shard_map/ppermute | solution.py:51
  128.8 6.5 %collective-permute-start.32 = (bf16[64,1024]{1,0:T(8,128)(2,1)S(1)}, bf16[64,1024]{1,0:T(8,128)(2,1)S(1)}, u32[]{:S(2)}, u32[]{:S(2)}) collective-permute-start(bf16[64,1024]{1,0:T(8,128)(2,1)S(1)} %gate.23.refs_0_), channel_id=1, source_target_pairs={{0,8},{8,0},{16,24},{24,16},{32,40},{40,32},{48,56},{56,48},{64,72... | collective-permute-start | bytes 393224 | tf_op jit(solution)/shard_map/ppermute | solution.py:51
  132.2 6.7 %collective-permute-start.33 = (bf16[64,1024]{1,0:T(8,128)(2,1)S(1)}, bf16[64,1024]{1,0:T(8,128)(2,1)S(1)}, u32[]{:S(2)}, u32[]{:S(2)}) collective-permute-start(bf16[64,1024]{1,0:T(8,128)(2,1)S(1)} %gate.23.refs_0_), channel_id=1, source_target_pairs={{0,16},{8,24},{16,32},{24,40},{32,48},{40,56},{48,0},{56,8},{64,80... | collective-permute-start | bytes 393224 | tf_op jit(solution)/shard_map/ppermute | solution.py:51
  132.5 8.0 %collective-permute-start.35 = (bf16[64,1024]{1,0:T(8,128)(2,1)S(1)}, bf16[64,1024]{1,0:T(8,128)(2,1)S(1)}, u32[]{:S(2)}, u32[]{:S(2)}) collective-permute-start(bf16[64,1024]{1,0:T(8,128)(2,1)S(1)} %gate.23.refs_0_), channel_id=1, source_target_pairs={{0,32},{8,40},{16,48},{24,56},{32,0},{40,8},{48,16},{56,24},{64,96... | collective-permute-start | bytes 393224 | tf_op jit(solution)/shard_map/ppermute | solution.py:51
  135.3 7.2 %collective-permute-start.28 = (bf16[64,1024]{1,0:T(8,128)(2,1)S(1)}, bf16[64,1024]{1,0:T(8,128)(2,1)S(1)}, u32[]{:S(2)}, u32[]{:S(2)}) collective-permute-start(bf16[64,1024]{1,0:T(8,128)(2,1)S(1)} %get-tuple-element.76.refs_4_.refs_0_), channel_id=1, source_target_pairs={{0,32},{8,40},{16,48},{24,56},{32,0},{40,8},{48,16},{56,24},{64,96... | collective-permute-start | bytes 393224 | tf_op jit(solution)/shard_map/ppermute | solution.py:51
  138.9 12.3 %collective-permute-start.37 = (bf16[64,1024]{1,0:T(8,128)(2,1)S(1)}, bf16[64,1024]{1,0:T(8,128)(2,1)S(1)}, u32[]{:S(2)}, u32[]{:S(2)}) collective-permute-start(bf16[64,1024]{1,0:T(8,128)(2,1)S(1)} %gate.23.refs_0_), channel_id=1, source_target_pairs={{0,48},{8,56},{16,0},{24,8},{32,16},{40,24},{48,32},{56,40},{64,11... | collective-permute-start | bytes 393224 | tf_op jit(solution)/shard_map/ppermute | solution.py:51
  140.5 11.3 %collective-permute-start.26 = (bf16[64,1024]{1,0:T(8,128)(2,1)S(1)}, bf16[64,1024]{1,0:T(8,128)(2,1)S(1)}, u32[]{:S(2)}, u32[]{:S(2)}) collective-permute-start(bf16[64,1024]{1,0:T(8,128)(2,1)S(1)} %get-tuple-element.76.refs_4_.refs_0_), channel_id=1, source_target_pairs={{0,16},{8,24},{16,32},{24,40},{32,48},{40,56},{48,0},{56,8},{64,80... | collective-permute-start | bytes 393224 | tf_op jit(solution)/shard_map/ppermute | solution.py:51
  142.4 9.4 %collective-permute-start.30 = (bf16[64,1024]{1,0:T(8,128)(2,1)S(1)}, bf16[64,1024]{1,0:T(8,128)(2,1)S(1)}, u32[]{:S(2)}, u32[]{:S(2)}) collective-permute-start(bf16[64,1024]{1,0:T(8,128)(2,1)S(1)} %get-tuple-element.76.refs_4_.refs_0_), channel_id=1, source_target_pairs={{0,48},{8,56},{16,0},{24,8},{32,16},{40,24},{48,32},{56,40},{64,11... | collective-permute-start | bytes 393224 | tf_op jit(solution)/shard_map/ppermute | solution.py:51
  144.5 7.8 %collective-permute-start.34 = (bf16[64,1024]{1,0:T(8,128)(2,1)S(1)}, bf16[64,1024]{1,0:T(8,128)(2,1)S(1)}, u32[]{:S(2)}, u32[]{:S(2)}) collective-permute-start(bf16[64,1024]{1,0:T(8,128)(2,1)S(1)} %collective-permute-done.33.refs_2_), channel_id=1, source_target_pairs={{0,8},{8,0},{16,24},{24,16},{32,40},{40,32},{48,56},{56,48},{64,72... | collective-permute-start | bytes 393224 | tf_op jit(solution)/shard_map/ppermute | solution.py:51
  147.8 4.6 %collective-permute-start.36 = (bf16[64,1024]{1,0:T(8,128)(2,1)S(1)}, bf16[64,1024]{1,0:T(8,128)(2,1)S(1)}, u32[]{:S(2)}, u32[]{:S(2)}) collective-permute-start(bf16[64,1024]{1,0:T(8,128)(2,1)S(1)} %collective-permute-done.35.refs_4_), channel_id=1, source_target_pairs={{0,8},{8,0},{16,24},{24,16},{32,40},{40,32},{48,56},{56,48},{64,72... | collective-permute-start | bytes 393224 | tf_op jit(solution)/shard_map/ppermute | solution.py:51
  151.2 4.4 %collective-permute-start.25 = (bf16[64,1024]{1,0:T(8,128)(2,1)S(1)}, bf16[64,1024]{1,0:T(8,128)(2,1)S(1)}, u32[]{:S(2)}, u32[]{:S(2)}) collective-permute-start(bf16[64,1024]{1,0:T(8,128)(2,1)S(1)} %get-tuple-element.76.refs_4_.refs_0_), channel_id=1, source_target_pairs={{0,8},{8,0},{16,24},{24,16},{32,40},{40,32},{48,56},{56,48},{64,72... | collective-permute-start | bytes 393224 | tf_op jit(solution)/shard_map/ppermute | solution.py:51
  151.8 1.3 collective-permute-start.38
  151.9 3.8 %collective-permute-start.27 = (bf16[64,1024]{1,0:T(8,128)(2,1)S(1)}, bf16[64,1024]{1,0:T(8,128)(2,1)S(1)}, u32[]{:S(2)}, u32[]{:S(2)}) collective-permute-start(bf16[64,1024]{1,0:T(8,128)(2,1)S(1)} %collective-permute-done.26.refs_2_), channel_id=1, source_target_pairs={{0,8},{8,0},{16,24},{24,16},{32,40},{40,32},{48,56},{56,48},{64,72... | collective-permute-start | bytes 393224 | tf_op jit(solution)/shard_map/ppermute | solution.py:51
  152.3 3.4 %collective-permute-start.31 = (bf16[64,1024]{1,0:T(8,128)(2,1)S(1)}, bf16[64,1024]{1,0:T(8,128)(2,1)S(1)}, u32[]{:S(2)}, u32[]{:S(2)}) collective-permute-start(bf16[64,1024]{1,0:T(8,128)(2,1)S(1)} %collective-permute-done.30.refs_6_), channel_id=1, source_target_pairs={{0,8},{8,0},{16,24},{24,16},{32,40},{40,32},{48,56},{56,48},{64,72... | collective-permute-start | bytes 393224 | tf_op jit(solution)/shard_map/ppermute | solution.py:51
  152.4 3.3 %collective-permute-start.29 = (bf16[64,1024]{1,0:T(8,128)(2,1)S(1)}, bf16[64,1024]{1,0:T(8,128)(2,1)S(1)}, u32[]{:S(2)}, u32[]{:S(2)}) collective-permute-start(bf16[64,1024]{1,0:T(8,128)(2,1)S(1)} %gate.21.refs_4_), channel_id=1, source_target_pairs={{0,8},{8,0},{16,24},{24,16},{32,40},{40,32},{48,56},{56,48},{64,72... | collective-permute-start | bytes 393224 | tf_op jit(solution)/shard_map/ppermute | solution.py:51
  (5 other events, 9.2 us)
